TPU v7x, 32 devices: a whole 2x2x4 slice. The times are simulated.
32 devices in a mesh: groups: 2 (over x), rows: 8 (over z, y), loop: 2 (over core).
Axes of the slice: x: 2, y: 2, z: 4, core: 2. Of those that a mesh axis runs over, the one named last changes fastest.
Arguments:
- frame_one: bfloat16 [32, 256, 256], P(('groups', 'rows')), parts along dimension 0, may hold values from -12.2 to 12.2
- frame_two: bfloat16 [32, 256, 256], P(('groups', 'rows'), 'loop'), parts along dimension 0, may hold values from -12.2 to 12.2
- context: bfloat16 [32, 256, 128], P(('groups', 'rows')), parts along dimension 0, may hold values from -6 to 6
- carry_hidden: bfloat16 [24576, 128], P(('groups', 'rows')), parts along dimension 0, may hold values from -1 to 1
- carry_flow: bfloat16 [24576, 2], P(('groups', 'rows')), parts along dimension 0, may hold values from -48 to 48
- slot_target: int32 [24576], P(('groups', 'rows')), parts along dimension 0, may hold values from 0 to 4095, as said below
- slot_count: int32 [16], P(('groups', 'rows')), parts along dimension 0, may hold values from 8 to 1536, as said below
- match_weight: bfloat16 [512, 128], replicated, may hold values from -0.25 to 0.25
- offset_weight: float32 [6, 128], replicated, may hold values from -2.5 to 2.5
- gate_weight: bfloat16 [2, 5, 384, 256], replicated, may hold values from -0.125 to 0.125
- state_weight: bfloat16 [2, 5, 384, 128], replicated, may hold values from -0.125 to 0.125
- gru_bias: float32 [2, 384], replicated, may hold values from -3 to 3
- head_weight: bfloat16 [128, 256], replicated, may hold values from -0.5 to 0.5
- delta_weight: bfloat16 [2, 256], replicated, may hold values from -0.375 to 0.375
Outputs:
- hidden_out: float32 [32, 256, 128], P(('groups', 'rows')), parts along dimension 0
- flow_out: float32 [2, 32, 256], P(None, ('groups', 'rows')), parts along dimension 1
There are 2 independent parts, one for each index of `groups`. A program takes and returns all parts, laid end to end along the dimension named above; an argument that names none is the same for every part. Nothing has to cross between parts.
Inputs may be any that keep to these rules, and one draw needn't show every extreme that they name: `slot_target`: over all blocks, the counted slots (the first slot_count[b] of block b of 1536) name every pixel index exactly once, so that every index r of rows, owning pixel indices r * 512 to (r + 1) * 512 - 1, gets exactly 512 counted slots. Of one block's counted slots at most 192 belong to one index of rows, and some block has 192 for every index. Slots past the count hold arbitrary pixel indices. `slot_count`: some block has all 1536 slots counted.
All inputs are finite; a program needn't handle non-finite values.
Results may differ from a plain program's by a relative error of at most 0.0035.
Values may be sent and summed in bfloat16 or wider, within the bound.
No kernel may reach another device: no remote copies, remote signals or barrier semaphores. Data moves between devices by JAX's collectives and lax.ppermute only.
A program may use at most 128 MiB of HBM per device.

v0:
```python
import math

import jax
import jax.numpy as jnp
from jax import lax
from jax.sharding import PartitionSpec as P

ITERS = 2


offset_scale = 0.03125


def merged_2(x, axis, combine):
    everything = jax.tree.map(lambda part: lax.all_gather(part, axis), x)
    first = jax.tree.map(lambda part: part[0], everything)

    def step(k, so_far):
        return combine(so_far, jax.tree.map(lambda part: part[k], everything))

    return lax.fori_loop(1, lax.axis_size(axis), step, first)


def extended_2(block, sides, width):
    for axis, dim in sides:
        count = lax.axis_size(axis)
        forward = [(i, i + 1) for i in range(count - 1)]
        backward = [(target, source) for source, target in forward]
        low = lax.ppermute(
            lax.slice_in_dim(block, block.shape[dim] - width, None, axis=dim), axis, forward
        )
        high = lax.ppermute(lax.slice_in_dim(block, 0, width, axis=dim), axis, backward)
        block = jnp.concatenate([low, block, high], axis=dim)
    return block


def pool_quads(frames):
    values = frames.astype(jnp.float32)
    summed = values[0::2, 0::2] + values[0::2, 1::2] + values[1::2, 0::2] + values[1::2, 1::2]
    return (summed * 0.25).astype(jnp.bfloat16)


def absorb(partial_value, scores, key_block, key_rows, key_cols):
    peak_now, weight_sum, accumulated, row_sum, col_sum = partial_value
    new_peak = jnp.maximum(peak_now, jnp.max(scores, axis=1))
    rescale = jnp.exp(peak_now - new_peak)
    expo_terms = jnp.exp(scores - new_peak[:, None])
    weight_sum = weight_sum * rescale + jnp.sum(expo_terms, axis=1)
    accumulated = accumulated * rescale[:, None] + jnp.dot(
        expo_terms.astype(jnp.bfloat16), key_block, preferred_element_type=jnp.float32
    )
    row_sum = row_sum * rescale + jnp.sum(expo_terms * key_rows[None, :], axis=1)
    col_sum = col_sum * rescale + jnp.sum(expo_terms * key_cols[None, :], axis=1)
    return (new_peak, weight_sum, accumulated, row_sum, col_sum)


def combine_level(first_part, second_part):
    joint_peak = jnp.maximum(first_part[0], second_part[0])
    scale_first = jnp.exp(first_part[0] - joint_peak)
    scale_second = jnp.exp(second_part[0] - joint_peak)
    return (
        joint_peak,
        first_part[1] * scale_first + second_part[1] * scale_second,
        first_part[2] * scale_first[:, None] + second_part[2] * scale_second[:, None],
        first_part[3] * scale_first + second_part[3] * scale_second,
        first_part[4] * scale_first + second_part[4] * scale_second,
    )


def combine_all(first_part, second_part):
    return tuple(combine_level(first_part[:5], second_part[:5])) + tuple(
        combine_level(first_part[5:], second_part[5:])
    )


def settle(partial_value, own_rows, own_cols):
    matched = (partial_value[2] / partial_value[1][:, None]).astype(jnp.bfloat16)
    return (
        matched,
        partial_value[3] / partial_value[1] - own_rows,
        partial_value[4] / partial_value[1] - own_cols,
    )


def conv_along(extended, weights, axis_index, length):
    outcome = None
    for tap_index in range(weights.shape[0]):
        window = lax.slice_in_dim(extended, tap_index, tap_index + length, axis=axis_index)
        product = jnp.dot(
            window.reshape(-1, window.shape[-1]),
            weights[tap_index],
            preferred_element_type=jnp.float32,
        )
        outcome = product if outcome is None else outcome + product
    return outcome


def fine_positions(first_shard, shard_count, rows_per, columns, half_index):
    shard_span = rows_per * columns
    index_all = jnp.arange(shard_count * shard_span, dtype=jnp.int32)
    shard_at = first_shard + index_all // shard_span
    key_rows = (shard_at * rows_per + index_all % shard_span // columns).astype(jnp.float32)
    key_cols = (half_index * columns + index_all % columns).astype(jnp.float32)
    return (key_rows, key_cols)


def coarse_positions(first_shard, shard_count, quarter, half_index):
    index_all = jnp.arange(shard_count * quarter, dtype=jnp.int32)
    key_rows = ((first_shard + index_all // quarter) * 2).astype(jnp.float32) + 0.5
    key_cols = ((half_index * quarter + index_all % quarter) * 2).astype(jnp.float32) + 0.5
    return (key_rows, key_cols)


def local(
    frame_one,
    frame_two,
    context,
    carry_hidden,
    carry_flow,
    slot_target,
    slot_count,
    match_weight,
    offset_weight,
    gate_weight,
    state_weight,
    gru_bias,
    head_weight,
    delta_weight,
):
    half_index = lax.axis_index("loop")
    row_index = lax.axis_index("rows")
    rows_per, width_all, channels = frame_one.shape
    columns = frame_two.shape[1]
    quarter = columns // 2
    pixels = rows_per * width_all
    hidden_size = carry_hidden.shape[1]
    queries = frame_one.reshape(pixels, channels)

    def blank_level():
        return (
            jnp.full((pixels,), -jnp.inf, jnp.float32),
            jnp.zeros((pixels,), jnp.float32),
            jnp.zeros((pixels, channels), jnp.float32),
            jnp.zeros((pixels,), jnp.float32),
            jnp.zeros((pixels,), jnp.float32),
        )

    fine_local = frame_two.reshape(1, rows_per * columns, channels)
    start_state = blank_level() + blank_level()
    coarse_local = pool_quads(frame_two)
    fine_part = lax.all_gather(fine_local, "rows", axis=0, tiled=True)
    shard_count = fine_part.shape[0]
    coarse_part = lax.all_gather(coarse_local, "rows", axis=0, tiled=True)
    group_size = math.gcd(shard_count, 8)
    turn_count = shard_count // group_size
    fine_blocks = fine_part.reshape(turn_count, group_size * rows_per * columns, channels)
    coarse_blocks = coarse_part.reshape(turn_count, group_size * quarter, channels)

    def advance(carried, inputs):
        fine_block, coarse_block, turn_index = inputs
        lead_shard = turn_index * group_size
        fine_rows, fine_cols = fine_positions(lead_shard, group_size, rows_per, columns, half_index)
        coarse_rows, coarse_cols = coarse_positions(lead_shard, group_size, quarter, half_index)
        fine_scores = jnp.einsum(
            "qc,kc->qk", queries, fine_block, preferred_element_type=jnp.float32
        ) / math.sqrt(channels)
        coarse_scores = (
            jnp.sum(
                fine_scores.reshape(pixels, group_size, rows_per, quarter, 2), axis=(2, 4)
            ).reshape(pixels, group_size * quarter)
            * 0.25
        )
        level_zero = absorb(carried[:5], fine_scores, fine_block, fine_rows, fine_cols)
        level_one = absorb(carried[5:], coarse_scores, coarse_block, coarse_rows, coarse_cols)
        return (level_zero + level_one, None)

    result, unused = lax.scan(
        advance,
        tuple(start_state),
        (fine_blocks, coarse_blocks, jnp.arange(turn_count, dtype=jnp.int32)),
    )
    merged = merged_2(
        (
            result[0],
            result[1],
            result[2],
            result[3],
            result[4],
            result[5],
            result[6],
            result[7],
            result[8],
            result[9],
        ),
        "loop",
        combine_all,
    )
    local_index = jnp.arange(pixels, dtype=jnp.int32)
    own_rows = (row_index * rows_per + local_index // width_all).astype(jnp.float32)
    own_cols = (local_index % width_all).astype(jnp.float32)
    matched_zero, row_zero, col_zero = settle(merged[:5], own_rows, own_cols)
    matched_one, row_one, col_one = settle(merged[5:], own_rows, own_cols)
    base_motion = jnp.dot(
        jnp.concatenate([matched_zero, matched_one], axis=1),
        match_weight,
        preferred_element_type=jnp.float32,
    )
    rows_size = lax.axis_size("rows")
    slot_total = slot_target.shape[0]
    capacity = slot_total // rows_size
    counted = jnp.arange(slot_total, dtype=jnp.int32) < slot_count[0]
    owners = slot_target // pixels
    within = slot_target % pixels
    matches_owner = (
        (owners[:, None] == jnp.arange(rows_size, dtype=jnp.int32)[None, :]) & counted[:, None]
    ).astype(jnp.int32)
    ranking = jnp.sum(jnp.cumsum(matches_owner, axis=0) * matches_owner, axis=1) - 1
    landing = jnp.where(counted, owners * capacity + ranking, rows_size * capacity)
    send_hidden = (
        jnp.zeros((rows_size * capacity, hidden_size), jnp.bfloat16)
        .at[landing]
        .set(carry_hidden, mode="drop")
    )
    send_flow = (
        jnp.zeros((rows_size * capacity, 2), jnp.bfloat16).at[landing].set(carry_flow, mode="drop")
    )
    send_place = (
        jnp.full((rows_size * capacity,), pixels, jnp.int32).at[landing].set(within, mode="drop")
    )
    got_hidden, got_flow, got_place = (
        lax.all_to_all(
            send_hidden.reshape(rows_size, capacity, hidden_size),
            "rows",
            split_axis=0,
            concat_axis=0,
            tiled=True,
        ),
        lax.all_to_all(
            send_flow.reshape(rows_size, capacity, 2),
            "rows",
            split_axis=0,
            concat_axis=0,
            tiled=True,
        ),
        lax.all_to_all(
            send_place.reshape(rows_size, capacity), "rows", split_axis=0, concat_axis=0, tiled=True
        ),
    )
    place_all = got_place.reshape(-1)
    hidden = (
        jnp.zeros((pixels, hidden_size), jnp.float32)
        .at[place_all]
        .set(got_hidden.reshape(-1, hidden_size).astype(jnp.float32), mode="drop")
    )
    flow_field = (
        jnp.zeros((pixels, 2), jnp.float32)
        .at[place_all]
        .set(got_flow.reshape(-1, 2).astype(jnp.float32), mode="drop")
        .T
    )
    context_rows = context.reshape(pixels, context.shape[-1])
    grid_pixels = rows_per * width_all
    for iteration in range(ITERS):
        features = (
            (row_zero - flow_field[0]) * offset_scale,
            (col_zero - flow_field[1]) * offset_scale,
            (row_one - flow_field[0]) * offset_scale,
            (col_one - flow_field[1]) * offset_scale,
            flow_field[0] * offset_scale,
            flow_field[1] * offset_scale,
        )
        motion = base_motion
        for feature_index in range(6):
            motion = (
                motion + features[feature_index][:, None] * offset_weight[feature_index][None, :]
            )
        motion = jax.nn.relu(motion)
        inputs = jnp.concatenate([context_rows, motion.astype(jnp.bfloat16)], axis=1).reshape(
            rows_per, width_all, -1
        )
        column_rounded = hidden.astype(jnp.bfloat16).reshape(rows_per, width_all, hidden_size)
        column_joined = jnp.concatenate([column_rounded, inputs], axis=2)
        column_extended = jnp.pad(column_joined, ((0, 0), (2, 2), (0, 0)))
        column_gate_values = jax.nn.sigmoid(
            conv_along(column_extended, gate_weight[0], 1, width_all)
            + gru_bias[0, : 2 * hidden_size]
        )
        column_update_gate = column_gate_values[:, :hidden_size]
        column_reset_gate = column_gate_values[:, hidden_size:]
        column_reset_state = (
            (
                column_reset_gate
                * column_rounded.reshape(grid_pixels, hidden_size).astype(jnp.float32)
            )
            .astype(jnp.bfloat16)
            .reshape(rows_per, width_all, hidden_size)
        )
        column_reset_wide = jnp.pad(column_reset_state, ((0, 0), (2, 2), (0, 0)))
        column_candidate = jnp.tanh(
            conv_along(
                jnp.concatenate([column_reset_wide, column_extended[:, :, hidden_size:]], axis=2),
                state_weight[0],
                1,
                width_all,
            )
            + gru_bias[0, 2 * hidden_size :]
        )
        hidden = (1.0 - column_update_gate) * hidden + column_update_gate * column_candidate
        rounded = hidden.astype(jnp.bfloat16).reshape(rows_per, width_all, hidden_size)
        joined = jnp.concatenate([rounded, inputs], axis=2)
        extended = extended_2(joined, (("rows", 0),), 2)
        gate_values = jax.nn.sigmoid(
            conv_along(extended, gate_weight[1], 0, rows_per) + gru_bias[1, : 2 * hidden_size]
        )
        update_gate = gate_values[:, :hidden_size]
        reset_gate = gate_values[:, hidden_size:]
        reset_state = (
            (reset_gate * rounded.reshape(grid_pixels, hidden_size).astype(jnp.float32))
            .astype(jnp.bfloat16)
            .reshape(rows_per, width_all, hidden_size)
        )
        reset_wide = extended_2(reset_state, (("rows", 0),), 2)
        candidate = jnp.tanh(
            conv_along(
                jnp.concatenate([reset_wide, extended[:, :, hidden_size:]], axis=2),
                state_weight[1],
                0,
                rows_per,
            )
            + gru_bias[1, 2 * hidden_size :]
        )
        hidden = (1.0 - update_gate) * hidden + update_gate * candidate
        lifted = jax.nn.relu(
            jnp.dot(hidden.astype(jnp.bfloat16), head_weight, preferred_element_type=jnp.float32)
        ).astype(jnp.bfloat16)
        flow_field = flow_field + jnp.einsum(
            "kc,pc->kp", delta_weight, lifted, preferred_element_type=jnp.float32
        )
    hidden_grid = hidden.reshape(rows_per, width_all, hidden_size)
    flow_grid = flow_field.reshape(2, rows_per, width_all)
    return (hidden_grid, flow_grid)


def solution(mesh):
    return jax.shard_map(
        local,
        mesh=mesh,
        in_specs=(
            P(("groups", "rows"), None, None),
            P(("groups", "rows"), "loop", None),
            P(("groups", "rows"), None, None),
            P(("groups", "rows"), None),
            P(("groups", "rows"), None),
            P(("groups", "rows")),
            P(("groups", "rows")),
            P(),
            P(),
            P(),
            P(),
            P(),
            P(),
            P(),
        ),
        out_specs=(P(("groups", "rows"), None, None), P(None, ("groups", "rows"), None)),
        check_vma=False,
    )
```

profile of v0, /device:TPU:0, one launch (start us, length us, event | category | flops | bytes accessed | tf_op | source)
XLA Modules:
  0.0 244.0 jit_solution(5791564520391139311)
XLA Ops:
  7.2 0.7 all-gather.16.cloned.1.call-update
  8.6 0.7 add_select_fusion.3
  9.3 2.3 reduce-window.6
  12.2 6.2 %scatter_custom_fusion = s32[1536]{0:T(1024)S(1)} fusion(s32[1536]{0:T(1024)S(1)} %compare_select_fusion.1, s32[1536]{0:T(1024)S(1)} %get-tuple-element.165, s32[]{:T(128)} %constant.196.clone.1), kind=kCustom, calls=%fused_computation.374 | custom fusion | bytes 6148 | tf_op jit(solution)/shard_map/scatter | solution.py:228
  18.4 0.7 all_to_all.12
  19.1 7.3 %all-to-all-start = ((s32[8,1,192]{2,1,0:T(1,128)}), s32[8,1,192]{2,1,0:T(1,128)S(1)}, u32[]{:S(2)}, u32[]{:S(2)}) async-start(s32[8,1,192]{2,1,0:T(1,128)} %all_to_all.12), calls=%async_computation | async-start | bytes 16384 | tf_op jit(solution)/shard_map/all_to_all | solution.py:245
  26.4 0.9 slice.393
  27.2 0.9 slice.395
  28.1 0.9 slice.396
  29.0 0.9 slice.394
  29.9 0.8 fusion.308
  30.6 0.9 slice_bitcast_fusion.7
  31.6 0.8 slice_bitcast_fusion
  32.3 0.9 copy.30
  33.3 4.6 %scatter_custom_fusion.3 = bf16[1536,2]{1,0:T(8,128)(2,1)S(1)} fusion(s32[1536]{0:T(1024)S(1)} %compare_select_fusion.1, bf16[1536,2]{1,0:T(8,128)(2,1)S(1)} %copy.30, bf16[]{:T(256)} %constant.205.clone.1), kind=kCustom, calls=%fused_computation.220 | custom fusion | bytes 6146 | tf_op jit(solution)/shard_map/scatter | solution.py:225
  37.8 0.8 copy.31
  38.6 6.0 %all-to-all-start.2 = ((bf16[8,192,2]{1,2,0:T(2,128)(2,1)}), bf16[8,192,2]{1,2,0:T(2,128)(2,1)S(1)}, u32[]{:S(2)}, u32[]{:S(2)}) async-start(bf16[8,192,2]{1,2,0:T(2,128)(2,1)} %copy.31), calls=%async_computation.2 | async-start | bytes 16384 | tf_op jit(solution)/shard_map/all_to_all | solution.py:238
  44.6 5.5 %scatter_custom_fusion.1 = bf16[1536,128]{1,0:T(8,128)(2,1)} fusion(s32[1536]{0:T(1024)S(1)} %compare_select_fusion.1, bf16[1536,128]{1,0:T(8,128)(2,1)} %param.17, bf16[]{:T(256)} %constant.205.clone.1), kind=kCustom, calls=%fused_computation.222 | custom fusion | bytes 393728 | tf_op jit(solution)/shard_map/scatter | solution.py:222
  50.2 1.0 all-to-all-done.2
  51.1 5.0 %all-to-all-start.1 = ((bf16[8,192,128]{2,1,0:T(8,128)(2,1)}), bf16[8,192,128]{2,1,0:T(8,128)(2,1)S(1)}, u32[]{:S(2)}, u32[]{:S(2)}) async-start(bf16[8,192,128]{2,1,0:T(8,128)(2,1)} %bitcast.3), calls=%async_computation.1 | async-start | bytes 786432 | tf_op jit(solution)/shard_map/all_to_all | solution.py:231
  56.2 34.6 %all_gather.60 = bf16[8,64,256]{2,1,0:T(8,128)(2,1)S(1)} all-gather(bf16[1,64,256]{2,1,0:T(8,128)(2,1)S(1)} %multiply_convert_fusion), channel_id=1, replica_groups=mesh['groups'=2,'rows'=8,'loop'=2] {'rows'}, dimensions={0}, use_global_device_ids=true | all-gather | bytes 294912 | tf_op jit(solution)/shard_map/all_gather | solution.py:153
  91.3 4.4 %scatter_custom_fusion.4 = f32[512,2]{1,0:T(8,128)S(1)} fusion(s32[1536]{0:T(1024)S(1)} %fusion.246, f32[1536,2]{1,0:T(8,128)S(1)} %bitcast.354, f32[]{:T(128)} %constant.195.clone.1), kind=kCustom, calls=%fused_computation.245 | custom fusion | bytes 4100 | tf_op jit(solution)/shard_map/scatter | solution.py:258
  95.8 4.6 %scatter_custom_fusion.2 = f32[512,128]{1,0:T(8,128)S(1)} fusion(s32[1536]{0:T(1024)S(1)} %fusion.246, bf16[1536,128]{1,0:T(8,128)(2,1)S(1)} %bitcast.319, f32[]{:T(128)} %constant.195.clone.1), kind=kCustom, calls=%fused_computation.118 | custom fusion | flops 196608 | bytes 655364 | tf_op jit(solution)/shard_map/scatter | solution.py:253
  100.5 3.9 %fusion.309 = (f32[512]{0:T(512)S(1)}, f32[512,2048]{1,0:T(8,128)}) fusion(bf16[512,256]{1,0:T(8,128)(2,1)S(1)} %bitcast.295, bf16[2048,256]{1,0:T(8,128)(2,1)} %bitcast.351), kind=kOutput, calls=%fused_computation.450 | convolution fusion | flops 538967552 | bytes 5507072 | tf_op jit(solution)/shard_map/while/body/eval_jaxpr/qc,kc->qk/dot_general | solution.py:164
  104.5 5.4 %copy.29 = f32[512,2048]{0,1:T(8,128)} copy(f32[512,2048]{1,0:T(8,128)} %get-tuple-element.222) | data formatting | bytes 8388608 | tf_op jit(solution)/shard_map/while/body/eval_jaxpr/div | solution.py:164
  109.9 5.8 %reshape.919 = f32[512,8,2,64,2]{0,4,3,2,1:T(2,128)} reshape(f32[512,2048]{0,1:T(8,128)} %copy.29) | data formatting | bytes 8388608 | tf_op jit(solution)/shard_map/while/body/eval_jaxpr/reshape | solution.py:169
  115.7 5.3 %reduce_sum.94 = f32[512,8,64]{0,2,1:T(8,128)S(1)} reduce(f32[512,8,2,64,2]{0,4,3,2,1:T(2,128)} %reshape.919, f32[]{:T(128)} %constant.195.clone.1), dimensions={2,4}, to_apply=%region_8.9 | reduce | flops 786432 | bytes 5242884 | tf_op jit(solution)/shard_map/while/body/eval_jaxpr/reduce_sum | solution.py:168
  121.1 3.6 %multiply_reduce_fusion.1 = (f32[512]{0:T(512)S(1)}, f32[512]{0:T(512)S(1)}, f32[512]{0:T(512)S(1)}) fusion(f32[512,2048]{1,0:T(8,128)} %get-tuple-element.222, f32[2048]{0:T(1024)S(1)} %get-tuple-element.231, f32[512]{0:T(512)S(1)} %get-tuple-element.221, f32[2048]{0:T(1024)S(1)} %get-tuple-element.232), kind=kLoop, calls=%fused_computation.6 | loop fusion | flops 6289920 | bytes 4218880 | tf_op jit(solution)/shard_map/while/body/eval_jaxpr/reduce_sum | solution.py:52
  124.8 1.8 all-gather.8
  126.5 1.8 all-gather.9
  128.7 1.2 fusion.38
  130.0 1.8 all-gather.10
  131.7 1.8 all-gather.11
  133.5 1.8 all-gather.7
  135.3 1.8 all-gather.6
  137.1 1.8 all-gather.5
  138.8 2.0 all-gather.4
  140.9 3.8 %fusion.35 = f32[512,256]{1,0:T(8,128)} fusion(bf16[2048,256]{1,0:T(8,128)(2,1)S(1)} %bitcast.352, f32[512,2048]{1,0:T(8,128)} %get-tuple-element.222, f32[512]{0:T(512)S(1)} %get-tuple-element.221, f32[512]{0:T(512)S(1)} %get-tuple-element.209), kind=kOutput, calls=%fused_computation.61 | convolution fusion | flops 539099136 | bytes 5771264 | tf_op jit(solution)/shard_map/while/body/eval_jaxpr/dot_general | solution.py:49
  144.8 1.5 fusion.91
  146.2 5.2 %all-gather.18.cloned.1.call-done = f32[1024,256]{1,0:T(8,128)} async-done(((f32[512,256]{1,0:T(8,128)}), f32[1024,256]{1,0:T(8,128)}) %all-gather.18.cloned.1.call-update) | async-done | bytes 1048592 | tf_op jit(solution)/shard_map/all_gather | solution.py:15
  151.4 1.5 fusion.90
  152.9 0.5 maximum_convert_fusion.1
  153.9 1.1 copy-done.3
  157.0 0.8 copy-done.2
  159.3 1.3 collective-permute-start.1
  160.6 4.6 %collective-permute-start = (bf16[2,256,384]{2,1,0:T(8,128)(2,1)S(1)}, bf16[2,256,384]{2,1,0:T(8,128)(2,1)S(1)}, u32[]{:S(2)}, u32[]{:S(2)}) collective-permute-start(bf16[2,256,384]{2,1,0:T(8,128)(2,1)S(1)} %pad_maximum_fusion.14), channel_id=1, source_target_pairs={{0,2},{2,4},{4,6},{6,8},{8,10},{10,12},{12,14},{1,3},{3,5},{5,7},{... | collective-permute-start | bytes 1179656 | tf_op jit(solution)/shard_map/ppermute | solution.py:29
  165.5 7.0 %collective-permute-done.1 = bf16[2,256,384]{2,1,0:T(8,128)(2,1)S(1)} collective-permute-done((bf16[2,256,384]{2,1,0:T(8,128)(2,1)S(1)}, bf16[2,256,384]{2,1,0:T(8,128)(2,1)S(1)}, u32[]{:S(2)}, u32[]{:S(2)}) %collective-permute-start.1) | collective-permute-done | bytes 393248 | tf_op jit(solution)/shard_map/ppermute | solution.py:32
  172.8 8.3 %collective-permute-done = bf16[2,256,384]{2,1,0:T(8,128)(2,1)S(1)} collective-permute-done((bf16[2,256,384]{2,1,0:T(8,128)(2,1)S(1)}, bf16[2,256,384]{2,1,0:T(8,128)(2,1)S(1)}, u32[]{:S(2)}, u32[]{:S(2)}) %collective-permute-start) | collective-permute-done | bytes 393248 | tf_op jit(solution)/shard_map/ppermute | solution.py:29
  182.1 1.3 collective-permute-start.3
  183.4 5.0 %collective-permute-start.2 = (bf16[2,256,128]{2,1,0:T(8,128)(2,1)S(1)}, bf16[2,256,128]{2,1,0:T(8,128)(2,1)S(1)}, u32[]{:S(2)}, u32[]{:S(2)}) collective-permute-start(bf16[2,256,128]{2,1,0:T(8,128)(2,1)S(1)} %bitcast.358), channel_id=1, source_target_pairs={{0,2},{2,4},{4,6},{6,8},{8,10},{10,12},{12,14},{1,3},{3,5},{5,7},{... | collective-permute-start | bytes 393224 | tf_op jit(solution)/shard_map/ppermute | solution.py:29
  188.4 1.7 collective-permute-done.3
  190.2 3.0 %collective-permute-done.2 = bf16[2,256,128]{2,1,0:T(8,128)(2,1)S(1)} collective-permute-done((bf16[2,256,128]{2,1,0:T(8,128)(2,1)S(1)}, bf16[2,256,128]{2,1,0:T(8,128)(2,1)S(1)}, u32[]{:S(2)}, u32[]{:S(2)}) %collective-permute-start.2) | collective-permute-done | bytes 131104 | tf_op jit(solution)/shard_map/ppermute | solution.py:29
  195.0 0.4 fusion.74
  195.4 0.5 maximum_convert_fusion
  196.3 0.6 copy-done.4
  200.3 1.3 collective-permute-start.5
  201.6 5.3 %collective-permute-start.4 = (bf16[2,256,384]{2,1,0:T(8,128)(2,1)S(1)}, bf16[2,256,384]{2,1,0:T(8,128)(2,1)S(1)}, u32[]{:S(2)}, u32[]{:S(2)}) collective-permute-start(bf16[2,256,384]{2,1,0:T(8,128)(2,1)S(1)} %pad_maximum_fusion.18), channel_id=1, source_target_pairs={{0,2},{2,4},{4,6},{6,8},{8,10},{10,12},{12,14},{1,3},{3,5},{5,7},{... | collective-permute-start | bytes 1179656 | tf_op jit(solution)/shard_map/ppermute | solution.py:29
  207.2 6.8 %collective-permute-done.5 = bf16[2,256,384]{2,1,0:T(8,128)(2,1)S(1)} collective-permute-done((bf16[2,256,384]{2,1,0:T(8,128)(2,1)S(1)}, bf16[2,256,384]{2,1,0:T(8,128)(2,1)S(1)}, u32[]{:S(2)}, u32[]{:S(2)}) %collective-permute-start.5) | collective-permute-done | bytes 393248 | tf_op jit(solution)/shard_map/ppermute | solution.py:32
  214.3 8.3 %collective-permute-done.4 = bf16[2,256,384]{2,1,0:T(8,128)(2,1)S(1)} collective-permute-done((bf16[2,256,384]{2,1,0:T(8,128)(2,1)S(1)}, bf16[2,256,384]{2,1,0:T(8,128)(2,1)S(1)}, u32[]{:S(2)}, u32[]{:S(2)}) %collective-permute-start.4) | collective-permute-done | bytes 393248 | tf_op jit(solution)/shard_map/ppermute | solution.py:29
  223.6 1.3 collective-permute-start.7
  224.9 5.0 %collective-permute-start.6 = (bf16[2,256,128]{2,1,0:T(8,128)(2,1)S(1)}, bf16[2,256,128]{2,1,0:T(8,128)(2,1)S(1)}, u32[]{:S(2)}, u32[]{:S(2)}) collective-permute-start(bf16[2,256,128]{2,1,0:T(8,128)(2,1)S(1)} %bitcast.361), channel_id=1, source_target_pairs={{0,2},{2,4},{4,6},{6,8},{8,10},{10,12},{12,14},{1,3},{3,5},{5,7},{... | collective-permute-start | bytes 393224 | tf_op jit(solution)/shard_map/ppermute | solution.py:29
  230.0 1.7 collective-permute-done.7
  231.7 3.0 %collective-permute-done.6 = bf16[2,256,128]{2,1,0:T(8,128)(2,1)S(1)} collective-permute-done((bf16[2,256,128]{2,1,0:T(8,128)(2,1)S(1)}, bf16[2,256,128]{2,1,0:T(8,128)(2,1)S(1)}, u32[]{:S(2)}, u32[]{:S(2)}) %collective-permute-start.6) | collective-permute-done | bytes 131104 | tf_op jit(solution)/shard_map/ppermute | solution.py:29
  236.9 0.6 reshape.965
  (125 shorter events, 16.7 us)
Async XLA Ops:
  7.2 93.4 %copy-start = (bf16[2,256,256]{2,1,0:T(8,128)(2,1)S(1)}, bf16[2,256,256]{2,1,0:T(8,128)(2,1)}, u32[]{:S(2)}) copy-start(bf16[2,256,256]{2,1,0:T(8,128)(2,1)} %param.14) | copy-start | bytes 786436
  7.2 93.3 %all-gather.16.cloned.1.call-start = ((), (), s32[]{:S(2)}) async-start(), calls=%async_computation.3 | async-start | bytes 1179648 | tf_op jit(solution)/shard_map/all_gather | solution.py:151
  19.1 19.5 %all-to-all-start = ((s32[8,1,192]{2,1,0:T(1,128)}), s32[8,1,192]{2,1,0:T(1,128)S(1)}, u32[]{:S(2)}, u32[]{:S(2)}) async-start(s32[8,1,192]{2,1,0:T(1,128)} %all_to_all.12), calls=%async_computation | async-start | bytes 16384 | tf_op jit(solution)/shard_map/all_to_all | solution.py:245
  38.6 12.5 %all-to-all-start.2 = ((bf16[8,192,2]{1,2,0:T(2,128)(2,1)}), bf16[8,192,2]{1,2,0:T(2,128)(2,1)S(1)}, u32[]{:S(2)}, u32[]{:S(2)}) async-start(bf16[8,192,2]{1,2,0:T(2,128)(2,1)} %copy.31), calls=%async_computation.2 | async-start | bytes 16384 | tf_op jit(solution)/shard_map/all_to_all | solution.py:238
  51.1 44.7 %all-to-all-start.1 = ((bf16[8,192,128]{2,1,0:T(8,128)(2,1)}), bf16[8,192,128]{2,1,0:T(8,128)(2,1)S(1)}, u32[]{:S(2)}, u32[]{:S(2)}) async-start(bf16[8,192,128]{2,1,0:T(8,128)(2,1)} %bitcast.3), calls=%async_computation.1 | async-start | bytes 786432 | tf_op jit(solution)/shard_map/all_to_all | solution.py:231
  56.2 88.6 %all-gather.20.cloned.1.call-start = ((), (), s32[]{:S(2)}) async-start(), calls=%async_computation.5 | async-start | bytes 1572864 | tf_op jit(solution)/shard_map/all_gather | solution.py:15
  128.3 12.5 %copy-start.5 = (bf16[8,256,256]{2,1,0:T(8,128)(2,1)S(1)}, bf16[8,256,256]{2,1,0:T(8,128)(2,1)}, u32[]{:S(2)}) copy-start(bf16[8,256,256]{2,1,0:T(8,128)(2,1)} %all-gather.16.cloned.1.call-done) | copy-start | bytes 3145732
  129.9 21.5 %all-gather.18.cloned.1.call-start = ((), (), s32[]{:S(2)}) async-start(), calls=%async_computation.4 | async-start | bytes 1572864 | tf_op jit(solution)/shard_map/all_gather | solution.py:15
  144.6 8.3 %copy-start.9 = (bf16[512,128]{1,0:T(8,128)(2,1)S(1)}, bf16[512,128]{1,0:T(8,128)(2,1)}, u32[]{:S(2)}) copy-start(bf16[512,128]{1,0:T(8,128)(2,1)} %param.21) | copy-start | bytes 393220
  146.2 7.2 %copy-start.1 = (bf16[2,256,128]{2,1,0:T(8,128)(2,1)S(1)}, bf16[2,256,128]{2,1,0:T(8,128)(2,1)}, u32[]{:S(2)}) copy-start(bf16[2,256,128]{2,1,0:T(8,128)(2,1)} %param.16) | copy-start | bytes 393220
  153.5 1.5 copy-start.3
  156.6 1.2 copy-start.2
  159.3 13.2 %collective-permute-start.1 = (bf16[2,256,384]{2,1,0:T(8,128)(2,1)S(1)}, bf16[2,256,384]{2,1,0:T(8,128)(2,1)S(1)}, u32[]{:S(2)}, u32[]{:S(2)}) collective-permute-start(bf16[2,256,384]{2,1,0:T(8,128)(2,1)S(1)} %pad_maximum_fusion.14), channel_id=1, source_target_pairs={{2,0},{4,2},{6,4},{8,6},{10,8},{12,10},{14,12},{3,1},{5,3},{7,5},{... | collective-permute-start | bytes 1179656 | tf_op jit(solution)/shard_map/ppermute | solution.py:32
  160.6 20.5 %collective-permute-start = (bf16[2,256,384]{2,1,0:T(8,128)(2,1)S(1)}, bf16[2,256,384]{2,1,0:T(8,128)(2,1)S(1)}, u32[]{:S(2)}, u32[]{:S(2)}) collective-permute-start(bf16[2,256,384]{2,1,0:T(8,128)(2,1)S(1)} %pad_maximum_fusion.14), channel_id=1, source_target_pairs={{0,2},{2,4},{4,6},{6,8},{8,10},{10,12},{12,14},{1,3},{3,5},{5,7},{... | collective-permute-start | bytes 1179656 | tf_op jit(solution)/shard_map/ppermute | solution.py:29
  182.1 8.1 %collective-permute-start.3 = (bf16[2,256,128]{2,1,0:T(8,128)(2,1)S(1)}, bf16[2,256,128]{2,1,0:T(8,128)(2,1)S(1)}, u32[]{:S(2)}, u32[]{:S(2)}) collective-permute-start(bf16[2,256,128]{2,1,0:T(8,128)(2,1)S(1)} %bitcast.357), channel_id=1, source_target_pairs={{2,0},{4,2},{6,4},{8,6},{10,8},{12,10},{14,12},{3,1},{5,3},{7,5},{... | collective-permute-start | bytes 393224 | tf_op jit(solution)/shard_map/ppermute | solution.py:32
  183.4 9.7 %collective-permute-start.2 = (bf16[2,256,128]{2,1,0:T(8,128)(2,1)S(1)}, bf16[2,256,128]{2,1,0:T(8,128)(2,1)S(1)}, u32[]{:S(2)}, u32[]{:S(2)}) collective-permute-start(bf16[2,256,128]{2,1,0:T(8,128)(2,1)S(1)} %bitcast.358), channel_id=1, source_target_pairs={{0,2},{2,4},{4,6},{6,8},{8,10},{10,12},{12,14},{1,3},{3,5},{5,7},{... | collective-permute-start | bytes 393224 | tf_op jit(solution)/shard_map/ppermute | solution.py:29
  194.1 0.9 copy-start.7
  194.1 0.9 copy-start.8
  195.4 1.6 copy-start.4
  200.3 13.7 %collective-permute-start.5 = (bf16[2,256,384]{2,1,0:T(8,128)(2,1)S(1)}, bf16[2,256,384]{2,1,0:T(8,128)(2,1)S(1)}, u32[]{:S(2)}, u32[]{:S(2)}) collective-permute-start(bf16[2,256,384]{2,1,0:T(8,128)(2,1)S(1)} %pad_maximum_fusion.18), channel_id=1, source_target_pairs={{2,0},{4,2},{6,4},{8,6},{10,8},{12,10},{14,12},{3,1},{5,3},{7,5},{... | collective-permute-start | bytes 1179656 | tf_op jit(solution)/shard_map/ppermute | solution.py:32
  201.6 21.0 %collective-permute-start.4 = (bf16[2,256,384]{2,1,0:T(8,128)(2,1)S(1)}, bf16[2,256,384]{2,1,0:T(8,128)(2,1)S(1)}, u32[]{:S(2)}, u32[]{:S(2)}) collective-permute-start(bf16[2,256,384]{2,1,0:T(8,128)(2,1)S(1)} %pad_maximum_fusion.18), channel_id=1, source_target_pairs={{0,2},{2,4},{4,6},{6,8},{8,10},{10,12},{12,14},{1,3},{3,5},{5,7},{... | collective-permute-start | bytes 1179656 | tf_op jit(solution)/shard_map/ppermute | solution.py:29
  223.6 8.1 %collective-permute-start.7 = (bf16[2,256,128]{2,1,0:T(8,128)(2,1)S(1)}, bf16[2,256,128]{2,1,0:T(8,128)(2,1)S(1)}, u32[]{:S(2)}, u32[]{:S(2)}) collective-permute-start(bf16[2,256,128]{2,1,0:T(8,128)(2,1)S(1)} %bitcast.360), channel_id=1, source_target_pairs={{2,0},{4,2},{6,4},{8,6},{10,8},{12,10},{14,12},{3,1},{5,3},{7,5},{... | collective-permute-start | bytes 393224 | tf_op jit(solution)/shard_map/ppermute | solution.py:32
  224.9 9.7 %collective-permute-start.6 = (bf16[2,256,128]{2,1,0:T(8,128)(2,1)S(1)}, bf16[2,256,128]{2,1,0:T(8,128)(2,1)S(1)}, u32[]{:S(2)}, u32[]{:S(2)}) collective-permute-start(bf16[2,256,128]{2,1,0:T(8,128)(2,1)S(1)} %bitcast.361), channel_id=1, source_target_pairs={{0,2},{2,4},{4,6},{6,8},{8,10},{10,12},{12,14},{1,3},{3,5},{5,7},{... | collective-permute-start | bytes 393224 | tf_op jit(solution)/shard_map/ppermute | solution.py:29
  236.5 1.0 copy-start.6
Sparse Core Ops, SparseCore 0:
  10.1 42.8 all-gather.15
  130.0 6.6 all-gather.19
  144.8 6.6 all-gather.17
where the time goes:
time: 245 us; the launch traced here: 244 us
  blocking collectives  49 us (20%)
  waiting for transfers between devices  46.7 us (19%)
  local copies, waits for them, and re-layouts  46.1 us (19%)
  starting transfers between devices  43.5 us (18%)
  other arithmetic  22 us (9%)
  matrix products  21.5 us (9%)
  between operations  15.3 us (6%)
    all_gather x1, blocking collectives, local(): coarse_part = lax.all_gather(coarse_local, 'rows', axis=0, tiled=True)  34.6 us
    ppermute x4, waiting for transfers between devices, extended_2(): lax.ppermute(lax.slice_in_dim(block, block.shape[dim] - width, None, axis...  22.5 us
    ppermute x4, starting transfers between devices, extended_2(): lax.ppermute(lax.slice_in_dim(block, block.shape[dim] - width, None, axis...  19.9 us
    ppermute x4, waiting for transfers between devices, extended_2(): lax.ppermute(lax.slice_in_dim(block, 0, width, axis=dim), axis, backward)  17.3 us
    all_gather x8, blocking collectives, merged_2(): everything = jax.tree.map(lambda part: lax.all_gather(part, axis), x)  14.4 us
    dot_general x40, matrix products, conv_along(): jnp.dot(window.reshape(-1, window.shape[-1]), weights[tap_index], preferr...  11.3 us
    all_to_all x1, starting transfers between devices, local(): lax.all_to_all(send_place.reshape(rows_size, capacity), 'rows', split_axi...  7.28 us
    scatter x1, local copies, waits for them, and re-layouts, local(): jnp.full((rows_size * capacity,), pixels, jnp.int32).at[landing]  6.18 us
  transfers between devices with their start and end apart: 14, of which 10 were waited for; matrix products, arithmetic and copies ran while one was open for 18% of the time, Pallas kernels for 0%

commit v1 on v0

v1 whole, which is shorter than its diff:
```python
import functools
import math

import jax
import jax.numpy as jnp
from jax import lax
from jax.experimental import pallas as pl
from jax.experimental.pallas import tpu as pltpu
from jax.sharding import PartitionSpec as P

ITERS = 2
WIN = 32
HALO = 8
TILE = 512
OFFSET_SCALE = 0.03125
F32 = jnp.float32
BF16 = jnp.bfloat16
VMEM = pltpu.VMEM
NT = (((1,), (1,)), ((), ()))


def iota(shape, dim):
    return lax.broadcasted_iota(jnp.int32, shape, dim)


def round_up(value, step):
    return -(-value // step) * step


def dot(a, b):
    return jnp.dot(a, b, preferred_element_type=F32)


def dot_nt(a, b):
    return lax.dot_general(a, b, NT, preferred_element_type=F32)


def vmem_specs(count):
    return [pl.BlockSpec(memory_space=VMEM)] * count


def smem_spec():
    return pl.BlockSpec(memory_space=pltpu.SMEM)


def loop(count, body, carry):
    return lax.fori_loop(0, count, body, carry, unroll=count <= 4)


def call(kernel, out_shape, in_specs, scratch, cost, *args):
    single = not isinstance(out_shape, (tuple, list))
    return pl.pallas_call(
        kernel,
        out_shape=out_shape,
        in_specs=in_specs,
        out_specs=vmem_specs(1)[0] if single else vmem_specs(len(out_shape)),
        scratch_shapes=scratch,
        compiler_params=pltpu.CompilerParams(vmem_limit_bytes=56 * 1024 * 1024),
        cost_estimate=pl.CostEstimate(flops=cost[0], bytes_accessed=cost[1], transcendentals=cost[2]),
    )(*args)


def pack_kernel(dests, cap, pixels, count_ref, target_ref, flow_ref, hidden_ref, out_ref):
    slots = target_ref.shape[1]
    target = target_ref[...]
    counted = iota((1, slots), 1) < count_ref[0]
    owner = target // pixels
    within = target % pixels
    belongs = (iota((dests, slots), 0) == owner) & counted
    member = jnp.where(belongs, 1.0, 0.0)
    upper = jnp.where(iota((128, 128), 0) <= iota((128, 128), 1), 1.0, 0.0).astype(BF16)
    before = jnp.zeros((dests, 1), F32)
    ranks = []
    for start in range(0, slots, 128):
        running = dot(member[:, start : start + 128].astype(BF16), upper) + before
        before = running[:, 127:128]
        ranks.append(running)
    rank = jnp.concatenate(ranks, axis=1) - 1.0
    place_at = jnp.sum(
        jnp.where(belongs, rank + iota((dests, slots), 0).astype(F32) * cap, 0.0), axis=0, keepdims=True
    )
    landing = jnp.where(counted, place_at, -1.0).astype(jnp.int32)
    row = iota((8, slots), 0)
    flow = flow_ref[...]
    side = jnp.where(row == 0, flow[0:1], 0.0)
    side = jnp.where(row == 1, flow[1:2], side)
    side = jnp.where(row == 2, (within // 256).astype(F32), side)
    side = jnp.where(row == 3, (within % 256).astype(F32), side)
    side = jnp.where(row == 4, 1.0, side).astype(BF16)
    hidden = hidden_ref[...]
    rows_hidden = round_up(cap, 16)
    together = max(1, min(dests, 192 // cap))
    for first in range(0, dests, together):
        spots = together * cap
        chosen = jnp.where(iota((spots, slots), 0) + first * cap == landing, 1.0, 0.0).astype(BF16)
        moved = dot(chosen, hidden)
        moved_side = dot_nt(side, chosen)
        for k in range(together):
            out_ref[first + k, 0:cap, :] = moved[k * cap : (k + 1) * cap].astype(BF16)
            for t in range(-(-cap // 128)):
                width = min(128, cap - t * 128)
                piece = moved_side[:, k * cap + t * 128 : k * cap + t * 128 + width]
                if width < 128:
                    piece = jnp.concatenate([piece, jnp.zeros((8, 128 - width), F32)], axis=1)
                base = rows_hidden + 8 * t
                out_ref[first + k, base : base + 8, :] = piece.astype(BF16)


def place_kernel(cap, half_wide, rows_per, where_ref, got_ref, ow_ref, hidden_ref, flow_ref, term_ref, wide_hidden, wide_term):
    half = where_ref[1]
    dests = got_ref.shape[0]
    pixels = flow_ref.shape[1]
    width = pixels // rows_per
    rows_hidden = round_up(cap, 16)
    hidden = jnp.zeros((pixels, 128), F32)
    flow = jnp.zeros((8, pixels), F32)
    for j in range(dests):
        pieces = []
        for t in range(-(-cap // 128)):
            base = rows_hidden + 8 * t
            pieces.append(got_ref[j, base : base + 8, 0 : min(128, cap - t * 128)].astype(F32))
        side = pieces[0] if len(pieces) == 1 else jnp.concatenate(pieces, axis=1)
        place = jnp.where(side[4:5] > 0.5, side[2:3] * 256.0 + side[3:4], -1.0).astype(jnp.int32)
        chosen = jnp.where(iota((pixels, cap), 0) == place, 1.0, 0.0).astype(BF16)
        hidden = hidden + dot(chosen, got_ref[j, 0:cap, :])
        flow = flow + dot_nt(side.astype(BF16), chosen)
    flow_ref[...] = flow
    columns = flow.T
    ow = ow_ref[...]
    term = columns[:, 0:1] * (OFFSET_SCALE * (ow[4:5] - ow[0:1] - ow[2:3])) + columns[:, 1:2] * (
        OFFSET_SCALE * (ow[5:6] - ow[1:2] - ow[3:4])
    )
    start = pl.multiple_of(half * (width // 2), 128)
    for wide, value, out in ((wide_hidden, hidden, hidden_ref), (wide_term, term, term_ref)):
        wide[...] = jnp.zeros_like(wide)
        for r in range(rows_per):
            wide[r, HALO : HALO + width, :] = value[r * width : (r + 1) * width]
            out[r] = wide[r, pl.ds(start, half_wide), :].astype(out.dtype)


def match_kernel(
    count, flip, half_wide, rows_per, where_ref, queries_ref, weight_ref, ow_ref, *refs
):
    key_refs, (keep_ref, send_ref, fine, coarse, scores, mixed, wide) = refs[:count], refs[count:]
    me, half = where_ref[0], where_ref[1]
    pixels, channels = queries_ref.shape
    width = pixels // rows_per
    columns = width // 2
    quarter = columns // 2
    chunks = fine.shape[0]
    shards = chunks * 2
    per_ref = shards // count
    spread = jnp.where(
        iota((columns, columns), 1)
        == jnp.where(iota((columns, columns), 0) < quarter, 2 * iota((columns, columns), 0), 2 * (iota((columns, columns), 0) - quarter) + 1),
        1.0,
        0.0,
    ).astype(BF16)

    def sort_shard(ref, m, shard, lane):
        even, odd = [], []
        for r in range(rows_per):
            parted = dot(spread, ref[m, r])
            even.append(parted[:quarter])
            odd.append(parted[quarter:])
            for p, part in ((0, even[-1]), (1, odd[-1])):
                g = 2 * r + p
                fine[shard, g * 2 * quarter + lane * quarter : g * 2 * quarter + (lane + 1) * quarter, :] = part.astype(BF16)
        pooled = (even[0] + odd[0] + even[1] + odd[1]) * 0.25
        coarse[shard, lane * quarter : (lane + 1) * quarter, :] = pooled.astype(BF16)

    if per_ref == 1:
        for m in range(shards):
            sort_shard(key_refs[m], 0, m // 2, m % 2)
    else:
        def sort_chunk(c, carry):
            for lane in range(2):
                sort_shard(key_refs[0], c * 2 + lane, c, lane)
            return carry

        lax.fori_loop(0, chunks, sort_chunk, 0)

    group = 2 * quarter
    tile = scores.shape[1]
    lane = iota((1, group), 1)
    lane_col = ((lane % quarter) * 2 + half * columns).astype(F32)
    ow = ow_ref[...] * OFFSET_SCALE
    weight = weight_ref[...]

    def lane_row(c):
        arrival = c * 2 + lane // quarter
        shard = lax.bitwise_xor(arrival, me) if flip else arrival
        return (shard * rows_per).astype(F32)

    wide[...] = jnp.zeros_like(wide)

    def one_tile(t, carry):
        first = pl.multiple_of(t * tile, tile)
        queries = queries_ref[pl.ds(first, tile), :] * jnp.asarray(1.0 / math.sqrt(channels), BF16)

        def score(c, peaks):
            values = dot_nt(queries, fine[c])
            scores[c] = values
            parts = [values[:, g * group : (g + 1) * group] for g in range(4)]
            blended = (parts[0] + parts[1] + parts[2] + parts[3]) * 0.25
            high = jnp.maximum(jnp.maximum(parts[0], parts[1]), jnp.maximum(parts[2], parts[3]))
            return jnp.maximum(peaks[0], high), jnp.maximum(peaks[1], blended)

        low = jnp.full((tile, group), -jnp.inf, F32)
        peaks = loop(chunks, score, (low, low))
        peak_fine = jnp.max(peaks[0], axis=1, keepdims=True)
        peak_coarse = jnp.max(peaks[1], axis=1, keepdims=True)

        def absorb(c, so_far):
            total, below, right, rows, c_total, c_rows, acc_fine, acc_coarse = so_far
            parts = [scores[c, :, g * group : (g + 1) * group] for g in range(4)]
            blended = (parts[0] + parts[1] + parts[2] + parts[3]) * 0.25
            expo = [jnp.exp(part - peak_fine) for part in parts]
            c_expo = jnp.exp(blended - peak_coarse)
            lower = expo[2] + expo[3]
            everything = expo[0] + expo[1] + lower
            at = lane_row(c)
            weights = jnp.concatenate([e.astype(BF16) for e in expo], axis=1)
            return (
                total + everything,
                below + lower,
                right + (expo[1] + expo[3]),
                rows + everything * at,
                c_total + c_expo,
                c_rows + c_expo * at,
                acc_fine + dot(weights, fine[c]),
                acc_coarse + dot(c_expo.astype(BF16), coarse[c]),
            )

        zero = jnp.zeros((tile, group), F32)
        blank = jnp.zeros((tile, channels), F32)
        total, below, right, rows, c_total, c_rows, acc_fine, acc_coarse = loop(
            chunks, absorb, (zero, zero, zero, zero, zero, zero, blank, blank)
        )

        def over(value):
            return jnp.sum(value, axis=1, keepdims=True)

        pixel = first + iota((tile, 1), 0)
        own_row = (me * rows_per + pixel // width).astype(F32)
        own_col = (pixel % width).astype(F32)
        fine_sum, coarse_sum = over(total), over(c_total)
        fine_row = over(rows + below) / fine_sum - own_row
        fine_col = over(total * lane_col + right) / fine_sum - own_col
        coarse_row = over(c_rows) / coarse_sum + 0.5 - own_row
        coarse_col = over(c_total * lane_col) / coarse_sum + 0.5 - own_col
        fine_out = dot((acc_fine / fine_sum).astype(BF16), weight[:channels])
        coarse_out = dot((acc_coarse / coarse_sum).astype(BF16), weight[channels:])
        mixed[pl.ds(first, tile), 0:128] = fine_out + fine_row * ow[0:1] + fine_col * ow[1:2]
        mixed[pl.ds(first, tile), 128:256] = coarse_out + coarse_row * ow[2:3] + coarse_col * ow[3:4]
        mixed[pl.ds(first, tile), 256:384] = jnp.where(
            iota((tile, 128), 1) < 64,
            peak_fine + jnp.log(fine_sum),
            peak_coarse + jnp.log(coarse_sum),
        )
        return carry

    lax.fori_loop(0, pixels // tile, one_tile, 0)
    start = pl.multiple_of(half * columns, 128)
    other = pl.multiple_of((1 - half) * columns, 128)
    for r in range(rows_per):
        wide[r, HALO : HALO + width, :] = mixed[r * width : (r + 1) * width, :]
        keep_ref[r] = wide[r, pl.ds(start, half_wide), :]
        send_ref[r] = wide[r, pl.ds(other, half_wide), :]


def merge_kernel(own, keep_ref, got_ref, term_ref, hidden_ref, out_ref):
    dests = out_ref.shape[0]
    for r in range(keep_ref.shape[0]):
        keep, got = keep_ref[r], got_ref[r]
        gap = got[:, 256:384] - keep[:, 256:384]
        share = 1.0 / (1.0 + jnp.exp(gap))
        share_fine, share_coarse = share[:, 0:1], share[:, 64:65]
        base = (
            got[:, 0:128]
            + (keep[:, 0:128] - got[:, 0:128]) * share_fine
            + got[:, 128:256]
            + (keep[:, 128:256] - got[:, 128:256]) * share_coarse
            + term_ref[r]
        )
        hidden = hidden_ref[r].astype(F32)
        for j in range(dests):
            out_ref[j, r * WIN : (r + 1) * WIN, 0:128] = base[j * own : j * own + WIN].astype(BF16)
            out_ref[j, r * WIN : (r + 1) * WIN, 128:256] = hidden[j * own : j * own + WIN].astype(BF16)


def window_kernel(own, half_wide, where_ref, context_ref, out_ref, wide):
    rows_per, width, _ = context_ref.shape
    start = pl.multiple_of(where_ref[1] * (width // 2), 128)
    wide[...] = jnp.zeros_like(wide)
    for r in range(rows_per):
        wide[r, HALO : HALO + width, :] = context_ref[r].astype(F32)
        part = wide[r, pl.ds(start, half_wide), :]
        for j in range(out_ref.shape[0]):
            out_ref[j, r * WIN : (r + 1) * WIN, :] = part[j * own : j * own + WIN].astype(BF16)


def sigmoid(x):
    return 1.0 / (1.0 + jnp.exp(-x))


def update_kernel(
    own, width, where_ref, got_ref, context_ref, ow_ref, gate_ref, state_ref, bias_ref, head_ref, delta_ref,
    out_ref, base, hidden, inputs, states, resets, updates, col_in, col_st, flow, flow_cols,
):
    me, half = where_ref[0], where_ref[1]
    dests, per_dest, _ = got_ref.shape
    rows_per = per_dest // WIN
    count = dests * per_dest
    pad = 2 * WIN
    tiles = count // TILE
    first_col = (half * dests + me) * own - HALO
    column = first_col + iota((TILE, 128), 0) % WIN
    inside = (column >= 0) & (column < width)
    mask = jnp.where(inside, 1.0, 0.0)
    ow = ow_ref[...]
    add_row = OFFSET_SCALE * (ow[4:5] - ow[0:1] - ow[2:3])
    add_col = OFFSET_SCALE * (ow[5:6] - ow[1:2] - ow[3:4])
    bias = bias_ref[...]

    for ref in (inputs, states, resets):
        ref[0:pad, :] = jnp.zeros((pad, ref.shape[1]), BF16)
        ref[pad + count : pad + count + pad, :] = jnp.zeros((pad, ref.shape[1]), BF16)
    for j in range(dests):
        at = j * per_dest
        base[at : at + per_dest, :] = got_ref[j, :, 0:128]
        hidden[at : at + per_dest, :] = got_ref[j, :, 128:256].astype(F32)
        inputs[pad + at : pad + at + per_dest, 0:128] = context_ref[j]
    flow[...] = jnp.zeros_like(flow)
    flow_cols[...] = jnp.zeros_like(flow_cols)

    def each(body):
        def step(t, carry):
            body(pl.multiple_of(t * TILE, TILE))
            return carry

        lax.fori_loop(0, tiles, step, 0, unroll=tiles == 1)

    def shifted(value, tap):
        return value if tap == 2 else pltpu.roll(value, (2 - tap) % TILE, 0)

    def finish(at, update, candidate):
        old = hidden[pl.ds(at, TILE), :]
        hidden[pl.ds(at, TILE), :] = ((1.0 - update) * old + update * candidate) * mask

    for iteration in range(ITERS):

        def columns_pass(at):
            motion = base[pl.ds(at, TILE), :].astype(F32)
            if iteration > 0:
                moved = flow_cols[pl.ds(at, TILE), :]
                motion = (motion + moved[:, 0:1] * add_row + moved[:, 1:2] * add_col) * mask
            motion = jnp.maximum(motion, 0.0)
            inputs[pl.ds(pad + at, TILE), 128:256] = motion.astype(BF16)
            context = inputs[pl.ds(pad + at, TILE), 0:128].astype(F32)
            motion = motion.astype(BF16).astype(F32)
            state = hidden[pl.ds(at, TILE), :].astype(BF16).astype(F32)
            for tap in range(5):
                if iteration == 0:
                    col_in[pl.ds(at, TILE), tap * 256 : tap * 256 + 128] = shifted(context, tap).astype(BF16)
                col_in[pl.ds(at, TILE), tap * 256 + 128 : tap * 256 + 256] = shifted(motion, tap).astype(BF16)
                col_st[:, tap * 128 : (tap + 1) * 128] = shifted(state, tap).astype(BF16)
            gates = dot(col_st[...], gate_ref[0, :, 0:128, :].reshape(640, 256)) + dot(
                col_in[pl.ds(at, TILE), :], gate_ref[0, :, 128:384, :].reshape(1280, 256)
            )
            gates = sigmoid(gates + bias[0:1, 0:256])
            reset = (gates[:, 128:256] * state).astype(BF16).astype(F32)
            for tap in range(5):
                col_st[:, tap * 128 : (tap + 1) * 128] = shifted(reset, tap).astype(BF16)
            candidate = dot(col_st[...], state_ref[0, :, 0:128, :].reshape(640, 128)) + dot(
                col_in[pl.ds(at, TILE), :], state_ref[0, :, 128:384, :].reshape(1280, 128)
            )
            finish(at, gates[:, 0:128], jnp.tanh(candidate + bias[0:1, 256:384]))
            states[pl.ds(pad + at, TILE), :] = hidden[pl.ds(at, TILE), :].astype(BF16)

        def gate_rows(at):
            total = None
            for tap in range(5):
                part = dot(states[pl.ds(at + tap * WIN, TILE), :], gate_ref[1, tap, 0:128, :]) + dot(
                    inputs[pl.ds(at + tap * WIN, TILE), :], gate_ref[1, tap, 128:384, :]
                )
                total = part if total is None else total + part
            gates = sigmoid(total + bias[1:2, 0:256])
            updates[pl.ds(at, TILE), :] = gates[:, 0:128]
            resets[pl.ds(pad + at, TILE), :] = (
                gates[:, 128:256] * states[pl.ds(pad + at, TILE), :].astype(F32)
            ).astype(BF16)

        def state_rows(at):
            total = None
            for tap in range(5):
                part = dot(resets[pl.ds(at + tap * WIN, TILE), :], state_ref[1, tap, 0:128, :]) + dot(
                    inputs[pl.ds(at + tap * WIN, TILE), :], state_ref[1, tap, 128:384, :]
                )
                total = part if total is None else total + part
            finish(at, updates[pl.ds(at, TILE), :], jnp.tanh(total + bias[1:2, 256:384]))
            lifted = jnp.maximum(dot(hidden[pl.ds(at, TILE), :].astype(BF16), head_ref[...]), 0.0).astype(BF16)
            step = dot_nt(delta_ref[...], lifted)
            flow[:, pl.ds(at, TILE)] = flow[:, pl.ds(at, TILE)] + step
            flow_cols[pl.ds(at, TILE), :] = flow_cols[pl.ds(at, TILE), :] + step.T

        each(columns_pass)
        each(gate_rows)
        each(state_rows)

    for j in range(dests):
        for r in range(rows_per):
            at = j * per_dest + r * WIN + HALO
            out_ref[j, r * own : (r + 1) * own, :] = hidden[at : at + own, :]
        moved = flow[:, j * per_dest : (j + 1) * per_dest]
        out_ref[j, rows_per * own : rows_per * own + 8, :] = jnp.concatenate(
            [moved, jnp.zeros((8, 128 - per_dest), F32)], axis=1
        )


def local(
    frame_one,
    frame_two,
    context,
    carry_hidden,
    carry_flow,
    slot_target,
    slot_count,
    match_weight,
    offset_weight,
    gate_weight,
    state_weight,
    gru_bias,
    head_weight,
    delta_weight,
):
    half = lax.axis_index("loop")
    me = lax.axis_index("rows")
    dests = lax.axis_size("rows")
    halves = lax.axis_size("loop")
    rows_per, width, channels = frame_one.shape
    columns = frame_two.shape[1]
    pixels = rows_per * width
    slots, hidden_size = carry_hidden.shape
    cap = slots // dests
    own = columns // dests
    half_wide = round_up(columns - own + WIN, 8)
    padded = columns + half_wide
    here = jnp.stack([me, half]).astype(jnp.int32)

    shard = frame_two.reshape(1, rows_per, columns, channels)
    if dests == 8:

        def swap(value, flip):
            return lax.ppermute(value, "rows", [(i, i ^ flip) for i in range(dests)])

        beside, near, across, wrap = (swap(shard, flip) for flip in (1, 2, 4, 6))
        keys = (shard, beside, near, swap(near, 1), across, swap(across, 1), wrap, swap(wrap, 1))
    else:
        keys = (lax.all_gather(shard, "rows", axis=0, tiled=True),)

    rows_hidden = round_up(cap, 16)
    rows_slot = rows_hidden + round_up(8 * (-(-cap // 128)), 16)
    packed = call(
        functools.partial(pack_kernel, dests, cap, pixels),
        jax.ShapeDtypeStruct((dests, rows_slot, hidden_size), BF16),
        [smem_spec()] + vmem_specs(3),
        [],
        (2 * slots * slots * 128, 1 << 20, 0),
        slot_count,
        slot_target.reshape(1, slots),
        carry_flow.T.astype(F32),
        carry_hidden,
    )
    windows = call(
        functools.partial(window_kernel, own, half_wide),
        jax.ShapeDtypeStruct((dests, rows_per * WIN, hidden_size), BF16),
        [smem_spec()] + vmem_specs(1),
        [pltpu.VMEM((rows_per, padded, 128), F32)],
        (0, 1 << 18, 0),
        here,
        context,
    )
    early = lax.all_to_all(jnp.concatenate([packed, windows], axis=1), "rows", 0, 0, tiled=True)
    ow = jnp.pad(offset_weight, ((0, 2), (0, 0)))
    hidden_wide, flow_first, term = call(
        functools.partial(place_kernel, cap, half_wide, rows_per),
        (
            jax.ShapeDtypeStruct((rows_per, half_wide, 128), BF16),
            jax.ShapeDtypeStruct((8, pixels), F32),
            jax.ShapeDtypeStruct((rows_per, half_wide, 128), F32),
        ),
        [smem_spec()] + vmem_specs(2),
        [pltpu.VMEM((rows_per, padded, 128), F32)] * 2,
        (2 * slots * pixels * 128, 1 << 20, 0),
        here,
        early,
        ow,
    )
    chunks = dests // 2
    tile = 128
    keep, send = call(
        functools.partial(match_kernel, len(keys), len(keys) > 1, half_wide, rows_per),
        (jax.ShapeDtypeStruct((rows_per, half_wide, 384), F32),) * 2,
        [smem_spec()] + vmem_specs(3 + len(keys)),
        [
            pltpu.VMEM((chunks, 4 * columns, channels), BF16),
            pltpu.VMEM((chunks, columns, channels), BF16),
            pltpu.VMEM((chunks, tile, 4 * columns), F32),
            pltpu.VMEM((pixels, 384), F32),
            pltpu.VMEM((rows_per, padded, 384), F32),
        ],
        (4 * pixels * chunks * 4 * columns * channels, 1 << 21, pixels * chunks * 5 * columns),
        here,
        frame_one.reshape(pixels, channels),
        match_weight,
        ow,
        *keys,
    )
    other = lax.ppermute(send, "loop", [(i, (i + 1) % halves) for i in range(halves)])
    sending = call(
        functools.partial(merge_kernel, own),
        jax.ShapeDtypeStruct((dests, rows_per * WIN, 256), BF16),
        vmem_specs(4),
        [],
        (0, 1 << 20, 0),
        keep,
        other,
        term,
        hidden_wide,
    )
    arrived = lax.all_to_all(sending, "rows", 0, 0, tiled=True)
    count = dests * rows_per * WIN
    back_rows = rows_per * own + 8
    outgoing = call(
        functools.partial(update_kernel, own, width),
        jax.ShapeDtypeStruct((dests, back_rows, 128), F32),
        [smem_spec()] + vmem_specs(8),
        [
            pltpu.VMEM((count, 128), BF16),
            pltpu.VMEM((count, 128), F32),
            pltpu.VMEM((count + 4 * WIN, 256), BF16),
            pltpu.VMEM((count + 4 * WIN, 128), BF16),
            pltpu.VMEM((count + 4 * WIN, 128), BF16),
            pltpu.VMEM((count, 128), F32),
            pltpu.VMEM((count, 1280), BF16),
            pltpu.VMEM((TILE, 640), BF16),
            pltpu.VMEM((8, count), F32),
            pltpu.VMEM((count, 8), F32),
        ],
        (16 * count * 5 * 384 * 256, 1 << 22, 8 * count * 384),
        here,
        arrived,
        early[:, rows_slot:, :],
        ow,
        gate_weight,
        state_weight,
        gru_bias,
        head_weight,
        jnp.pad(delta_weight, ((0, 6), (0, 0))),
    )
    back = lax.all_to_all(outgoing, "rows", 0, 0, tiled=True)
    both = lax.all_gather(back, "loop", axis=0)
    cells = both[:, :, : rows_per * own, :].reshape(halves, dests, rows_per, own, hidden_size)
    hidden_out = cells.transpose(2, 0, 1, 3, 4).reshape(rows_per, width, hidden_size)
    moved = both[:, :, rows_per * own : rows_per * own + 2, : rows_per * WIN]
    moved = moved.reshape(halves, dests, 2, rows_per, WIN)[..., HALO : HALO + own]
    moved = moved.transpose(2, 3, 0, 1, 4).reshape(2, rows_per, width)
    flow_out = flow_first[:2].reshape(2, rows_per, width) + moved
    return (hidden_out, flow_out)


def solution(mesh):
    return jax.shard_map(
        local,
        mesh=mesh,
        in_specs=(
            P(("groups", "rows"), None, None),
            P(("groups", "rows"), "loop", None),
            P(("groups", "rows"), None, None),
            P(("groups", "rows"), None),
            P(("groups", "rows"), None),
            P(("groups", "rows")),
            P(("groups", "rows")),
            P(),
            P(),
            P(),
            P(),
            P(),
            P(),
            P(),
        ),
        out_specs=(P(("groups", "rows"), None, None), P(None, ("groups", "rows"), None)),
        check_vma=False,
    )
```

time: 245 us -> 110 us (0.45)
  blocking collectives: 49 us -> 2.03 us
  local copies, waits for them, and re-layouts: 46.1 us -> 8.72 us
  Pallas kernels: 0 us -> 32.3 us
  matrix products: 21.5 us -> 0 us
  starting transfers between devices: 43.5 us -> 25.5 us
  other arithmetic: 22 us -> 4.45 us
  between operations: 15.3 us -> 1.41 us
  waiting for transfers between devices: 46.7 us -> 34.6 us
    all_gather x9 -> x1, blocking collectives: 49 us -> 2.03 us  [local(): both = lax.all_gather(back, 'loop', axis=0)]
    pallas_call x0 -> x6, Pallas kernels: none -> 32.3 us  [call(): pl.pallas_call(kernel, out_shape=out_shape, in_specs=in_specs, out_specs=...]
    dot_general x46 -> x0, matrix products: 21.5 us -> none  [the longest x40 11.3 us: conv_along(): jnp.dot(window.reshape(-1, window.shape[-1]), weights[tap_index], preferr...]
    scatter x5 -> x0, local copies, waits for them, and re-layouts: 20.8 us -> none  [the longest x1 6.18 us: local(): jnp.full((rows_size * capacity,), pixels, jnp.int32).at[landing]]
    ppermute x8, waiting for transfers between devices: 39.8 us -> 20.2 us  [the longest x7 20.2 us: swap(): return lax.ppermute(value, 'rows', [(i, i ^ flip) for i in range(dests)])]
    ppermute x8, starting transfers between devices: 25.1 us -> 10.5 us  [the longest x7 10.5 us: swap(): return lax.ppermute(value, 'rows', [(i, i ^ flip) for i in range(dests)])]
    all_to_all x3, waiting for transfers between devices: 0.98 us -> 14.4 us  [the longest x1 7.43 us: local(): arrived = lax.all_to_all(sending, 'rows', 0, 0, tiled=True)]
    reduce_sum x4 -> x0, other arithmetic: 9.32 us -> none  [the longest x1 5.3 us: advance(): jnp.sum(fine_scores.reshape(pixels, group_size, rows_per, quarter, 2), ax...]
  transfers between devices with their start and end apart: 14 -> 11, of which waited for: 10 -> 6; matrix products, arithmetic and copies ran while one was open for 18% -> 3% of each run, Pallas kernels for 0% -> 10%
where the time goes in v1:
time: 110 us; the launch traced here: 109 us
  waiting for transfers between devices  34.6 us (31%)
  Pallas kernels  32.3 us (29%)
  starting transfers between devices  25.5 us (23%)
  local copies, waits for them, and re-layouts  8.72 us (8%)
  other arithmetic  4.45 us (4%)
  blocking collectives  2.03 us (2%)
  between operations  1.41 us (1%)
    pallas_call x6, Pallas kernels, call(): pl.pallas_call(kernel, out_shape=out_shape, in_specs=in_specs, out_specs=...  32.3 us
    ppermute x7, waiting for transfers between devices, swap(): return lax.ppermute(value, 'rows', [(i, i ^ flip) for i in range(dests)])  20.2 us
    ppermute x7, starting transfers between devices, swap(): return lax.ppermute(value, 'rows', [(i, i ^ flip) for i in range(dests)])  10.5 us
    all_to_all x1, waiting for transfers between devices, local(): arrived = lax.all_to_all(sending, 'rows', 0, 0, tiled=True)  7.43 us
    all_to_all x1, starting transfers between devices, local(): lax.all_to_all(jnp.concatenate([packed, windows], axis=1), 'rows', 0, 0,...  7.28 us
    all_to_all x1, waiting for transfers between devices, local(): back = lax.all_to_all(outgoing, 'rows', 0, 0, tiled=True)  6.94 us
    all_to_all x1, starting transfers between devices, local(): arrived = lax.all_to_all(sending, 'rows', 0, 0, tiled=True)  4.09 us
    all_to_all x1, starting transfers between devices, local(): back = lax.all_to_all(outgoing, 'rows', 0, 0, tiled=True)  3.59 us
  transfers between devices with their start and end apart: 11, of which 6 were waited for; matrix products, arithmetic and copies ran while one was open for 3% of the time, Pallas kernels for 10%

profile of v1, /device:TPU:0, one launch (start us, length us, event | category | flops | bytes accessed | tf_op | source)
XLA Modules:
  0.0 109.0 jit_solution(3888332411615495771)
XLA Ops:
  0.6 1.3 %convert_bitcast_fusion.flow_ref = f32[2,1536]{1,0:T(2,128)} fusion(bf16[1536,2]{0,1:T(2,128)(2,1)} %param.18), kind=kLoop, calls=%fused_computation.2 | loop fusion | flops 3072 | bytes 18432 | tf_op jit(solution)/shard_map/convert_element_type | solution.py:472
  1.9 1.3 %reshape.30.target_ref = s32[1,1536]{1,0:T(1,128)} reshape(s32[1536]{0:T(1024)} %param.19) | data formatting | bytes 12288 | tf_op jit(solution)/shard_map/reshape | solution.py:471
  3.9 0.7 pad_add_fusion.where_ref
  4.5 1.6 %shard_map.151 = bf16[8,64,128]{2,1,0:T(8,128)(2,1)} custom-call(s32[2]{0:T(128)} %pad_add_fusion.where_ref, bf16[2,256,128]{2,1,0:T(8,128)(2,1)} %context_ref.1), custom_call_target="tpu_custom_call" | custom-call | bytes 262144 | tf_op jit(solution)/shard_map/pallas_call | solution.py:52
  6.1 0.0 copy-start.1
  6.1 5.1 %shard_map.150 = bf16[8,208,128]{2,1,0:T(8,128)(2,1)} custom-call(s32[1]{0:T(128)S(6)} %copy.23.count_ref, s32[1,1536]{1,0:T(1,128)} %reshape.30.target_ref, f32[2,1536]{1,0:T(2,128)} %convert_bitcast_fusion.flow_ref, bf16[1536,128]{1,0:T(8,128)(2,1)} %hidden_ref.1), custom_call_target="tpu_custom_call" | custom-call | flops 603979776 | bytes 1048576 | tf_op jit(solution)/shard_map/pallas_call | solution.py:52
  11.3 0.0 copy-done.1
  11.3 0.0 copy-start.6
  11.3 0.0 copy-start.4
  11.3 1.9 %pad_maximum_fusion = bf16[8,272,128]{2,1,0:T(8,128)(2,1)} fusion(bf16[8,64,128]{2,1,0:T(8,128)(2,1)S(1)} %copy-done.1, bf16[8,208,128]{2,1,0:T(8,128)(2,1)} %shard_map.150), kind=kLoop, calls=%fused_computation | loop fusion | flops 1114112 | bytes 1114112 | tf_op jit(solution)/shard_map/concatenate | solution.py:484
  13.2 7.3 %all-to-all-start = ((bf16[8,272,128]{2,1,0:T(8,128)(2,1)}), bf16[8,272,128]{2,1,0:T(8,128)(2,1)S(1)}, u32[]{:S(2)}, u32[]{:S(2)}) async-start(bf16[8,272,128]{2,1,0:T(8,128)(2,1)} %pad_maximum_fusion), calls=%async_computation | async-start | bytes 1114112 | tf_op jit(solution)/shard_map/all_to_all | solution.py:484
  20.5 0.0 copy-done.6
  20.5 2.0 %collective-permute-start.1 = (bf16[1,2,128,256]{3,2,1,0:T(8,128)(2,1)S(1)}, bf16[1,2,128,256]{3,2,1,0:T(8,128)(2,1)S(1)}, u32[]{:S(2)}, u32[]{:S(2)}) collective-permute-start(bf16[1,2,128,256]{3,2,1,0:T(8,128)(2,1)S(1)} %bitcast.23), channel_id=1, source_target_pairs={{0,4},{2,6},{4,0},{6,2},{8,12},{10,14},{12,8},{14,10},{1,5},{3,7},... | collective-permute-start | bytes 393224 | tf_op jit(solution)/shard_map/ppermute | solution.py:455
  22.5 2.4 %collective-permute-start.3 = (bf16[1,2,128,256]{3,2,1,0:T(8,128)(2,1)S(1)}, bf16[1,2,128,256]{3,2,1,0:T(8,128)(2,1)S(1)}, u32[]{:S(2)}, u32[]{:S(2)}) collective-permute-start(bf16[1,2,128,256]{3,2,1,0:T(8,128)(2,1)S(1)} %bitcast.24), channel_id=1, source_target_pairs={{0,8},{2,10},{4,12},{6,14},{8,0},{10,2},{12,4},{14,6},{1,9},{3,11}... | collective-permute-start | bytes 393224 | tf_op jit(solution)/shard_map/ppermute | solution.py:455
  24.9 0.1 collective-permute-start.5
  24.9 2.0 %collective-permute-start = (bf16[1,2,128,256]{3,2,1,0:T(8,128)(2,1)S(1)}, bf16[1,2,128,256]{3,2,1,0:T(8,128)(2,1)S(1)}, u32[]{:S(2)}, u32[]{:S(2)}) collective-permute-start(bf16[1,2,128,256]{3,2,1,0:T(8,128)(2,1)S(1)} %bitcast.26), channel_id=1, source_target_pairs={{0,2},{2,0},{4,6},{6,4},{8,10},{10,8},{12,14},{14,12},{1,3},{3,1},... | collective-permute-start | bytes 393224 | tf_op jit(solution)/shard_map/ppermute | solution.py:455
  26.9 6.6 %collective-permute-done.1.refs_2_ = bf16[1,2,128,256]{3,2,1,0:T(8,128)(2,1)S(1)} collective-permute-done((bf16[1,2,128,256]{3,2,1,0:T(8,128)(2,1)S(1)}, bf16[1,2,128,256]{3,2,1,0:T(8,128)(2,1)S(1)}, u32[]{:S(2)}, u32[]{:S(2)}) %collective-permute-start.1) | collective-permute-done | bytes 131104 | tf_op jit(solution)/shard_map/ppermute | solution.py:455
  33.5 0.0 copy-start.7
  33.5 2.1 %collective-permute-start.2 = (bf16[1,2,128,256]{3,2,1,0:T(8,128)(2,1)S(1)}, bf16[1,2,128,256]{3,2,1,0:T(8,128)(2,1)S(1)}, u32[]{:S(2)}, u32[]{:S(2)}) collective-permute-start(bf16[1,2,128,256]{3,2,1,0:T(8,128)(2,1)S(1)} %collective-permute-done.1.refs_2_), channel_id=1, source_target_pairs={{0,2},{2,0},{4,6},{6,4},{8,10},{10,8},{12,14},{14,12},{1,3},{3,1},... | collective-permute-start | bytes 393224 | tf_op jit(solution)/shard_map/ppermute | solution.py:455
  35.6 9.8 %collective-permute-done.3.refs_4_ = bf16[1,2,128,256]{3,2,1,0:T(8,128)(2,1)S(1)} collective-permute-done((bf16[1,2,128,256]{3,2,1,0:T(8,128)(2,1)S(1)}, bf16[1,2,128,256]{3,2,1,0:T(8,128)(2,1)S(1)}, u32[]{:S(2)}, u32[]{:S(2)}) %collective-permute-start.3) | collective-permute-done | bytes 131104 | tf_op jit(solution)/shard_map/ppermute | solution.py:455
  45.5 0.0 copy-start.8
  45.5 1.1 %collective-permute-start.4 = (bf16[1,2,128,256]{3,2,1,0:T(8,128)(2,1)S(1)}, bf16[1,2,128,256]{3,2,1,0:T(8,128)(2,1)S(1)}, u32[]{:S(2)}, u32[]{:S(2)}) collective-permute-start(bf16[1,2,128,256]{3,2,1,0:T(8,128)(2,1)S(1)} %collective-permute-done.3.refs_4_), channel_id=1, source_target_pairs={{0,2},{2,0},{4,6},{6,4},{8,10},{10,8},{12,14},{14,12},{1,3},{3,1},... | collective-permute-start | bytes 393224 | tf_op jit(solution)/shard_map/ppermute | solution.py:455
  46.6 0.0 collective-permute-done.5.refs_6_
  46.6 0.0 copy-start.9
  46.6 0.9 collective-permute-start.6
  47.5 0.0 copy-done.4
  47.5 0.6 pad.8.ow_ref
  48.1 0.0 collective-permute-done.refs_1_
  48.1 0.0 collective-permute-done.2.refs_3_
  48.1 0.0 copy-start.11
  48.1 2.3 %collective-permute-done.4.refs_5_ = bf16[1,2,128,256]{3,2,1,0:T(8,128)(2,1)S(1)} collective-permute-done((bf16[1,2,128,256]{3,2,1,0:T(8,128)(2,1)S(1)}, bf16[1,2,128,256]{3,2,1,0:T(8,128)(2,1)S(1)}, u32[]{:S(2)}, u32[]{:S(2)}) %collective-permute-start.4) | collective-permute-done | bytes 131104 | tf_op jit(solution)/shard_map/ppermute | solution.py:455
  50.5 1.4 %collective-permute-done.6.refs_7_ = bf16[1,2,128,256]{3,2,1,0:T(8,128)(2,1)S(1)} collective-permute-done((bf16[1,2,128,256]{3,2,1,0:T(8,128)(2,1)S(1)}, bf16[1,2,128,256]{3,2,1,0:T(8,128)(2,1)S(1)}, u32[]{:S(2)}, u32[]{:S(2)}) %collective-permute-start.6) | collective-permute-done | bytes 131104 | tf_op jit(solution)/shard_map/ppermute | solution.py:455
  51.9 0.0 copy-done.7
  51.9 0.0 copy-done.8
  51.9 0.0 copy-done.9
  51.9 0.0 copy-done.10
  51.9 0.0 copy-done.11
  51.9 0.0 copy-done.12
  51.9 0.6 copy-done.13
  52.5 7.9 %shard_map.149 = (f32[2,144,384]{2,1,0:T(8,128)}, f32[2,144,384]{2,1,0:T(8,128)}) custom-call(s32[2]{0:T(128)} %pad_add_fusion.where_ref, bf16[512,256]{1,0:T(8,128)(2,1)} %bitcast.21, bf16[512,128]{1,0:T(8,128)(2,1)} %weight_ref.1, f32[8,128]{1,0:T(8,128)} %pad.8.ow_ref, bf16[1,2,128,256]{3,2,1,0:T(8,128)(2,1)} %bitcast.22, ...), custom_call_target="tpu_custom_call" | custom-call | flops 1073741824 | bytes 2097152 | tf_op jit(solution)/shard_map/pallas_call | solution.py:52
  60.4 0.0 collective-permute-start.7
  60.4 0.0 all-to-all-done.got_ref
  60.4 0.0 copy-start
  60.4 0.8 copy-done
  61.2 3.4 %shard_map.152 = (bf16[2,144,128]{2,1,0:T(8,128)(2,1)}, f32[8,512]{1,0:T(8,128)}, f32[2,144,128]{2,1,0:T(8,128)}) custom-call(s32[2]{0:T(128)} %pad_add_fusion.where_ref, bf16[8,272,128]{2,1,0:T(8,128)(2,1)} %copy-done, f32[8,128]{1,0:T(8,128)} %pad.8.ow_ref), custom_call_target="tpu_custom_call" | custom-call | flops 201326592 | bytes 1048576 | tf_op jit(solution)/shard_map/pallas_call | solution.py:52
  64.6 0.0 collective-permute-done.7.got_ref
  64.6 0.8 copy-done.2
  65.4 2.1 %shard_map.153 = bf16[8,64,256]{2,1,0:T(8,128)(2,1)} custom-call(f32[2,144,384]{2,1,0:T(8,128)} %get-tuple-element.7.keep_ref, f32[2,144,384]{2,1,0:T(8,128)} %copy-done.2, f32[2,144,128]{2,1,0:T(8,128)} %get-tuple-element.9.term_ref, bf16[2,144,128]{2,1,0:T(8,128)(2,1)} %get-tuple-element.10.hidden_ref), custom_call_target="tpu_custom_call" | custom-call | bytes 1048576 | tf_op jit(solution)/shard_map/pallas_call | solution.py:52
  67.4 4.1 %all-to-all-start.1 = ((bf16[8,64,256]{2,1,0:T(8,128)(2,1)}), bf16[8,64,256]{2,1,0:T(8,128)(2,1)S(1)}, u32[]{:S(2)}, u32[]{:S(2)}) async-start(bf16[8,64,256]{2,1,0:T(8,128)(2,1)} %shard_map.153), calls=%async_computation.1 | async-start | bytes 524288 | tf_op jit(solution)/shard_map/all_to_all | solution.py:532
  71.5 0.0 copy-done.5
  71.5 0.6 pad.9.delta_ref
  72.1 1.6 %slice.20.context_ref = bf16[8,64,128]{2,1,0:T(8,128)(2,1)} slice(bf16[8,272,128]{2,1,0:T(8,128)(2,1)} %copy-done), slice={[0:8], [208:272], [0:128]} | slice | bytes 262144 | tf_op jit(solution)/shard_map/slice | solution.py:554
  73.7 7.4 %all-to-all-done.1.got_ref = bf16[8,64,256]{2,1,0:T(8,128)(2,1)S(1)} async-done(((bf16[8,64,256]{2,1,0:T(8,128)(2,1)}), bf16[8,64,256]{2,1,0:T(8,128)(2,1)S(1)}, u32[]{:S(2)}, u32[]{:S(2)}) %all-to-all-start.1) | async-done | bytes 262176 | tf_op jit(solution)/shard_map/all_to_all | solution.py:532
  81.1 0.7 copy-done.3
  81.8 12.2 %shard_map.154 = f32[8,40,128]{2,1,0:T(8,128)} custom-call(s32[2]{0:T(128)} %pad_add_fusion.where_ref, bf16[8,64,256]{2,1,0:T(8,128)(2,1)} %copy-done.3, bf16[8,64,128]{2,1,0:T(8,128)(2,1)} %slice.20.context_ref, f32[8,128]{1,0:T(8,128)} %pad.8.ow_ref, bf16[2,5,384,256]{3,2,1,0:T(8,128)(2,1)} %gate_ref.1, bf16[2,5,384,128]{3,2,1,0:T(8,128)(2,1)} %state_ref.1, ...), custom_call_target="tpu_custom_call" | custom-call | flops 4026531840 | bytes 4194304 | tf_op jit(solution)/shard_map/pallas_call | solution.py:52
  94.1 3.6 %all-to-all-start.2 = ((f32[8,40,128]{2,1,0:T(8,128)}), f32[8,40,128]{2,1,0:T(8,128)S(1)}, u32[]{:S(2)}, u32[]{:S(2)}) async-start(f32[8,40,128]{2,1,0:T(8,128)} %shard_map.154), calls=%async_computation.2 | async-start | bytes 327680 | tf_op jit(solution)/shard_map/all_to_all | solution.py:562
  97.7 0.7 slice.17
  98.4 6.9 %all-to-all-done.2 = f32[8,40,128]{2,1,0:T(8,128)S(1)} async-done(((f32[8,40,128]{2,1,0:T(8,128)}), f32[8,40,128]{2,1,0:T(8,128)S(1)}, u32[]{:S(2)}, u32[]{:S(2)}) %all-to-all-start.2) | async-done | bytes 163872 | tf_op jit(solution)/shard_map/all_to_all | solution.py:562
  105.3 2.0 %all-gather = f32[16,40,128]{2,1,0:T(8,128)S(1)} all-gather(f32[8,40,128]{2,1,0:T(8,128)S(1)} %all-to-all-done.2), channel_id=2, replica_groups=mesh['groups'=2,'rows'=8,'loop'=2] {'loop'}, dimensions={0}, use_global_device_ids=true | all-gather | bytes 491520 | tf_op jit(solution)/shard_map/all_gather | solution.py:563
  107.4 0.1 reshape.34
  107.5 0.1 slice.23
  107.6 0.1 reshape.35
  107.7 0.7 copy.18
  108.4 0.6 add.7
  (10 shorter events, 0.1 us)
Async XLA Ops:
  6.1 5.1 %copy-start.1 = (bf16[8,64,128]{2,1,0:T(8,128)(2,1)S(1)}, bf16[8,64,128]{2,1,0:T(8,128)(2,1)}, u32[]{:S(2)}) copy-start(bf16[8,64,128]{2,1,0:T(8,128)(2,1)} %shard_map.151) | copy-start | bytes 393220
  11.3 9.2 %copy-start.6 = (bf16[2,128,256]{2,1,0:T(8,128)(2,1)S(1)}, bf16[2,128,256]{2,1,0:T(8,128)(2,1)}, u32[]{:S(2)}) copy-start(bf16[2,128,256]{2,1,0:T(8,128)(2,1)} %param.15) | copy-start | bytes 393220
  11.3 36.3 %copy-start.4 = (f32[6,128]{1,0:T(8,128)S(1)}, f32[6,128]{1,0:T(8,128)}, u32[]{:S(2)}) copy-start(f32[6,128]{1,0:T(8,128)} %param.22) | copy-start | bytes 9220
  13.2 47.2 %all-to-all-start = ((bf16[8,272,128]{2,1,0:T(8,128)(2,1)}), bf16[8,272,128]{2,1,0:T(8,128)(2,1)S(1)}, u32[]{:S(2)}, u32[]{:S(2)}) async-start(bf16[8,272,128]{2,1,0:T(8,128)(2,1)} %pad_maximum_fusion), calls=%async_computation | async-start | bytes 1114112 | tf_op jit(solution)/shard_map/all_to_all | solution.py:484
  20.5 13.1 %collective-permute-start.1 = (bf16[1,2,128,256]{3,2,1,0:T(8,128)(2,1)S(1)}, bf16[1,2,128,256]{3,2,1,0:T(8,128)(2,1)S(1)}, u32[]{:S(2)}, u32[]{:S(2)}) collective-permute-start(bf16[1,2,128,256]{3,2,1,0:T(8,128)(2,1)S(1)} %bitcast.23), channel_id=1, source_target_pairs={{0,4},{2,6},{4,0},{6,2},{8,12},{10,14},{12,8},{14,10},{1,5},{3,7},... | collective-permute-start | bytes 393224 | tf_op jit(solution)/shard_map/ppermute | solution.py:455
  22.5 23.0 %collective-permute-start.3 = (bf16[1,2,128,256]{3,2,1,0:T(8,128)(2,1)S(1)}, bf16[1,2,128,256]{3,2,1,0:T(8,128)(2,1)S(1)}, u32[]{:S(2)}, u32[]{:S(2)}) collective-permute-start(bf16[1,2,128,256]{3,2,1,0:T(8,128)(2,1)S(1)} %bitcast.24), channel_id=1, source_target_pairs={{0,8},{2,10},{4,12},{6,14},{8,0},{10,2},{12,4},{14,6},{1,9},{3,11}... | collective-permute-start | bytes 393224 | tf_op jit(solution)/shard_map/ppermute | solution.py:455
  24.9 21.8 %collective-permute-start.5 = (bf16[1,2,128,256]{3,2,1,0:T(8,128)(2,1)S(1)}, bf16[1,2,128,256]{3,2,1,0:T(8,128)(2,1)S(1)}, u32[]{:S(2)}, u32[]{:S(2)}) collective-permute-start(bf16[1,2,128,256]{3,2,1,0:T(8,128)(2,1)S(1)} %bitcast.25), channel_id=1, source_target_pairs={{0,12},{2,14},{4,8},{6,10},{8,4},{10,6},{12,0},{14,2},{1,13},{3,15... | collective-permute-start | bytes 393224 | tf_op jit(solution)/shard_map/ppermute | solution.py:455
  24.9 23.2 %collective-permute-start = (bf16[1,2,128,256]{3,2,1,0:T(8,128)(2,1)S(1)}, bf16[1,2,128,256]{3,2,1,0:T(8,128)(2,1)S(1)}, u32[]{:S(2)}, u32[]{:S(2)}) collective-permute-start(bf16[1,2,128,256]{3,2,1,0:T(8,128)(2,1)S(1)} %bitcast.26), channel_id=1, source_target_pairs={{0,2},{2,0},{4,6},{6,4},{8,10},{10,8},{12,14},{14,12},{1,3},{3,1},... | collective-permute-start | bytes 393224 | tf_op jit(solution)/shard_map/ppermute | solution.py:455
  33.5 18.3 %copy-start.7 = (bf16[1,2,128,256]{3,2,1,0:T(8,128)(2,1)}, bf16[1,2,128,256]{3,2,1,0:T(8,128)(2,1)S(1)}, u32[]{:S(2)}) copy-start(bf16[1,2,128,256]{3,2,1,0:T(8,128)(2,1)S(1)} %collective-permute-done.1.refs_2_) | copy-start | bytes 393220
  33.5 14.6 %collective-permute-start.2 = (bf16[1,2,128,256]{3,2,1,0:T(8,128)(2,1)S(1)}, bf16[1,2,128,256]{3,2,1,0:T(8,128)(2,1)S(1)}, u32[]{:S(2)}, u32[]{:S(2)}) collective-permute-start(bf16[1,2,128,256]{3,2,1,0:T(8,128)(2,1)S(1)} %collective-permute-done.1.refs_2_), channel_id=1, source_target_pairs={{0,2},{2,0},{4,6},{6,4},{8,10},{10,8},{12,14},{14,12},{1,3},{3,1},... | collective-permute-start | bytes 393224 | tf_op jit(solution)/shard_map/ppermute | solution.py:455
  45.5 6.4 %copy-start.8 = (bf16[1,2,128,256]{3,2,1,0:T(8,128)(2,1)}, bf16[1,2,128,256]{3,2,1,0:T(8,128)(2,1)S(1)}, u32[]{:S(2)}) copy-start(bf16[1,2,128,256]{3,2,1,0:T(8,128)(2,1)S(1)} %collective-permute-done.3.refs_4_) | copy-start | bytes 393220
  45.5 5.0 %collective-permute-start.4 = (bf16[1,2,128,256]{3,2,1,0:T(8,128)(2,1)S(1)}, bf16[1,2,128,256]{3,2,1,0:T(8,128)(2,1)S(1)}, u32[]{:S(2)}, u32[]{:S(2)}) collective-permute-start(bf16[1,2,128,256]{3,2,1,0:T(8,128)(2,1)S(1)} %collective-permute-done.3.refs_4_), channel_id=1, source_target_pairs={{0,2},{2,0},{4,6},{6,4},{8,10},{10,8},{12,14},{14,12},{1,3},{3,1},... | collective-permute-start | bytes 393224 | tf_op jit(solution)/shard_map/ppermute | solution.py:455
  46.6 5.3 %copy-start.9 = (bf16[1,2,128,256]{3,2,1,0:T(8,128)(2,1)}, bf16[1,2,128,256]{3,2,1,0:T(8,128)(2,1)S(1)}, u32[]{:S(2)}) copy-start(bf16[1,2,128,256]{3,2,1,0:T(8,128)(2,1)S(1)} %collective-permute-done.5.refs_6_) | copy-start | bytes 393220
  46.6 5.3 %collective-permute-start.6 = (bf16[1,2,128,256]{3,2,1,0:T(8,128)(2,1)S(1)}, bf16[1,2,128,256]{3,2,1,0:T(8,128)(2,1)S(1)}, u32[]{:S(2)}, u32[]{:S(2)}) collective-permute-start(bf16[1,2,128,256]{3,2,1,0:T(8,128)(2,1)S(1)} %collective-permute-done.5.refs_6_), channel_id=1, source_target_pairs={{0,2},{2,0},{4,6},{6,4},{8,10},{10,8},{12,14},{14,12},{1,3},{3,1},... | collective-permute-start | bytes 393224 | tf_op jit(solution)/shard_map/ppermute | solution.py:455
  48.1 3.8 %copy-start.10 = (bf16[1,2,128,256]{3,2,1,0:T(8,128)(2,1)}, bf16[1,2,128,256]{3,2,1,0:T(8,128)(2,1)S(1)}, u32[]{:S(2)}) copy-start(bf16[1,2,128,256]{3,2,1,0:T(8,128)(2,1)S(1)} %collective-permute-done.refs_1_) | copy-start | bytes 393220
  48.1 3.8 %copy-start.11 = (bf16[1,2,128,256]{3,2,1,0:T(8,128)(2,1)}, bf16[1,2,128,256]{3,2,1,0:T(8,128)(2,1)S(1)}, u32[]{:S(2)}) copy-start(bf16[1,2,128,256]{3,2,1,0:T(8,128)(2,1)S(1)} %collective-permute-done.2.refs_3_) | copy-start | bytes 393220
  50.5 1.4 %copy-start.12 = (bf16[1,2,128,256]{3,2,1,0:T(8,128)(2,1)}, bf16[1,2,128,256]{3,2,1,0:T(8,128)(2,1)S(1)}, u32[]{:S(2)}) copy-start(bf16[1,2,128,256]{3,2,1,0:T(8,128)(2,1)S(1)} %collective-permute-done.4.refs_5_) | copy-start | bytes 393220
  51.9 0.6 copy-start.13
  60.4 4.2 %collective-permute-start.7 = (f32[2,144,384]{2,1,0:T(8,128)}, f32[2,144,384]{2,1,0:T(8,128)S(1)}, u32[]{:S(2)}, u32[]{:S(2)}) collective-permute-start(f32[2,144,384]{2,1,0:T(8,128)} %get-tuple-element.8), channel_id=1, source_target_pairs={{0,1},{1,0},{2,3},{3,2},{4,5},{5,4},{6,7},{7,6},{8,9},{9,8},{10,11... | collective-permute-start | bytes 1327112 | tf_op jit(solution)/shard_map/ppermute | solution.py:520
  60.4 0.8 copy-start
  64.6 6.9 %copy-start.5 = (bf16[2,256]{1,0:T(2,128)(2,1)S(1)}, bf16[2,256]{1,0:T(2,128)(2,1)}, u32[]{:S(2)}) copy-start(bf16[2,256]{1,0:T(2,128)(2,1)} %param.27) | copy-start | bytes 3076
  64.6 0.8 copy-start.2
  67.4 13.7 %all-to-all-start.1 = ((bf16[8,64,256]{2,1,0:T(8,128)(2,1)}), bf16[8,64,256]{2,1,0:T(8,128)(2,1)S(1)}, u32[]{:S(2)}, u32[]{:S(2)}) async-start(bf16[8,64,256]{2,1,0:T(8,128)(2,1)} %shard_map.153), calls=%async_computation.1 | async-start | bytes 524288 | tf_op jit(solution)/shard_map/all_to_all | solution.py:532
  81.1 0.7 copy-start.3
  94.1 11.3 %all-to-all-start.2 = ((f32[8,40,128]{2,1,0:T(8,128)}), f32[8,40,128]{2,1,0:T(8,128)S(1)}, u32[]{:S(2)}, u32[]{:S(2)}) async-start(f32[8,40,128]{2,1,0:T(8,128)} %shard_map.154), calls=%async_computation.2 | async-start | bytes 327680 | tf_op jit(solution)/shard_map/all_to_all | solution.py:562

commit v2 on v1

--- a/solution.py
+++ b/solution.py
@@ -47,7 +47,7 @@
     return lax.fori_loop(0, count, body, carry, unroll=count <= 4)
 
 
-def call(kernel, out_shape, in_specs, scratch, cost, *args):
+def call(kernel, out_shape, in_specs, scratch, cost, room, *args):
     single = not isinstance(out_shape, (tuple, list))
     return pl.pallas_call(
         kernel,
@@ -55,14 +55,14 @@
         in_specs=in_specs,
         out_specs=vmem_specs(1)[0] if single else vmem_specs(len(out_shape)),
         scratch_shapes=scratch,
-        compiler_params=pltpu.CompilerParams(vmem_limit_bytes=56 * 1024 * 1024),
+        compiler_params=pltpu.CompilerParams(vmem_limit_bytes=room * 1024 * 1024),
         cost_estimate=pl.CostEstimate(flops=cost[0], bytes_accessed=cost[1], transcendentals=cost[2]),
     )(*args)
 
 
-def pack_kernel(dests, cap, pixels, count_ref, target_ref, flow_ref, hidden_ref, out_ref):
-    slots = target_ref.shape[1]
-    target = target_ref[...]
+def pack_kernel(dests, cap, pixels, own, half_wide, count_ref, target_ref, flow_ref, hidden_ref, context_ref, out_ref, wide):
+    slots = hidden_ref.shape[0]
+    target = jnp.concatenate([target_ref[k : k + 1, :] for k in range(slots // 128)], axis=1)
     counted = iota((1, slots), 1) < count_ref[0]
     owner = target // pixels
     within = target % pixels
@@ -81,7 +81,7 @@
     )
     landing = jnp.where(counted, place_at, -1.0).astype(jnp.int32)
     row = iota((8, slots), 0)
-    flow = flow_ref[...]
+    flow = flow_ref[...].astype(F32)
     side = jnp.where(row == 0, flow[0:1], 0.0)
     side = jnp.where(row == 1, flow[1:2], side)
     side = jnp.where(row == 2, (within // 256).astype(F32), side)
@@ -104,10 +104,19 @@
                     piece = jnp.concatenate([piece, jnp.zeros((8, 128 - width), F32)], axis=1)
                 base = rows_hidden + 8 * t
                 out_ref[first + k, base : base + 8, :] = piece.astype(BF16)
-
-
-def place_kernel(cap, half_wide, rows_per, where_ref, got_ref, ow_ref, hidden_ref, flow_ref, term_ref, wide_hidden, wide_term):
-    half = where_ref[1]
+    rows_per, width, _ = context_ref.shape
+    top = out_ref.shape[1] - rows_per * WIN
+    start = pl.multiple_of(lax.axis_index("loop") * (width // 2), 128)
+    wide[...] = jnp.zeros_like(wide)
+    for r in range(rows_per):
+        wide[r, HALO : HALO + width, :] = context_ref[r].astype(F32)
+        part = wide[r, pl.ds(start, half_wide), :]
+        for j in range(dests):
+            out_ref[j, top + r * WIN : top + (r + 1) * WIN, :] = part[j * own : j * own + WIN].astype(BF16)
+
+
+def place_kernel(cap, half_wide, rows_per, got_ref, ow_ref, hidden_ref, flow_ref, term_ref, wide_hidden, wide_term):
+    half = lax.axis_index("loop")
     dests = got_ref.shape[0]
     pixels = flow_ref.shape[1]
     width = pixels // rows_per
@@ -139,10 +148,10 @@
 
 
 def match_kernel(
-    count, flip, half_wide, rows_per, where_ref, queries_ref, weight_ref, ow_ref, *refs
+    count, flip, half_wide, rows_per, queries_ref, weight_ref, ow_ref, *refs
 ):
     key_refs, (keep_ref, send_ref, fine, coarse, scores, mixed, wide) = refs[:count], refs[count:]
-    me, half = where_ref[0], where_ref[1]
+    me, half = lax.axis_index("rows"), lax.axis_index("loop")
     pixels, channels = queries_ref.shape
     width = pixels // rows_per
     columns = width // 2
@@ -289,26 +298,15 @@
             out_ref[j, r * WIN : (r + 1) * WIN, 128:256] = hidden[j * own : j * own + WIN].astype(BF16)
 
 
-def window_kernel(own, half_wide, where_ref, context_ref, out_ref, wide):
-    rows_per, width, _ = context_ref.shape
-    start = pl.multiple_of(where_ref[1] * (width // 2), 128)
-    wide[...] = jnp.zeros_like(wide)
-    for r in range(rows_per):
-        wide[r, HALO : HALO + width, :] = context_ref[r].astype(F32)
-        part = wide[r, pl.ds(start, half_wide), :]
-        for j in range(out_ref.shape[0]):
-            out_ref[j, r * WIN : (r + 1) * WIN, :] = part[j * own : j * own + WIN].astype(BF16)
-
-
 def sigmoid(x):
     return 1.0 / (1.0 + jnp.exp(-x))
 
 
 def update_kernel(
-    own, width, where_ref, got_ref, context_ref, ow_ref, gate_ref, state_ref, bias_ref, head_ref, delta_ref,
+    own, width, got_ref, context_ref, ow_ref, gate_ref, state_ref, bias_ref, head_ref, delta_ref,
     out_ref, base, hidden, inputs, states, resets, updates, col_in, col_st, flow, flow_cols,
 ):
-    me, half = where_ref[0], where_ref[1]
+    me, half = lax.axis_index("rows"), lax.axis_index("loop")
     dests, per_dest, _ = got_ref.shape
     rows_per = per_dest // WIN
     count = dests * per_dest
@@ -434,8 +432,6 @@
     head_weight,
     delta_weight,
 ):
-    half = lax.axis_index("loop")
-    me = lax.axis_index("rows")
     dests = lax.axis_size("rows")
     halves = lax.axis_size("loop")
     rows_per, width, channels = frame_one.shape
@@ -446,7 +442,7 @@
     own = columns // dests
     half_wide = round_up(columns - own + WIN, 8)
     padded = columns + half_wide
-    here = jnp.stack([me, half]).astype(jnp.int32)
+    room = 16 if dests <= 8 else 56
 
     shard = frame_two.reshape(1, rows_per, columns, channels)
     if dests == 8:
@@ -454,34 +450,33 @@
         def swap(value, flip):
             return lax.ppermute(value, "rows", [(i, i ^ flip) for i in range(dests)])
 
-        beside, near, across, wrap = (swap(shard, flip) for flip in (1, 2, 4, 6))
+        beside, *others = (swap(shard, flip) for flip in (1, 2, 4, 6))
+    else:
+        beside, others = lax.all_gather(shard, "rows", axis=0, tiled=True), ()
+
+    rows_hidden = round_up(cap, 16)
+    rows_slot = rows_hidden + round_up(8 * (-(-cap // 128)), 16)
+    slot_target, beside = lax.optimization_barrier((slot_target, beside))
+    packed = call(
+        functools.partial(pack_kernel, dests, cap, pixels, own, half_wide),
+        jax.ShapeDtypeStruct((dests, rows_slot + rows_per * WIN, hidden_size), BF16),
+        [smem_spec()] + vmem_specs(4),
+        [pltpu.VMEM((rows_per, padded, 128), F32)],
+        (2 * slots * slots * 128, 1 << 20, 0),
+        room,
+        slot_count,
+        slot_target.reshape(slots // 128, 128),
+        carry_flow.T,
+        carry_hidden,
+        context,
+    )
+    packed, others = lax.optimization_barrier((packed, others))
+    early = lax.all_to_all(packed, "rows", 0, 0, tiled=True)
+    if others:
+        near, across, wrap = others
         keys = (shard, beside, near, swap(near, 1), across, swap(across, 1), wrap, swap(wrap, 1))
     else:
-        keys = (lax.all_gather(shard, "rows", axis=0, tiled=True),)
-
-    rows_hidden = round_up(cap, 16)
-    rows_slot = rows_hidden + round_up(8 * (-(-cap // 128)), 16)
-    packed = call(
-        functools.partial(pack_kernel, dests, cap, pixels),
-        jax.ShapeDtypeStruct((dests, rows_slot, hidden_size), BF16),
-        [smem_spec()] + vmem_specs(3),
-        [],
-        (2 * slots * slots * 128, 1 << 20, 0),
-        slot_count,
-        slot_target.reshape(1, slots),
-        carry_flow.T.astype(F32),
-        carry_hidden,
-    )
-    windows = call(
-        functools.partial(window_kernel, own, half_wide),
-        jax.ShapeDtypeStruct((dests, rows_per * WIN, hidden_size), BF16),
-        [smem_spec()] + vmem_specs(1),
-        [pltpu.VMEM((rows_per, padded, 128), F32)],
-        (0, 1 << 18, 0),
-        here,
-        context,
-    )
-    early = lax.all_to_all(jnp.concatenate([packed, windows], axis=1), "rows", 0, 0, tiled=True)
+        keys = (beside,)
     ow = jnp.pad(offset_weight, ((0, 2), (0, 0)))
     hidden_wide, flow_first, term = call(
         functools.partial(place_kernel, cap, half_wide, rows_per),
@@ -490,19 +485,21 @@
             jax.ShapeDtypeStruct((8, pixels), F32),
             jax.ShapeDtypeStruct((rows_per, half_wide, 128), F32),
         ),
-        [smem_spec()] + vmem_specs(2),
+        vmem_specs(2),
         [pltpu.VMEM((rows_per, padded, 128), F32)] * 2,
         (2 * slots * pixels * 128, 1 << 20, 0),
-        here,
+        room,
         early,
         ow,
     )
+    queries = frame_one.reshape(pixels, channels)
+    queries, hidden_wide, term = lax.optimization_barrier((queries, hidden_wide, term))
     chunks = dests // 2
     tile = 128
     keep, send = call(
         functools.partial(match_kernel, len(keys), len(keys) > 1, half_wide, rows_per),
         (jax.ShapeDtypeStruct((rows_per, half_wide, 384), F32),) * 2,
-        [smem_spec()] + vmem_specs(3 + len(keys)),
+        vmem_specs(3 + len(keys)),
         [
             pltpu.VMEM((chunks, 4 * columns, channels), BF16),
             pltpu.VMEM((chunks, columns, channels), BF16),
@@ -511,8 +508,8 @@
             pltpu.VMEM((rows_per, padded, 384), F32),
         ],
         (4 * pixels * chunks * 4 * columns * channels, 1 << 21, pixels * chunks * 5 * columns),
-        here,
-        frame_one.reshape(pixels, channels),
+        room,
+        queries,
         match_weight,
         ow,
         *keys,
@@ -524,6 +521,7 @@
         vmem_specs(4),
         [],
         (0, 1 << 20, 0),
+        room,
         keep,
         other,
         term,
@@ -535,7 +533,7 @@
     outgoing = call(
         functools.partial(update_kernel, own, width),
         jax.ShapeDtypeStruct((dests, back_rows, 128), F32),
-        [smem_spec()] + vmem_specs(8),
+        vmem_specs(8),
         [
             pltpu.VMEM((count, 128), BF16),
             pltpu.VMEM((count, 128), F32),
@@ -549,7 +547,7 @@
             pltpu.VMEM((count, 8), F32),
         ],
         (16 * count * 5 * 384 * 256, 1 << 22, 8 * count * 384),
-        here,
+        room,
         arrived,
         early[:, rows_slot:, :],
         ow,

time: 110 us -> 87 us (0.79)
  Pallas kernels: 32.3 us -> 22.5 us
  other arithmetic: 4.45 us -> 0.6 us
  waiting for transfers between devices: 34.6 us -> 31 us
  local copies, waits for them, and re-layouts: 8.72 us -> 5.58 us
  starting transfers between devices: 25.5 us -> 23.3 us
    ppermute x7, waiting for transfers between devices: 20.2 us -> 2.1 us  [swap(): return lax.ppermute(value, 'rows', [(i, i ^ flip) for i in range(dests)])]
    all_to_all x1, waiting for transfers between devices: 0.01 us -> 10.4 us  [local(): early = lax.all_to_all(packed, 'rows', 0, 0, tiled=True)]
    pallas_call x6 -> x5, Pallas kernels: 32.3 us -> 22.5 us  [call(): pl.pallas_call(kernel, out_shape=out_shape, in_specs=in_specs, out_specs=...]
    all_to_all x1, starting transfers between devices: 7.28 us -> 3.75 us  [local(): early = lax.all_to_all(packed, 'rows', 0, 0, tiled=True)]
    concatenate x1 -> x0, other arithmetic: 1.91 us -> none  [local(): jnp.concatenate([packed, windows], axis=1)]
    ppermute x1, waiting for transfers between devices: 0.01 us -> 1.78 us  [local(): lax.ppermute(send, 'loop', [(i, (i + 1) % halves) for i in range(halves)])]
    all_to_all x1, waiting for transfers between devices: 7.43 us -> 9.18 us  [local(): arrived = lax.all_to_all(sending, 'rows', 0, 0, tiled=True)]
    unnamed x29 -> x27, local copies, waits for them, and re-layouts: 2.92 us -> 4.52 us
  transfers between devices with their start and end apart: 11 -> 11, of which waited for: 6 -> 5; matrix products, arithmetic and copies ran while one was open for 3% -> 0% of each run, Pallas kernels for 10% -> 7%
where the time goes in v2:
time: 87 us; the launch traced here: 86.4 us
  waiting for transfers between devices  31 us (36%)
  starting transfers between devices  23.3 us (27%)
  Pallas kernels  22.5 us (26%)
  local copies, waits for them, and re-layouts  5.58 us (6%)
  blocking collectives  2.03 us (2%)
  between operations  1.49 us (2%)
    pallas_call x5, Pallas kernels, call(): pl.pallas_call(kernel, out_shape=out_shape, in_specs=in_specs, out_specs=...  22.5 us
    ppermute x7, starting transfers between devices, swap(): return lax.ppermute(value, 'rows', [(i, i ^ flip) for i in range(dests)])  11.5 us
    all_to_all x1, waiting for transfers between devices, local(): early = lax.all_to_all(packed, 'rows', 0, 0, tiled=True)  10.4 us
    all_to_all x1, waiting for transfers between devices, local(): arrived = lax.all_to_all(sending, 'rows', 0, 0, tiled=True)  9.18 us
    all_to_all x1, waiting for transfers between devices, local(): back = lax.all_to_all(outgoing, 'rows', 0, 0, tiled=True)  7.54 us
    unnamed x27, local copies, waits for them, and re-layouts  4.52 us
    all_to_all x1, starting transfers between devices, local(): arrived = lax.all_to_all(sending, 'rows', 0, 0, tiled=True)  4.38 us
    all_to_all x1, starting transfers between devices, local(): early = lax.all_to_all(packed, 'rows', 0, 0, tiled=True)  3.75 us
  transfers between devices with their start and end apart: 11, of which 5 were waited for; matrix products, arithmetic and copies ran while one was open for 0% of the time, Pallas kernels for 7%

profile of v2, /device:TPU:0, one launch (start us, length us, event | category | flops | bytes accessed | tf_op | source)
XLA Modules:
  0.0 86.4 jit_solution(12107057518393623449)
XLA Ops:
  0.6 0.0 copy-start.11
  0.6 3.0 %collective-permute-start = (bf16[1,2,128,256]{3,2,1,0:T(8,128)(2,1)}, bf16[1,2,128,256]{3,2,1,0:T(8,128)(2,1)S(1)}, u32[]{:S(2)}, u32[]{:S(2)}) collective-permute-start(bf16[1,2,128,256]{3,2,1,0:T(8,128)(2,1)} %bitcast.15), channel_id=1, source_target_pairs={{0,2},{2,0},{4,6},{6,4},{8,10},{10,8},{12,14},{14,12},{1,3},{3,1},... | collective-permute-start | bytes 393224 | tf_op jit(solution)/shard_map/ppermute | solution.py:451
  3.7 3.6 %collective-permute-start.3 = (bf16[1,2,128,256]{3,2,1,0:T(8,128)(2,1)}, bf16[1,2,128,256]{3,2,1,0:T(8,128)(2,1)S(1)}, u32[]{:S(2)}, u32[]{:S(2)}) collective-permute-start(bf16[1,2,128,256]{3,2,1,0:T(8,128)(2,1)} %bitcast.16), channel_id=1, source_target_pairs={{0,12},{2,14},{4,8},{6,10},{8,4},{10,6},{12,0},{14,2},{1,13},{3,15... | collective-permute-start | bytes 393224 | tf_op jit(solution)/shard_map/ppermute | solution.py:451
  7.3 0.0 collective-permute-start.2
  7.3 0.8 collective-permute-start.1
  8.7 0.0 collective-permute-done.refs_1_
  8.7 0.0 copy-start.2
  8.7 1.0 %copy-done.2 = bf16[1536,128]{1,0:T(8,128)(2,1)S(1)} copy-done((bf16[1536,128]{1,0:T(8,128)(2,1)S(1)}, bf16[1536,128]{1,0:T(8,128)(2,1)}, u32[]{:S(2)}) %copy-start.2) | copy-done | bytes 393240
  9.7 0.0 copy-start.4
  9.7 0.9 %copy-done.4 = bf16[2,256,128]{2,1,0:T(8,128)(2,1)S(1)} copy-done((bf16[2,256,128]{2,1,0:T(8,128)(2,1)S(1)}, bf16[2,256,128]{2,1,0:T(8,128)(2,1)}, u32[]{:S(2)}) %copy-start.4) | copy-done | bytes 131096
  10.6 0.0 copy-start.8
  10.6 0.7 copy-done.8
  11.3 0.0 copy-start.9
  11.3 0.7 copy-done.9
  12.0 0.0 copy-start.3
  12.0 0.0 copy-start.5
  12.0 0.0 copy-start.6
  12.0 4.2 %shard_map.149 = bf16[8,272,128]{2,1,0:T(8,128)(2,1)} custom-call(s32[1]{0:T(128)S(6)} %copy.23.count_ref, s32[12,128]{1,0:T(8,128)S(1)} %bitcast.20, bf16[2,1536]{1,0:T(2,128)(2,1)S(1)} %bitcast.21, bf16[1536,128]{1,0:T(8,128)(2,1)S(1)} %copy-done.2, bf16[2,256,128]{2,1,0:T(8,128)(2,1)S(1)} %copy-done.4), custom_call_target="tpu_custom_call" | custom-call | flops 603979776 | bytes 1048576 | tf_op jit(solution)/shard_map/pallas_call | solution.py:52
  16.2 0.0 collective-permute-done.3.refs_6_
  16.2 2.1 %collective-permute-done.2.refs_4_ = bf16[1,2,128,256]{3,2,1,0:T(8,128)(2,1)S(1)} collective-permute-done((bf16[1,2,128,256]{3,2,1,0:T(8,128)(2,1)}, bf16[1,2,128,256]{3,2,1,0:T(8,128)(2,1)S(1)}, u32[]{:S(2)}, u32[]{:S(2)}) %collective-permute-start.2) | collective-permute-done | bytes 131104 | tf_op jit(solution)/shard_map/ppermute | solution.py:451
  18.3 0.0 collective-permute-done.1.refs_2_
  18.3 3.8 %all-to-all-start = ((bf16[8,272,128]{2,1,0:T(8,128)(2,1)}), bf16[8,272,128]{2,1,0:T(8,128)(2,1)S(1)}, u32[]{:S(2)}, u32[]{:S(2)}) async-start(bf16[8,272,128]{2,1,0:T(8,128)(2,1)} %shard_map.149), calls=%async_computation | async-start | bytes 1114112 | tf_op jit(solution)/shard_map/all_to_all | solution.py:474
  22.0 2.0 %collective-permute-start.4 = (bf16[1,2,128,256]{3,2,1,0:T(8,128)(2,1)S(1)}, bf16[1,2,128,256]{3,2,1,0:T(8,128)(2,1)S(1)}, u32[]{:S(2)}, u32[]{:S(2)}) collective-permute-start(bf16[1,2,128,256]{3,2,1,0:T(8,128)(2,1)S(1)} %collective-permute-done.1.refs_2_), channel_id=1, source_target_pairs={{0,2},{2,0},{4,6},{6,4},{8,10},{10,8},{12,14},{14,12},{1,3},{3,1},... | collective-permute-start | bytes 393224 | tf_op jit(solution)/shard_map/ppermute | solution.py:451
  24.1 0.0 collective-permute-start.5
  24.1 2.0 %collective-permute-start.6 = (bf16[1,2,128,256]{3,2,1,0:T(8,128)(2,1)S(1)}, bf16[1,2,128,256]{3,2,1,0:T(8,128)(2,1)S(1)}, u32[]{:S(2)}, u32[]{:S(2)}) collective-permute-start(bf16[1,2,128,256]{3,2,1,0:T(8,128)(2,1)S(1)} %collective-permute-done.3.refs_6_), channel_id=1, source_target_pairs={{0,2},{2,0},{4,6},{6,4},{8,10},{10,8},{12,14},{14,12},{1,3},{3,1},... | collective-permute-start | bytes 393224 | tf_op jit(solution)/shard_map/ppermute | solution.py:451
  26.1 0.0 copy-done.11
  26.1 10.4 %all-to-all-done.got_ref = bf16[8,272,128]{2,1,0:T(8,128)(2,1)S(1)} async-done(((bf16[8,272,128]{2,1,0:T(8,128)(2,1)}), bf16[8,272,128]{2,1,0:T(8,128)(2,1)S(1)}, u32[]{:S(2)}, u32[]{:S(2)}) %all-to-all-start) | async-done | bytes 557088 | tf_op jit(solution)/shard_map/all_to_all | solution.py:474
  36.5 1.6 %shard_map.150 = (bf16[2,144,128]{2,1,0:T(8,128)(2,1)S(1)}, f32[8,512]{1,0:T(8,128)S(1)}, f32[2,144,128]{2,1,0:T(8,128)S(1)}) custom-call(bf16[8,272,128]{2,1,0:T(8,128)(2,1)S(1)} %all-to-all-done.got_ref, f32[8,128]{1,0:T(8,128)S(1)} %pad.8.ow_ref), custom_call_target="tpu_custom_call" | custom-call | flops 201326592 | bytes 1048576 | tf_op jit(solution)/shard_map/pallas_call | solution.py:52
  38.1 0.0 copy-start.12
  38.1 0.0 collective-permute-done.4.refs_3_
  38.2 0.0 collective-permute-done.5.refs_5_
  38.2 0.0 collective-permute-done.6.refs_7_
  38.2 0.0 copy-done.3
  38.2 0.0 copy-done.5
  38.2 0.0 copy-done.6
  38.2 5.5 %shard_map.151 = (f32[2,144,384]{2,1,0:T(8,128)S(1)}, f32[2,144,384]{2,1,0:T(8,128)S(1)}) custom-call(bf16[512,256]{1,0:T(8,128)(2,1)S(1)} %bitcast.14, bf16[512,128]{1,0:T(8,128)(2,1)S(1)} %copy-done.5, f32[8,128]{1,0:T(8,128)S(1)} %pad.8.ow_ref, bf16[1,2,128,256]{3,2,1,0:T(8,128)(2,1)S(1)} %bitcast.19, ...), custom_call_target="tpu_custom_call" | custom-call | flops 1073741824 | bytes 2097152 | tf_op jit(solution)/shard_map/pallas_call | solution.py:52
  43.7 0.0 copy-start
  43.8 0.0 copy-start.7
  43.8 0.0 copy-start.10
  43.8 0.1 collective-permute-start.7
  43.9 1.8 %collective-permute-done.7.got_ref = f32[2,144,384]{2,1,0:T(8,128)S(1)} collective-permute-done((f32[2,144,384]{2,1,0:T(8,128)S(1)}, f32[2,144,384]{2,1,0:T(8,128)S(1)}, u32[]{:S(2)}, u32[]{:S(2)}) %collective-permute-start.7) | collective-permute-done | bytes 442400 | tf_op jit(solution)/shard_map/ppermute | solution.py:517
  45.6 0.9 %shard_map.152 = bf16[8,64,256]{2,1,0:T(8,128)(2,1)} custom-call(f32[2,144,384]{2,1,0:T(8,128)S(1)} %get-tuple-element.25.keep_ref, f32[2,144,384]{2,1,0:T(8,128)S(1)} %collective-permute-done.7.got_ref, f32[2,144,128]{2,1,0:T(8,128)S(1)} %get-tuple-element.27.term_ref, bf16[2,144,128]{2,1,0:T(8,128)(2,1)S(1)} %get-tuple-element.28.hidden_ref), custom_call_target="tpu_custom_call" | custom-call | bytes 1048576 | tf_op jit(solution)/shard_map/pallas_call | solution.py:52
  46.5 4.4 %all-to-all-start.1 = ((bf16[8,64,256]{2,1,0:T(8,128)(2,1)}), bf16[8,64,256]{2,1,0:T(8,128)(2,1)S(1)}, u32[]{:S(2)}, u32[]{:S(2)}) async-start(bf16[8,64,256]{2,1,0:T(8,128)(2,1)} %shard_map.152), calls=%async_computation.1 | async-start | bytes 524288 | tf_op jit(solution)/shard_map/all_to_all | solution.py:530
  50.9 0.0 copy-done.12
  50.9 9.2 %all-to-all-done.1.got_ref = bf16[8,64,256]{2,1,0:T(8,128)(2,1)S(1)} async-done(((bf16[8,64,256]{2,1,0:T(8,128)(2,1)}), bf16[8,64,256]{2,1,0:T(8,128)(2,1)S(1)}, u32[]{:S(2)}, u32[]{:S(2)}) %all-to-all-start.1) | async-done | bytes 262176 | tf_op jit(solution)/shard_map/all_to_all | solution.py:530
  60.1 0.0 copy-done
  60.1 0.0 copy-done.7
  60.1 0.0 copy-done.10
  60.1 0.0 copy-start.1
  60.1 1.2 %copy-done.1 = bf16[2,5,384,128]{3,2,1,0:T(8,128)(2,1)S(1)} copy-done((bf16[2,5,384,128]{3,2,1,0:T(8,128)(2,1)S(1)}, bf16[2,5,384,128]{3,2,1,0:T(8,128)(2,1)}, u32[]{:S(2)}) %copy-start.1) | copy-done | bytes 983064
  61.3 10.3 %shard_map.153 = f32[8,40,128]{2,1,0:T(8,128)} custom-call(bf16[8,64,256]{2,1,0:T(8,128)(2,1)S(1)} %all-to-all-done.1.got_ref, bf16[8,64,128]{2,1,0:T(8,128)(2,1)S(1)} %slice.20.context_ref, f32[8,128]{1,0:T(8,128)S(1)} %pad.8.ow_ref, bf16[2,5,384,256]{3,2,1,0:T(8,128)(2,1)S(1)} %copy-done, bf16[2,5,384,128]{3,2,1,0:T(8,128)(2,1)S(1)} %copy-done.1, ...), custom_call_target="tpu_custom_call" | custom-call | flops 4026531840 | bytes 4194304 | tf_op jit(solution)/shard_map/pallas_call | solution.py:52
  71.6 3.6 %all-to-all-start.2 = ((f32[8,40,128]{2,1,0:T(8,128)}), f32[8,40,128]{2,1,0:T(8,128)S(1)}, u32[]{:S(2)}, u32[]{:S(2)}) async-start(f32[8,40,128]{2,1,0:T(8,128)} %shard_map.153), calls=%async_computation.2 | async-start | bytes 327680 | tf_op jit(solution)/shard_map/all_to_all | solution.py:560
  75.2 7.5 %all-to-all-done.2 = f32[8,40,128]{2,1,0:T(8,128)S(1)} async-done(((f32[8,40,128]{2,1,0:T(8,128)}), f32[8,40,128]{2,1,0:T(8,128)S(1)}, u32[]{:S(2)}, u32[]{:S(2)}) %all-to-all-start.2) | async-done | bytes 163872 | tf_op jit(solution)/shard_map/all_to_all | solution.py:560
  82.8 2.0 %all-gather = f32[16,40,128]{2,1,0:T(8,128)S(1)} all-gather(f32[8,40,128]{2,1,0:T(8,128)S(1)} %all-to-all-done.2), channel_id=2, replica_groups=mesh['groups'=2,'rows'=8,'loop'=2] {'loop'}, dimensions={0}, use_global_device_ids=true | all-gather | bytes 491520 | tf_op jit(solution)/shard_map/all_gather | solution.py:561
  84.8 0.7 copy.18
  85.5 0.1 reshape.34
  85.6 0.1 slice.23
  85.8 0.1 reshape.35
  85.8 0.6 add.7
  (8 shorter events, 0.1 us)
Async XLA Ops:
  0.6 25.5 %copy-start.11 = (f32[6,128]{1,0:T(8,128)S(1)}, f32[6,128]{1,0:T(8,128)}, u32[]{:S(2)}) copy-start(f32[6,128]{1,0:T(8,128)} %param.22) | copy-start | bytes 9220
  0.6 8.1 %collective-permute-start = (bf16[1,2,128,256]{3,2,1,0:T(8,128)(2,1)}, bf16[1,2,128,256]{3,2,1,0:T(8,128)(2,1)S(1)}, u32[]{:S(2)}, u32[]{:S(2)}) collective-permute-start(bf16[1,2,128,256]{3,2,1,0:T(8,128)(2,1)} %bitcast.15), channel_id=1, source_target_pairs={{0,2},{2,0},{4,6},{6,4},{8,10},{10,8},{12,14},{14,12},{1,3},{3,1},... | collective-permute-start | bytes 393224 | tf_op jit(solution)/shard_map/ppermute | solution.py:451
  3.7 12.5 %collective-permute-start.3 = (bf16[1,2,128,256]{3,2,1,0:T(8,128)(2,1)}, bf16[1,2,128,256]{3,2,1,0:T(8,128)(2,1)S(1)}, u32[]{:S(2)}, u32[]{:S(2)}) collective-permute-start(bf16[1,2,128,256]{3,2,1,0:T(8,128)(2,1)} %bitcast.16), channel_id=1, source_target_pairs={{0,12},{2,14},{4,8},{6,10},{8,4},{10,6},{12,0},{14,2},{1,13},{3,15... | collective-permute-start | bytes 393224 | tf_op jit(solution)/shard_map/ppermute | solution.py:451
  7.3 11.0 %collective-permute-start.2 = (bf16[1,2,128,256]{3,2,1,0:T(8,128)(2,1)}, bf16[1,2,128,256]{3,2,1,0:T(8,128)(2,1)S(1)}, u32[]{:S(2)}, u32[]{:S(2)}) collective-permute-start(bf16[1,2,128,256]{3,2,1,0:T(8,128)(2,1)} %bitcast.17), channel_id=1, source_target_pairs={{0,8},{2,10},{4,12},{6,14},{8,0},{10,2},{12,4},{14,6},{1,9},{3,11}... | collective-permute-start | bytes 393224 | tf_op jit(solution)/shard_map/ppermute | solution.py:451
  7.3 11.0 %collective-permute-start.1 = (bf16[1,2,128,256]{3,2,1,0:T(8,128)(2,1)}, bf16[1,2,128,256]{3,2,1,0:T(8,128)(2,1)S(1)}, u32[]{:S(2)}, u32[]{:S(2)}) collective-permute-start(bf16[1,2,128,256]{3,2,1,0:T(8,128)(2,1)} %bitcast.18), channel_id=1, source_target_pairs={{0,4},{2,6},{4,0},{6,2},{8,12},{10,14},{12,8},{14,10},{1,5},{3,7},... | collective-permute-start | bytes 393224 | tf_op jit(solution)/shard_map/ppermute | solution.py:451
  8.7 1.0 %copy-start.2 = (bf16[1536,128]{1,0:T(8,128)(2,1)S(1)}, bf16[1536,128]{1,0:T(8,128)(2,1)}, u32[]{:S(2)}) copy-start(bf16[1536,128]{1,0:T(8,128)(2,1)} %hidden_ref.1) | copy-start | bytes 1179652
  9.7 0.9 %copy-start.4 = (bf16[2,256,128]{2,1,0:T(8,128)(2,1)S(1)}, bf16[2,256,128]{2,1,0:T(8,128)(2,1)}, u32[]{:S(2)}) copy-start(bf16[2,256,128]{2,1,0:T(8,128)(2,1)} %context_ref.1) | copy-start | bytes 393220
  10.6 0.7 copy-start.8
  11.3 0.7 copy-start.9
  12.0 26.2 %copy-start.3 = (bf16[2,256,256]{2,1,0:T(8,128)(2,1)S(1)}, bf16[2,256,256]{2,1,0:T(8,128)(2,1)}, u32[]{:S(2)}) copy-start(bf16[2,256,256]{2,1,0:T(8,128)(2,1)} %param.14) | copy-start | bytes 786436
  12.0 26.2 %copy-start.5 = (bf16[512,128]{1,0:T(8,128)(2,1)S(1)}, bf16[512,128]{1,0:T(8,128)(2,1)}, u32[]{:S(2)}) copy-start(bf16[512,128]{1,0:T(8,128)(2,1)} %weight_ref.1) | copy-start | bytes 393220
  12.0 26.2 %copy-start.6 = (bf16[2,128,256]{2,1,0:T(8,128)(2,1)S(1)}, bf16[2,128,256]{2,1,0:T(8,128)(2,1)}, u32[]{:S(2)}) copy-start(bf16[2,128,256]{2,1,0:T(8,128)(2,1)} %param.15) | copy-start | bytes 393220
  18.3 18.2 %all-to-all-start = ((bf16[8,272,128]{2,1,0:T(8,128)(2,1)}), bf16[8,272,128]{2,1,0:T(8,128)(2,1)S(1)}, u32[]{:S(2)}, u32[]{:S(2)}) async-start(bf16[8,272,128]{2,1,0:T(8,128)(2,1)} %shard_map.149), calls=%async_computation | async-start | bytes 1114112 | tf_op jit(solution)/shard_map/all_to_all | solution.py:474
  22.0 16.1 %collective-permute-start.4 = (bf16[1,2,128,256]{3,2,1,0:T(8,128)(2,1)S(1)}, bf16[1,2,128,256]{3,2,1,0:T(8,128)(2,1)S(1)}, u32[]{:S(2)}, u32[]{:S(2)}) collective-permute-start(bf16[1,2,128,256]{3,2,1,0:T(8,128)(2,1)S(1)} %collective-permute-done.1.refs_2_), channel_id=1, source_target_pairs={{0,2},{2,0},{4,6},{6,4},{8,10},{10,8},{12,14},{14,12},{1,3},{3,1},... | collective-permute-start | bytes 393224 | tf_op jit(solution)/shard_map/ppermute | solution.py:451
  24.1 14.1 %collective-permute-start.5 = (bf16[1,2,128,256]{3,2,1,0:T(8,128)(2,1)S(1)}, bf16[1,2,128,256]{3,2,1,0:T(8,128)(2,1)S(1)}, u32[]{:S(2)}, u32[]{:S(2)}) collective-permute-start(bf16[1,2,128,256]{3,2,1,0:T(8,128)(2,1)S(1)} %collective-permute-done.2.refs_4_), channel_id=1, source_target_pairs={{0,2},{2,0},{4,6},{6,4},{8,10},{10,8},{12,14},{14,12},{1,3},{3,1},... | collective-permute-start | bytes 393224 | tf_op jit(solution)/shard_map/ppermute | solution.py:451
  24.1 14.1 %collective-permute-start.6 = (bf16[1,2,128,256]{3,2,1,0:T(8,128)(2,1)S(1)}, bf16[1,2,128,256]{3,2,1,0:T(8,128)(2,1)S(1)}, u32[]{:S(2)}, u32[]{:S(2)}) collective-permute-start(bf16[1,2,128,256]{3,2,1,0:T(8,128)(2,1)S(1)} %collective-permute-done.3.refs_6_), channel_id=1, source_target_pairs={{0,2},{2,0},{4,6},{6,4},{8,10},{10,8},{12,14},{14,12},{1,3},{3,1},... | collective-permute-start | bytes 393224 | tf_op jit(solution)/shard_map/ppermute | solution.py:451
  38.1 12.8 %copy-start.12 = (bf16[2,256]{1,0:T(2,128)(2,1)S(1)}, bf16[2,256]{1,0:T(2,128)(2,1)}, u32[]{:S(2)}) copy-start(bf16[2,256]{1,0:T(2,128)(2,1)} %param.27) | copy-start | bytes 3076
  43.7 16.4 %copy-start = (bf16[2,5,384,256]{3,2,1,0:T(8,128)(2,1)S(1)}, bf16[2,5,384,256]{3,2,1,0:T(8,128)(2,1)}, u32[]{:S(2)}) copy-start(bf16[2,5,384,256]{3,2,1,0:T(8,128)(2,1)} %gate_ref.1) | copy-start | bytes 5898244
  43.8 16.4 %copy-start.7 = (bf16[128,256]{1,0:T(8,128)(2,1)S(1)}, bf16[128,256]{1,0:T(8,128)(2,1)}, u32[]{:S(2)}) copy-start(bf16[128,256]{1,0:T(8,128)(2,1)} %head_ref.1) | copy-start | bytes 196612
  43.8 16.4 %copy-start.10 = (f32[2,384]{1,0:T(2,128)S(1)}, f32[2,384]{1,0:T(2,128)}, u32[]{:S(2)}) copy-start(f32[2,384]{1,0:T(2,128)} %bias_ref.1) | copy-start | bytes 9220
  43.8 1.9 %collective-permute-start.7 = (f32[2,144,384]{2,1,0:T(8,128)S(1)}, f32[2,144,384]{2,1,0:T(8,128)S(1)}, u32[]{:S(2)}, u32[]{:S(2)}) collective-permute-start(f32[2,144,384]{2,1,0:T(8,128)S(1)} %get-tuple-element.26), channel_id=1, source_target_pairs={{0,1},{1,0},{2,3},{3,2},{4,5},{5,4},{6,7},{7,6},{8,9},{9,8},{10,11... | collective-permute-start | bytes 1327112 | tf_op jit(solution)/shard_map/ppermute | solution.py:517
  46.5 13.6 %all-to-all-start.1 = ((bf16[8,64,256]{2,1,0:T(8,128)(2,1)}), bf16[8,64,256]{2,1,0:T(8,128)(2,1)S(1)}, u32[]{:S(2)}, u32[]{:S(2)}) async-start(bf16[8,64,256]{2,1,0:T(8,128)(2,1)} %shard_map.152), calls=%async_computation.1 | async-start | bytes 524288 | tf_op jit(solution)/shard_map/all_to_all | solution.py:530
  60.1 1.2 %copy-start.1 = (bf16[2,5,384,128]{3,2,1,0:T(8,128)(2,1)S(1)}, bf16[2,5,384,128]{3,2,1,0:T(8,128)(2,1)}, u32[]{:S(2)}) copy-start(bf16[2,5,384,128]{3,2,1,0:T(8,128)(2,1)} %state_ref.1) | copy-start | bytes 2949124
  71.6 11.2 %all-to-all-start.2 = ((f32[8,40,128]{2,1,0:T(8,128)}), f32[8,40,128]{2,1,0:T(8,128)S(1)}, u32[]{:S(2)}, u32[]{:S(2)}) async-start(f32[8,40,128]{2,1,0:T(8,128)} %shard_map.153), calls=%async_computation.2 | async-start | bytes 327680 | tf_op jit(solution)/shard_map/all_to_all | solution.py:560

commit v3 on v2

--- a/solution.py
+++ b/solution.py
@@ -60,7 +60,8 @@
     )(*args)
 
 
-def pack_kernel(dests, cap, pixels, own, half_wide, count_ref, target_ref, flow_ref, hidden_ref, context_ref, out_ref, wide):
+def pack_kernel(dests, cap, pixels, own, half_wide, count_ref, target_ref, flow_ref, hidden_ref, context_ref, shard_ref, out_ref, pass_ref, wide):
+    pass_ref[...] = shard_ref[...]
     slots = hidden_ref.shape[0]
     target = jnp.concatenate([target_ref[k : k + 1, :] for k in range(slots // 128)], axis=1)
     counted = iota((1, slots), 1) < count_ref[0]
@@ -299,19 +300,86 @@
 
 
 def sigmoid(x):
-    return 1.0 / (1.0 + jnp.exp(-x))
+    return 0.5 * jnp.tanh(0.5 * x) + 0.5
+
+
+def shifted(value, tap):
+    return value if tap == 2 else pltpu.roll(value, (2 - tap) % TILE, 0)
+
+
+def each_tile(count, body):
+    def step(t, carry):
+        body(pl.multiple_of(t * TILE, TILE))
+        return carry
+
+    lax.fori_loop(0, count // TILE, step, 0, unroll=count == TILE)
+
+
+def fetch(copies, sems, first=0):
+    handles = []
+    for k, (source, target) in enumerate(copies):
+        handles.append(pltpu.make_async_copy(source, target, sems.at[first + k]))
+        handles[-1].start()
+    return handles
+
+
+def context_kernel(early_ref, gate_hbm, state_hbm, bias_ref, fixed_ref, gate_ref, state_ref, padded, taps, sems):
+    handles = fetch(
+        [
+            (gate_hbm.at[:, :, pl.ds(128, 128), :], gate_ref),
+            (state_hbm.at[:, :, pl.ds(128, 128), :], state_ref),
+        ],
+        sems,
+    )
+    dests = early_ref.shape[0]
+    count = fixed_ref.shape[1]
+    per_dest = count // dests
+    first = early_ref.shape[1] - per_dest
+    pad = 2 * WIN
+    padded[0:pad, :] = jnp.zeros((pad, 128), BF16)
+    padded[pad + count : pad + count + pad, :] = jnp.zeros((pad, 128), BF16)
+    for j in range(dests):
+        padded[pad + j * per_dest : pad + (j + 1) * per_dest, :] = early_ref[j, first : first + per_dest, :]
+    for handle in handles:
+        handle.wait()
+    for p in range(2):
+
+        def one(at):
+            for tap in range(5):
+                if p == 0:
+                    value = shifted(padded[pl.ds(pad + at, TILE), :].astype(F32), tap).astype(BF16)
+                else:
+                    value = padded[pl.ds(at + tap * WIN, TILE), :]
+                taps[:, tap * 128 : (tap + 1) * 128] = value
+            gate = gate_ref[p].reshape(640, 256)
+            state = state_ref[p].reshape(640, 128)
+            fixed_ref[p, pl.ds(at, TILE), 0:256] = dot(taps[...], gate) + bias_ref[p : p + 1, 0:256]
+            fixed_ref[p, pl.ds(at, TILE), 256:384] = dot(taps[...], state) + bias_ref[p : p + 1, 256:384]
+
+        each_tile(count, one)
 
 
 def update_kernel(
-    own, width, got_ref, context_ref, ow_ref, gate_ref, state_ref, bias_ref, head_ref, delta_ref,
-    out_ref, base, hidden, inputs, states, resets, updates, col_in, col_st, flow, flow_cols,
+    own, width, got_ref, fixed_ref, ow_ref, gate_hbm, state_hbm, head_ref, delta_ref,
+    out_ref, base, hidden, motions, states, resets, updates, taps, flow, flow_cols, gate_ref, state_ref, sems,
 ):
+    handles = []
+    for p in range(2):
+        for source, target in ((gate_hbm, gate_ref), (state_hbm, state_ref)):
+            parts = [
+                (source.at[p, :, pl.ds(256 * k, 128), :], target.at[p, :, pl.ds(128 * k, 128), :]) for k in range(2)
+            ]
+            handles.append(fetch(parts, sems, 2 * len(handles)))
+
+    def ready(k):
+        for handle in handles[k]:
+            handle.wait()
+
     me, half = lax.axis_index("rows"), lax.axis_index("loop")
     dests, per_dest, _ = got_ref.shape
     rows_per = per_dest // WIN
     count = dests * per_dest
     pad = 2 * WIN
-    tiles = count // TILE
     first_col = (half * dests + me) * own - HALO
     column = first_col + iota((TILE, 128), 0) % WIN
     inside = (column >= 0) & (column < width)
@@ -319,32 +387,20 @@
     ow = ow_ref[...]
     add_row = OFFSET_SCALE * (ow[4:5] - ow[0:1] - ow[2:3])
     add_col = OFFSET_SCALE * (ow[5:6] - ow[1:2] - ow[3:4])
-    bias = bias_ref[...]
-
-    for ref in (inputs, states, resets):
-        ref[0:pad, :] = jnp.zeros((pad, ref.shape[1]), BF16)
-        ref[pad + count : pad + count + pad, :] = jnp.zeros((pad, ref.shape[1]), BF16)
+
+    for ref in (motions, states, resets):
+        ref[0:pad, :] = jnp.zeros((pad, 128), BF16)
+        ref[pad + count : pad + count + pad, :] = jnp.zeros((pad, 128), BF16)
     for j in range(dests):
         at = j * per_dest
         base[at : at + per_dest, :] = got_ref[j, :, 0:128]
         hidden[at : at + per_dest, :] = got_ref[j, :, 128:256].astype(F32)
-        inputs[pad + at : pad + at + per_dest, 0:128] = context_ref[j]
-    flow[...] = jnp.zeros_like(flow)
-    flow_cols[...] = jnp.zeros_like(flow_cols)
-
-    def each(body):
-        def step(t, carry):
-            body(pl.multiple_of(t * TILE, TILE))
-            return carry
-
-        lax.fori_loop(0, tiles, step, 0, unroll=tiles == 1)
-
-    def shifted(value, tap):
-        return value if tap == 2 else pltpu.roll(value, (2 - tap) % TILE, 0)
 
     def finish(at, update, candidate):
         old = hidden[pl.ds(at, TILE), :]
-        hidden[pl.ds(at, TILE), :] = ((1.0 - update) * old + update * candidate) * mask
+        new = (old + update * (candidate - old)) * mask
+        hidden[pl.ds(at, TILE), :] = new
+        return new
 
     for iteration in range(ITERS):
 
@@ -354,57 +410,58 @@
                 moved = flow_cols[pl.ds(at, TILE), :]
                 motion = (motion + moved[:, 0:1] * add_row + moved[:, 1:2] * add_col) * mask
             motion = jnp.maximum(motion, 0.0)
-            inputs[pl.ds(pad + at, TILE), 128:256] = motion.astype(BF16)
-            context = inputs[pl.ds(pad + at, TILE), 0:128].astype(F32)
-            motion = motion.astype(BF16).astype(F32)
+            rounded = motion.astype(BF16)
+            motions[pl.ds(pad + at, TILE), :] = rounded
+            motion = rounded.astype(F32)
             state = hidden[pl.ds(at, TILE), :].astype(BF16).astype(F32)
             for tap in range(5):
-                if iteration == 0:
-                    col_in[pl.ds(at, TILE), tap * 256 : tap * 256 + 128] = shifted(context, tap).astype(BF16)
-                col_in[pl.ds(at, TILE), tap * 256 + 128 : tap * 256 + 256] = shifted(motion, tap).astype(BF16)
-                col_st[:, tap * 128 : (tap + 1) * 128] = shifted(state, tap).astype(BF16)
-            gates = dot(col_st[...], gate_ref[0, :, 0:128, :].reshape(640, 256)) + dot(
-                col_in[pl.ds(at, TILE), :], gate_ref[0, :, 128:384, :].reshape(1280, 256)
-            )
-            gates = sigmoid(gates + bias[0:1, 0:256])
+                taps[:, tap * 256 : tap * 256 + 128] = shifted(state, tap).astype(BF16)
+                taps[:, tap * 256 + 128 : tap * 256 + 256] = shifted(motion, tap).astype(BF16)
+            if iteration == 0 and count == TILE:
+                ready(0)
+            gates = sigmoid(dot(taps[...], gate_ref[0].reshape(1280, 256)) + fixed_ref[0, pl.ds(at, TILE), 0:256])
             reset = (gates[:, 128:256] * state).astype(BF16).astype(F32)
             for tap in range(5):
-                col_st[:, tap * 128 : (tap + 1) * 128] = shifted(reset, tap).astype(BF16)
-            candidate = dot(col_st[...], state_ref[0, :, 0:128, :].reshape(640, 128)) + dot(
-                col_in[pl.ds(at, TILE), :], state_ref[0, :, 128:384, :].reshape(1280, 128)
-            )
-            finish(at, gates[:, 0:128], jnp.tanh(candidate + bias[0:1, 256:384]))
-            states[pl.ds(pad + at, TILE), :] = hidden[pl.ds(at, TILE), :].astype(BF16)
+                taps[:, tap * 256 : tap * 256 + 128] = shifted(reset, tap).astype(BF16)
+            if iteration == 0 and count == TILE:
+                ready(1)
+            candidate = jnp.tanh(dot(taps[...], state_ref[0].reshape(1280, 128)) + fixed_ref[0, pl.ds(at, TILE), 256:384])
+            states[pl.ds(pad + at, TILE), :] = finish(at, gates[:, 0:128], candidate).astype(BF16)
+
+        def fill(first, at):
+            for tap in range(5):
+                taps[:, tap * 256 : tap * 256 + 128] = first[pl.ds(at + tap * WIN, TILE), :]
+                taps[:, tap * 256 + 128 : tap * 256 + 256] = motions[pl.ds(at + tap * WIN, TILE), :]
 
         def gate_rows(at):
-            total = None
-            for tap in range(5):
-                part = dot(states[pl.ds(at + tap * WIN, TILE), :], gate_ref[1, tap, 0:128, :]) + dot(
-                    inputs[pl.ds(at + tap * WIN, TILE), :], gate_ref[1, tap, 128:384, :]
-                )
-                total = part if total is None else total + part
-            gates = sigmoid(total + bias[1:2, 0:256])
+            fill(states, at)
+            gates = sigmoid(dot(taps[...], gate_ref[1].reshape(1280, 256)) + fixed_ref[1, pl.ds(at, TILE), 0:256])
             updates[pl.ds(at, TILE), :] = gates[:, 0:128]
             resets[pl.ds(pad + at, TILE), :] = (
                 gates[:, 128:256] * states[pl.ds(pad + at, TILE), :].astype(F32)
             ).astype(BF16)
 
         def state_rows(at):
-            total = None
-            for tap in range(5):
-                part = dot(resets[pl.ds(at + tap * WIN, TILE), :], state_ref[1, tap, 0:128, :]) + dot(
-                    inputs[pl.ds(at + tap * WIN, TILE), :], state_ref[1, tap, 128:384, :]
-                )
-                total = part if total is None else total + part
-            finish(at, updates[pl.ds(at, TILE), :], jnp.tanh(total + bias[1:2, 256:384]))
-            lifted = jnp.maximum(dot(hidden[pl.ds(at, TILE), :].astype(BF16), head_ref[...]), 0.0).astype(BF16)
+            fill(resets, at)
+            candidate = jnp.tanh(dot(taps[...], state_ref[1].reshape(1280, 128)) + fixed_ref[1, pl.ds(at, TILE), 256:384])
+            new = finish(at, updates[pl.ds(at, TILE), :], candidate)
+            lifted = jnp.maximum(dot(new.astype(BF16), head_ref[...]), 0.0).astype(BF16)
             step = dot_nt(delta_ref[...], lifted)
-            flow[:, pl.ds(at, TILE)] = flow[:, pl.ds(at, TILE)] + step
-            flow_cols[pl.ds(at, TILE), :] = flow_cols[pl.ds(at, TILE), :] + step.T
-
-        each(columns_pass)
-        each(gate_rows)
-        each(state_rows)
+            if iteration == 0:
+                flow[:, pl.ds(at, TILE)] = step
+                flow_cols[pl.ds(at, TILE), :] = step.T
+            else:
+                flow[:, pl.ds(at, TILE)] = flow[:, pl.ds(at, TILE)] + step
+
+        if iteration == 0 and count != TILE:
+            ready(0)
+            ready(1)
+        each_tile(count, columns_pass)
+        if iteration == 0:
+            ready(2)
+            ready(3)
+        each_tile(count, gate_rows)
+        each_tile(count, state_rows)
 
     for j in range(dests):
         for r in range(rows_per):
@@ -444,37 +501,38 @@
     padded = columns + half_wide
     room = 16 if dests <= 8 else 56
 
-    shard = frame_two.reshape(1, rows_per, columns, channels)
-    if dests == 8:
-
-        def swap(value, flip):
-            return lax.ppermute(value, "rows", [(i, i ^ flip) for i in range(dests)])
-
-        beside, *others = (swap(shard, flip) for flip in (1, 2, 4, 6))
-    else:
-        beside, others = lax.all_gather(shard, "rows", axis=0, tiled=True), ()
-
     rows_hidden = round_up(cap, 16)
     rows_slot = rows_hidden + round_up(8 * (-(-cap // 128)), 16)
-    slot_target, beside = lax.optimization_barrier((slot_target, beside))
-    packed = call(
+    packed, shard = call(
         functools.partial(pack_kernel, dests, cap, pixels, own, half_wide),
-        jax.ShapeDtypeStruct((dests, rows_slot + rows_per * WIN, hidden_size), BF16),
-        [smem_spec()] + vmem_specs(4),
+        (
+            jax.ShapeDtypeStruct((dests, rows_slot + rows_per * WIN, hidden_size), BF16),
+            jax.ShapeDtypeStruct((1, rows_per, columns, channels), BF16),
+        ),
+        [smem_spec()] + vmem_specs(5),
         [pltpu.VMEM((rows_per, padded, 128), F32)],
         (2 * slots * slots * 128, 1 << 20, 0),
-        room,
+        60,
         slot_count,
         slot_target.reshape(slots // 128, 128),
         carry_flow.T,
         carry_hidden,
         context,
-    )
-    packed, others = lax.optimization_barrier((packed, others))
+        frame_two.reshape(1, rows_per, columns, channels),
+    )
+    if dests == 8:
+
+        def swap(value, flip):
+            return lax.ppermute(value, "rows", [(i, i ^ flip) for i in range(dests)])
+
+        beside, *others = (swap(shard, flip) for flip in (1, 2, 4, 6))
+    else:
+        beside, others = lax.all_gather(shard, "rows", axis=0, tiled=True), ()
+
     early = lax.all_to_all(packed, "rows", 0, 0, tiled=True)
     if others:
         near, across, wrap = others
-        keys = (shard, beside, near, swap(near, 1), across, swap(across, 1), wrap, swap(wrap, 1))
+        keys = (frame_two[None], beside, near, swap(beside, 2), across, swap(across, 1), wrap, swap(beside, 6))
     else:
         keys = (beside,)
     ow = jnp.pad(offset_weight, ((0, 2), (0, 0)))
@@ -493,7 +551,6 @@
         ow,
     )
     queries = frame_one.reshape(pixels, channels)
-    queries, hidden_wide, term = lax.optimization_barrier((queries, hidden_wide, term))
     chunks = dests // 2
     tile = 128
     keep, send = call(
@@ -530,30 +587,52 @@
     arrived = lax.all_to_all(sending, "rows", 0, 0, tiled=True)
     count = dests * rows_per * WIN
     back_rows = rows_per * own + 8
+    hbm = pl.BlockSpec(memory_space=pltpu.HBM)
+    gate_weight = pltpu.with_memory_space_constraint(gate_weight, pltpu.HBM)
+    state_weight = pltpu.with_memory_space_constraint(state_weight, pltpu.HBM)
+    fixed = call(
+        context_kernel,
+        jax.ShapeDtypeStruct((2, count, 384), F32),
+        [vmem_specs(1)[0], hbm, hbm, vmem_specs(1)[0]],
+        [
+            pltpu.VMEM((2, 5, 128, 256), BF16),
+            pltpu.VMEM((2, 5, 128, 128), BF16),
+            pltpu.VMEM((count + 4 * WIN, 128), BF16),
+            pltpu.VMEM((TILE, 640), BF16),
+            pltpu.SemaphoreType.DMA((2,)),
+        ],
+        (4 * count * 5 * 128 * 384, 1 << 22, 0),
+        room,
+        early,
+        gate_weight,
+        state_weight,
+        gru_bias,
+    )
     outgoing = call(
         functools.partial(update_kernel, own, width),
         jax.ShapeDtypeStruct((dests, back_rows, 128), F32),
-        vmem_specs(8),
+        vmem_specs(3) + [hbm, hbm] + vmem_specs(2),
         [
             pltpu.VMEM((count, 128), BF16),
             pltpu.VMEM((count, 128), F32),
-            pltpu.VMEM((count + 4 * WIN, 256), BF16),
+            pltpu.VMEM((count + 4 * WIN, 128), BF16),
             pltpu.VMEM((count + 4 * WIN, 128), BF16),
             pltpu.VMEM((count + 4 * WIN, 128), BF16),
             pltpu.VMEM((count, 128), F32),
-            pltpu.VMEM((count, 1280), BF16),
-            pltpu.VMEM((TILE, 640), BF16),
+            pltpu.VMEM((TILE, 1280), BF16),
             pltpu.VMEM((8, count), F32),
             pltpu.VMEM((count, 8), F32),
+            pltpu.VMEM((2, 5, 256, 256), BF16),
+            pltpu.VMEM((2, 5, 256, 128), BF16),
+            pltpu.SemaphoreType.DMA((8,)),
         ],
-        (16 * count * 5 * 384 * 256, 1 << 22, 8 * count * 384),
+        (8 * count * 5 * 256 * 384, 1 << 22, 8 * count * 384),
         room,
         arrived,
-        early[:, rows_slot:, :],
+        fixed,
         ow,
         gate_weight,
         state_weight,
-        gru_bias,
         head_weight,
         jnp.pad(delta_weight, ((0, 6), (0, 0))),
     )

time: 87 us -> 94.2 us (1.083)
  waiting for transfers between devices: 31 us -> 41.6 us
  local copies, waits for them, and re-layouts: 5.58 us -> 1.09 us
  Pallas kernels: 22.5 us -> 25 us
  starting transfers between devices: 23.3 us -> 22 us
    ppermute x7, waiting for transfers between devices: 2.1 us -> 26.5 us  [swap(): return lax.ppermute(value, 'rows', [(i, i ^ flip) for i in range(dests)])]
    all_to_all x1, waiting for transfers between devices: 10.4 us -> 0.01 us  [local(): early = lax.all_to_all(packed, 'rows', 0, 0, tiled=True)]
    unnamed x27 -> x15, local copies, waits for them, and re-layouts: 4.52 us -> 0.04 us
    ppermute x7, starting transfers between devices: 11.5 us -> 7.47 us  [swap(): return lax.ppermute(value, 'rows', [(i, i ^ flip) for i in range(dests)])]
    all_to_all x1, starting transfers between devices: 3.75 us -> 7.28 us  [local(): early = lax.all_to_all(packed, 'rows', 0, 0, tiled=True)]
    pallas_call x5 -> x6, Pallas kernels: 22.5 us -> 25 us  [call(): pl.pallas_call(kernel, out_shape=out_shape, in_specs=in_specs, out_specs=...]
    all_to_all x1, waiting for transfers between devices: 9.18 us -> 7.27 us  [local(): arrived = lax.all_to_all(sending, 'rows', 0, 0, tiled=True)]
    ppermute x1, waiting for transfers between devices: 1.78 us -> 0.14 us  [local(): lax.ppermute(send, 'loop', [(i, (i + 1) % halves) for i in range(halves)])]
  transfers between devices with their start and end apart: 11 -> 11, of which waited for: 5 -> 7; matrix products, arithmetic and copies ran while one was open for 0% -> 0% of each run, Pallas kernels for 7% -> 10%
where the time goes in v3:
time: 94.2 us; the launch traced here: 93.7 us
  waiting for transfers between devices  41.6 us (44%)
  Pallas kernels  25 us (27%)
  starting transfers between devices  22 us (23%)
  blocking collectives  2.03 us (2%)
  between operations  1.53 us (2%)
  local copies, waits for them, and re-layouts  1.09 us (1%)
    ppermute x7, waiting for transfers between devices, swap(): return lax.ppermute(value, 'rows', [(i, i ^ flip) for i in range(dests)])  26.5 us
    pallas_call x6, Pallas kernels, call(): pl.pallas_call(kernel, out_shape=out_shape, in_specs=in_specs, out_specs=...  25 us
    all_to_all x1, waiting for transfers between devices, local(): back = lax.all_to_all(outgoing, 'rows', 0, 0, tiled=True)  7.67 us
    ppermute x7, starting transfers between devices, swap(): return lax.ppermute(value, 'rows', [(i, i ^ flip) for i in range(dests)])  7.47 us
    all_to_all x1, starting transfers between devices, local(): early = lax.all_to_all(packed, 'rows', 0, 0, tiled=True)  7.28 us
    all_to_all x1, waiting for transfers between devices, local(): arrived = lax.all_to_all(sending, 'rows', 0, 0, tiled=True)  7.27 us
    all_to_all x1, starting transfers between devices, local(): arrived = lax.all_to_all(sending, 'rows', 0, 0, tiled=True)  3.59 us
    all_to_all x1, starting transfers between devices, local(): back = lax.all_to_all(outgoing, 'rows', 0, 0, tiled=True)  3.57 us
  transfers between devices with their start and end apart: 11, of which 7 were waited for; matrix products, arithmetic and copies ran while one was open for 0% of the time, Pallas kernels for 10%

profile of v3, /device:TPU:0, one launch (start us, length us, event | category | flops | bytes accessed | tf_op | source)
XLA Modules:
  0.0 93.7 jit_solution(18413204621839220418)
XLA Ops:
  0.6 0.0 copy-start.3
  0.6 0.0 copy-start.5
  0.7 0.0 copy-start.2
  0.7 0.0 copy-start.1
  1.4 5.3 %shard_map.149 = (bf16[8,272,128]{2,1,0:T(8,128)(2,1)}, bf16[1,2,128,256]{3,2,1,0:T(8,128)(2,1)}) custom-call(s32[1]{0:T(128)S(6)} %copy.23.count_ref, s32[12,128]{1,0:T(8,128)} %bitcast.22, bf16[2,1536]{1,0:T(2,128)(2,1)} %bitcast.23, bf16[1536,128]{1,0:T(8,128)(2,1)} %hidden_ref.1, bf16[2,256,128]{2,1,0:T(8,128)(2,1)} %context_ref.1, ...), custom_call_target="tpu_custom_call" | custom-call | flops 603979776 | bytes 1048576 | tf_op jit(solution)/shard_map/pallas_call | solution.py:52
  6.6 7.3 %all-to-all-start = ((bf16[8,272,128]{2,1,0:T(8,128)(2,1)}), bf16[8,272,128]{2,1,0:T(8,128)(2,1)S(1)}, u32[]{:S(2)}, u32[]{:S(2)}) async-start(bf16[8,272,128]{2,1,0:T(8,128)(2,1)} %get-tuple-element.12), calls=%async_computation | async-start | bytes 1114112 | tf_op jit(solution)/shard_map/all_to_all | solution.py:532
  13.9 2.9 %collective-permute-start.3 = (bf16[1,2,128,256]{3,2,1,0:T(8,128)(2,1)}, bf16[1,2,128,256]{3,2,1,0:T(8,128)(2,1)S(1)}, u32[]{:S(2)}, u32[]{:S(2)}) collective-permute-start(bf16[1,2,128,256]{3,2,1,0:T(8,128)(2,1)} %get-tuple-element.9), channel_id=1, source_target_pairs={{0,8},{2,10},{4,12},{6,14},{8,0},{10,2},{12,4},{14,6},{1,9},{3,11}... | collective-permute-start | bytes 393224 | tf_op jit(solution)/shard_map/ppermute | solution.py:526
  16.8 1.5 %collective-permute-start = (bf16[1,2,128,256]{3,2,1,0:T(8,128)(2,1)}, bf16[1,2,128,256]{3,2,1,0:T(8,128)(2,1)S(1)}, u32[]{:S(2)}, u32[]{:S(2)}) collective-permute-start(bf16[1,2,128,256]{3,2,1,0:T(8,128)(2,1)} %get-tuple-element.9), channel_id=1, source_target_pairs={{0,2},{2,0},{4,6},{6,4},{8,10},{10,8},{12,14},{14,12},{1,3},{3,1},... | collective-permute-start | bytes 393224 | tf_op jit(solution)/shard_map/ppermute | solution.py:526
  18.3 1.5 %collective-permute-start.5 = (bf16[1,2,128,256]{3,2,1,0:T(8,128)(2,1)}, bf16[1,2,128,256]{3,2,1,0:T(8,128)(2,1)S(1)}, u32[]{:S(2)}, u32[]{:S(2)}) collective-permute-start(bf16[1,2,128,256]{3,2,1,0:T(8,128)(2,1)} %get-tuple-element.9), channel_id=1, source_target_pairs={{0,12},{2,14},{4,8},{6,10},{8,4},{10,6},{12,0},{14,2},{1,13},{3,15... | collective-permute-start | bytes 393224 | tf_op jit(solution)/shard_map/ppermute | solution.py:526
  19.8 0.0 collective-permute-start.1
  19.8 19.2 %collective-permute-done.3.refs_4_ = bf16[1,2,128,256]{3,2,1,0:T(8,128)(2,1)S(1)} collective-permute-done((bf16[1,2,128,256]{3,2,1,0:T(8,128)(2,1)}, bf16[1,2,128,256]{3,2,1,0:T(8,128)(2,1)S(1)}, u32[]{:S(2)}, u32[]{:S(2)}) %collective-permute-start.3) | collective-permute-done | bytes 131104 | tf_op jit(solution)/shard_map/ppermute | solution.py:526
  38.9 1.1 %collective-permute-start.4 = (bf16[1,2,128,256]{3,2,1,0:T(8,128)(2,1)S(1)}, bf16[1,2,128,256]{3,2,1,0:T(8,128)(2,1)S(1)}, u32[]{:S(2)}, u32[]{:S(2)}) collective-permute-start(bf16[1,2,128,256]{3,2,1,0:T(8,128)(2,1)S(1)} %collective-permute-done.3.refs_4_), channel_id=1, source_target_pairs={{0,2},{2,0},{4,6},{6,4},{8,10},{10,8},{12,14},{14,12},{1,3},{3,1},... | collective-permute-start | bytes 393224 | tf_op jit(solution)/shard_map/ppermute | solution.py:526
  40.0 0.0 collective-permute-done.refs_1_
  40.1 0.5 collective-permute-start.6
  40.6 0.0 collective-permute-start.2
  40.6 0.0 copy-done.5
  40.6 0.0 collective-permute-done.5.refs_6_
  40.6 0.0 collective-permute-done.1.refs_2_
  40.6 3.3 %collective-permute-done.4.refs_5_ = bf16[1,2,128,256]{3,2,1,0:T(8,128)(2,1)S(1)} collective-permute-done((bf16[1,2,128,256]{3,2,1,0:T(8,128)(2,1)S(1)}, bf16[1,2,128,256]{3,2,1,0:T(8,128)(2,1)S(1)}, u32[]{:S(2)}, u32[]{:S(2)}) %collective-permute-start.4) | collective-permute-done | bytes 131104 | tf_op jit(solution)/shard_map/ppermute | solution.py:526
  43.9 3.0 %collective-permute-done.6.refs_7_ = bf16[1,2,128,256]{3,2,1,0:T(8,128)(2,1)S(1)} collective-permute-done((bf16[1,2,128,256]{3,2,1,0:T(8,128)(2,1)S(1)}, bf16[1,2,128,256]{3,2,1,0:T(8,128)(2,1)S(1)}, u32[]{:S(2)}, u32[]{:S(2)}) %collective-permute-start.6) | collective-permute-done | bytes 131104 | tf_op jit(solution)/shard_map/ppermute | solution.py:526
  46.9 1.0 %collective-permute-done.2.refs_3_ = bf16[1,2,128,256]{3,2,1,0:T(8,128)(2,1)S(1)} collective-permute-done((bf16[1,2,128,256]{3,2,1,0:T(8,128)(2,1)S(1)}, bf16[1,2,128,256]{3,2,1,0:T(8,128)(2,1)S(1)}, u32[]{:S(2)}, u32[]{:S(2)}) %collective-permute-start.2) | collective-permute-done | bytes 131104 | tf_op jit(solution)/shard_map/ppermute | solution.py:526
  47.9 0.0 copy-done.3
  47.9 0.0 copy-done.2
  47.9 0.0 copy-done.1
  47.9 5.5 %shard_map.150 = (f32[2,144,384]{2,1,0:T(8,128)S(1)}, f32[2,144,384]{2,1,0:T(8,128)S(1)}) custom-call(bf16[512,256]{1,0:T(8,128)(2,1)S(1)} %bitcast.14, bf16[512,128]{1,0:T(8,128)(2,1)S(1)} %copy-done.2, f32[8,128]{1,0:T(8,128)S(1)} %pad.8.ow_ref, bf16[1,2,128,256]{3,2,1,0:T(8,128)(2,1)S(1)} %bitcast.16, ...), custom_call_target="tpu_custom_call" | custom-call | flops 1073741824 | bytes 2097152 | tf_op jit(solution)/shard_map/pallas_call | solution.py:52
  53.4 0.0 copy-start.6
  53.4 0.0 copy-start
  53.5 0.1 collective-permute-start.7
  53.5 0.0 all-to-all-done.got_ref.early_ref
  53.5 1.6 %shard_map.151 = (bf16[2,144,128]{2,1,0:T(8,128)(2,1)S(1)}, f32[8,512]{1,0:T(8,128)S(1)}, f32[2,144,128]{2,1,0:T(8,128)S(1)}) custom-call(bf16[8,272,128]{2,1,0:T(8,128)(2,1)S(1)} %all-to-all-done.got_ref.early_ref, f32[8,128]{1,0:T(8,128)S(1)} %pad.8.ow_ref), custom_call_target="tpu_custom_call" | custom-call | flops 201326592 | bytes 1048576 | tf_op jit(solution)/shard_map/pallas_call | solution.py:52
  55.2 0.1 collective-permute-done.7.got_ref
  55.3 0.9 shard_map.152
  56.2 3.6 %all-to-all-start.1 = ((bf16[8,64,256]{2,1,0:T(8,128)(2,1)}), bf16[8,64,256]{2,1,0:T(8,128)(2,1)S(1)}, u32[]{:S(2)}, u32[]{:S(2)}) async-start(bf16[8,64,256]{2,1,0:T(8,128)(2,1)} %shard_map.152), calls=%async_computation.1 | async-start | bytes 524288 | tf_op jit(solution)/shard_map/all_to_all | solution.py:587
  59.8 0.0 copy-done.6
  59.8 0.0 copy-done
  59.8 0.0 copy-start.4
  59.8 2.2 %shard_map.153.fixed_ref = f32[2,512,384]{2,1,0:T(8,128)S(1)} custom-call(bf16[8,272,128]{2,1,0:T(8,128)(2,1)S(1)} %all-to-all-done.got_ref.early_ref, bf16[2,5,384,256]{3,2,1,0:T(8,128)(2,1)} %gate_hbm.3, bf16[2,5,384,128]{3,2,1,0:T(8,128)(2,1)} %state_hbm.3, f32[2,384]{1,0:T(2,128)S(1)} %copy-done), custom_call_target="tpu_custom_call" | custom-call | flops 503316480 | bytes 4194304 | tf_op jit(solution)/shard_map/pallas_call | solution.py:52
  62.1 7.3 %all-to-all-done.1.got_ref = bf16[8,64,256]{2,1,0:T(8,128)(2,1)S(1)} async-done(((bf16[8,64,256]{2,1,0:T(8,128)(2,1)}), bf16[8,64,256]{2,1,0:T(8,128)(2,1)S(1)}, u32[]{:S(2)}, u32[]{:S(2)}) %all-to-all-start.1) | async-done | bytes 262176 | tf_op jit(solution)/shard_map/all_to_all | solution.py:587
  69.3 0.0 copy-done.4
  69.3 9.5 %shard_map.154 = f32[8,40,128]{2,1,0:T(8,128)} custom-call(bf16[8,64,256]{2,1,0:T(8,128)(2,1)S(1)} %all-to-all-done.1.got_ref, f32[2,512,384]{2,1,0:T(8,128)S(1)} %shard_map.153.fixed_ref, f32[8,128]{1,0:T(8,128)S(1)} %pad.8.ow_ref, bf16[2,5,384,256]{3,2,1,0:T(8,128)(2,1)} %gate_hbm.3, bf16[2,5,384,128]{3,2,1,0:T(8,128)(2,1)} %state_hbm.3, ...), custom_call_target="tpu_custom_call" | custom-call | flops 2013265920 | bytes 4194304 | tf_op jit(solution)/shard_map/pallas_call | solution.py:52
  78.8 3.6 %all-to-all-start.2 = ((f32[8,40,128]{2,1,0:T(8,128)}), f32[8,40,128]{2,1,0:T(8,128)S(1)}, u32[]{:S(2)}, u32[]{:S(2)}) async-start(f32[8,40,128]{2,1,0:T(8,128)} %shard_map.154), calls=%async_computation.2 | async-start | bytes 327680 | tf_op jit(solution)/shard_map/all_to_all | solution.py:639
  82.4 7.7 %all-to-all-done.2 = f32[8,40,128]{2,1,0:T(8,128)S(1)} async-done(((f32[8,40,128]{2,1,0:T(8,128)}), f32[8,40,128]{2,1,0:T(8,128)S(1)}, u32[]{:S(2)}, u32[]{:S(2)}) %all-to-all-start.2) | async-done | bytes 163872 | tf_op jit(solution)/shard_map/all_to_all | solution.py:639
  90.1 2.0 %all-gather = f32[16,40,128]{2,1,0:T(8,128)S(1)} all-gather(f32[8,40,128]{2,1,0:T(8,128)S(1)} %all-to-all-done.2), channel_id=2, replica_groups=mesh['groups'=2,'rows'=8,'loop'=2] {'loop'}, dimensions={0}, use_global_device_ids=true | all-gather | bytes 491520 | tf_op jit(solution)/shard_map/all_gather | solution.py:640
  92.1 0.7 copy.18
  92.8 0.1 reshape.31
  92.9 0.1 slice.18
  93.1 0.1 reshape.32
  93.1 0.6 add.7
  (7 shorter events, 0.1 us)
Async XLA Ops:
  0.6 47.3 %copy-start.3 = (bf16[2,128,256]{2,1,0:T(8,128)(2,1)S(1)}, bf16[2,128,256]{2,1,0:T(8,128)(2,1)}, u32[]{:S(2)}) copy-start(bf16[2,128,256]{2,1,0:T(8,128)(2,1)} %param.15) | copy-start | bytes 393220
  0.6 39.9 %copy-start.5 = (f32[6,128]{1,0:T(8,128)S(1)}, f32[6,128]{1,0:T(8,128)}, u32[]{:S(2)}) copy-start(f32[6,128]{1,0:T(8,128)} %param.22) | copy-start | bytes 9220
  0.7 47.2 %copy-start.2 = (bf16[512,128]{1,0:T(8,128)(2,1)S(1)}, bf16[512,128]{1,0:T(8,128)(2,1)}, u32[]{:S(2)}) copy-start(bf16[512,128]{1,0:T(8,128)(2,1)} %weight_ref.1) | copy-start | bytes 393220
  0.7 47.2 %copy-start.1 = (bf16[2,256,256]{2,1,0:T(8,128)(2,1)S(1)}, bf16[2,256,256]{2,1,0:T(8,128)(2,1)}, u32[]{:S(2)}) copy-start(bf16[2,256,256]{2,1,0:T(8,128)(2,1)} %param.14) | copy-start | bytes 786436
  6.6 46.9 %all-to-all-start = ((bf16[8,272,128]{2,1,0:T(8,128)(2,1)}), bf16[8,272,128]{2,1,0:T(8,128)(2,1)S(1)}, u32[]{:S(2)}, u32[]{:S(2)}) async-start(bf16[8,272,128]{2,1,0:T(8,128)(2,1)} %get-tuple-element.12), calls=%async_computation | async-start | bytes 1114112 | tf_op jit(solution)/shard_map/all_to_all | solution.py:532
  13.9 25.0 %collective-permute-start.3 = (bf16[1,2,128,256]{3,2,1,0:T(8,128)(2,1)}, bf16[1,2,128,256]{3,2,1,0:T(8,128)(2,1)S(1)}, u32[]{:S(2)}, u32[]{:S(2)}) collective-permute-start(bf16[1,2,128,256]{3,2,1,0:T(8,128)(2,1)} %get-tuple-element.9), channel_id=1, source_target_pairs={{0,8},{2,10},{4,12},{6,14},{8,0},{10,2},{12,4},{14,6},{1,9},{3,11}... | collective-permute-start | bytes 393224 | tf_op jit(solution)/shard_map/ppermute | solution.py:526
  16.8 23.2 %collective-permute-start = (bf16[1,2,128,256]{3,2,1,0:T(8,128)(2,1)}, bf16[1,2,128,256]{3,2,1,0:T(8,128)(2,1)S(1)}, u32[]{:S(2)}, u32[]{:S(2)}) collective-permute-start(bf16[1,2,128,256]{3,2,1,0:T(8,128)(2,1)} %get-tuple-element.9), channel_id=1, source_target_pairs={{0,2},{2,0},{4,6},{6,4},{8,10},{10,8},{12,14},{14,12},{1,3},{3,1},... | collective-permute-start | bytes 393224 | tf_op jit(solution)/shard_map/ppermute | solution.py:526
  18.3 22.3 %collective-permute-start.5 = (bf16[1,2,128,256]{3,2,1,0:T(8,128)(2,1)}, bf16[1,2,128,256]{3,2,1,0:T(8,128)(2,1)S(1)}, u32[]{:S(2)}, u32[]{:S(2)}) collective-permute-start(bf16[1,2,128,256]{3,2,1,0:T(8,128)(2,1)} %get-tuple-element.9), channel_id=1, source_target_pairs={{0,12},{2,14},{4,8},{6,10},{8,4},{10,6},{12,0},{14,2},{1,13},{3,15... | collective-permute-start | bytes 393224 | tf_op jit(solution)/shard_map/ppermute | solution.py:526
  19.8 20.8 %collective-permute-start.1 = (bf16[1,2,128,256]{3,2,1,0:T(8,128)(2,1)}, bf16[1,2,128,256]{3,2,1,0:T(8,128)(2,1)S(1)}, u32[]{:S(2)}, u32[]{:S(2)}) collective-permute-start(bf16[1,2,128,256]{3,2,1,0:T(8,128)(2,1)} %get-tuple-element.9), channel_id=1, source_target_pairs={{0,4},{2,6},{4,0},{6,2},{8,12},{10,14},{12,8},{14,10},{1,5},{3,7},... | collective-permute-start | bytes 393224 | tf_op jit(solution)/shard_map/ppermute | solution.py:526
  38.9 5.0 %collective-permute-start.4 = (bf16[1,2,128,256]{3,2,1,0:T(8,128)(2,1)S(1)}, bf16[1,2,128,256]{3,2,1,0:T(8,128)(2,1)S(1)}, u32[]{:S(2)}, u32[]{:S(2)}) collective-permute-start(bf16[1,2,128,256]{3,2,1,0:T(8,128)(2,1)S(1)} %collective-permute-done.3.refs_4_), channel_id=1, source_target_pairs={{0,2},{2,0},{4,6},{6,4},{8,10},{10,8},{12,14},{14,12},{1,3},{3,1},... | collective-permute-start | bytes 393224 | tf_op jit(solution)/shard_map/ppermute | solution.py:526
  40.1 6.9 %collective-permute-start.6 = (bf16[1,2,128,256]{3,2,1,0:T(8,128)(2,1)S(1)}, bf16[1,2,128,256]{3,2,1,0:T(8,128)(2,1)S(1)}, u32[]{:S(2)}, u32[]{:S(2)}) collective-permute-start(bf16[1,2,128,256]{3,2,1,0:T(8,128)(2,1)S(1)} %collective-permute-done.refs_1_), channel_id=1, source_target_pairs={{0,12},{2,14},{4,8},{6,10},{8,4},{10,6},{12,0},{14,2},{1,13},{3,15... | collective-permute-start | bytes 393224 | tf_op jit(solution)/shard_map/ppermute | solution.py:526
  40.6 7.3 %collective-permute-start.2 = (bf16[1,2,128,256]{3,2,1,0:T(8,128)(2,1)S(1)}, bf16[1,2,128,256]{3,2,1,0:T(8,128)(2,1)S(1)}, u32[]{:S(2)}, u32[]{:S(2)}) collective-permute-start(bf16[1,2,128,256]{3,2,1,0:T(8,128)(2,1)S(1)} %collective-permute-done.refs_1_), channel_id=1, source_target_pairs={{0,4},{2,6},{4,0},{6,2},{8,12},{10,14},{12,8},{14,10},{1,5},{3,7},... | collective-permute-start | bytes 393224 | tf_op jit(solution)/shard_map/ppermute | solution.py:526
  53.4 6.4 %copy-start.6 = (bf16[2,256]{1,0:T(2,128)(2,1)S(1)}, bf16[2,256]{1,0:T(2,128)(2,1)}, u32[]{:S(2)}) copy-start(bf16[2,256]{1,0:T(2,128)(2,1)} %param.27) | copy-start | bytes 3076
  53.4 6.4 %copy-start = (f32[2,384]{1,0:T(2,128)S(1)}, f32[2,384]{1,0:T(2,128)}, u32[]{:S(2)}) copy-start(f32[2,384]{1,0:T(2,128)} %bias_ref.1) | copy-start | bytes 9220
  53.5 1.9 %collective-permute-start.7 = (f32[2,144,384]{2,1,0:T(8,128)S(1)}, f32[2,144,384]{2,1,0:T(8,128)S(1)}, u32[]{:S(2)}, u32[]{:S(2)}) collective-permute-start(f32[2,144,384]{2,1,0:T(8,128)S(1)} %get-tuple-element.11), channel_id=1, source_target_pairs={{0,1},{1,0},{2,3},{3,2},{4,5},{5,4},{6,7},{7,6},{8,9},{9,8},{10,11... | collective-permute-start | bytes 1327112 | tf_op jit(solution)/shard_map/ppermute | solution.py:574
  56.2 13.1 %all-to-all-start.1 = ((bf16[8,64,256]{2,1,0:T(8,128)(2,1)}), bf16[8,64,256]{2,1,0:T(8,128)(2,1)S(1)}, u32[]{:S(2)}, u32[]{:S(2)}) async-start(bf16[8,64,256]{2,1,0:T(8,128)(2,1)} %shard_map.152), calls=%async_computation.1 | async-start | bytes 524288 | tf_op jit(solution)/shard_map/all_to_all | solution.py:587
  59.8 9.5 %copy-start.4 = (bf16[128,256]{1,0:T(8,128)(2,1)S(1)}, bf16[128,256]{1,0:T(8,128)(2,1)}, u32[]{:S(2)}) copy-start(bf16[128,256]{1,0:T(8,128)(2,1)} %head_ref.1) | copy-start | bytes 196612
  78.8 11.3 %all-to-all-start.2 = ((f32[8,40,128]{2,1,0:T(8,128)}), f32[8,40,128]{2,1,0:T(8,128)S(1)}, u32[]{:S(2)}, u32[]{:S(2)}) async-start(f32[8,40,128]{2,1,0:T(8,128)} %shard_map.154), calls=%async_computation.2 | async-start | bytes 327680 | tf_op jit(solution)/shard_map/all_to_all | solution.py:639

commit v4 on v3

--- a/solution.py
+++ b/solution.py
@@ -60,8 +60,7 @@
     )(*args)
 
 
-def pack_kernel(dests, cap, pixels, own, half_wide, count_ref, target_ref, flow_ref, hidden_ref, context_ref, shard_ref, out_ref, pass_ref, wide):
-    pass_ref[...] = shard_ref[...]
+def pack_kernel(dests, cap, pixels, own, half_wide, count_ref, target_ref, flow_ref, hidden_ref, context_ref, out_ref, wide):
     slots = hidden_ref.shape[0]
     target = jnp.concatenate([target_ref[k : k + 1, :] for k in range(slots // 128)], axis=1)
     counted = iota((1, slots), 1) < count_ref[0]
@@ -503,13 +502,21 @@
 
     rows_hidden = round_up(cap, 16)
     rows_slot = rows_hidden + round_up(8 * (-(-cap // 128)), 16)
-    packed, shard = call(
+    shard = frame_two.reshape(1, rows_per, columns, channels)
+    if dests == 8:
+
+        def swap(value, flip):
+            return lax.ppermute(value, "rows", [(i, i ^ flip) for i in range(dests)])
+
+        beside, near, wrap, across = (swap(shard, flip) for flip in (1, 2, 6, 4))
+        near_beside, wrap_beside = (swap(beside, flip) for flip in (2, 6))
+    else:
+        beside = lax.all_gather(shard, "rows", axis=0, tiled=True)
+    slot_target, beside = lax.optimization_barrier((slot_target, beside))
+    packed = call(
         functools.partial(pack_kernel, dests, cap, pixels, own, half_wide),
-        (
-            jax.ShapeDtypeStruct((dests, rows_slot + rows_per * WIN, hidden_size), BF16),
-            jax.ShapeDtypeStruct((1, rows_per, columns, channels), BF16),
-        ),
-        [smem_spec()] + vmem_specs(5),
+        jax.ShapeDtypeStruct((dests, rows_slot + rows_per * WIN, hidden_size), BF16),
+        [smem_spec()] + vmem_specs(4),
         [pltpu.VMEM((rows_per, padded, 128), F32)],
         (2 * slots * slots * 128, 1 << 20, 0),
         60,
@@ -518,23 +525,15 @@
         carry_flow.T,
         carry_hidden,
         context,
-        frame_two.reshape(1, rows_per, columns, channels),
     )
     if dests == 8:
-
-        def swap(value, flip):
-            return lax.ppermute(value, "rows", [(i, i ^ flip) for i in range(dests)])
-
-        beside, *others = (swap(shard, flip) for flip in (1, 2, 4, 6))
-    else:
-        beside, others = lax.all_gather(shard, "rows", axis=0, tiled=True), ()
-
-    early = lax.all_to_all(packed, "rows", 0, 0, tiled=True)
-    if others:
-        near, across, wrap = others
-        keys = (frame_two[None], beside, near, swap(beside, 2), across, swap(across, 1), wrap, swap(beside, 6))
+        packed, near, wrap, across, near_beside, wrap_beside = lax.optimization_barrier(
+            (packed, near, wrap, across, near_beside, wrap_beside)
+        )
+        keys = (shard, beside, near, near_beside, across, swap(across, 1), wrap, wrap_beside)
     else:
         keys = (beside,)
+    early = lax.all_to_all(packed, "rows", 0, 0, tiled=True)
     ow = jnp.pad(offset_weight, ((0, 2), (0, 0)))
     hidden_wide, flow_first, term = call(
         functools.partial(place_kernel, cap, half_wide, rows_per),

time: 94.2 us -> 86.2 us (0.915)
  waiting for transfers between devices: 41.6 us -> 28 us
  starting transfers between devices: 22 us -> 27.6 us
    ppermute x7, waiting for transfers between devices: 26.5 us -> 13.1 us  [swap(): return lax.ppermute(value, 'rows', [(i, i ^ flip) for i in range(dests)])]
    ppermute x7, starting transfers between devices: 7.47 us -> 12.6 us  [swap(): return lax.ppermute(value, 'rows', [(i, i ^ flip) for i in range(dests)])]
    all_to_all x1, starting transfers between devices: 3.59 us -> 6.04 us  [local(): arrived = lax.all_to_all(sending, 'rows', 0, 0, tiled=True)]
    all_to_all x1, starting transfers between devices: 7.28 us -> 5.31 us  [local(): early = lax.all_to_all(packed, 'rows', 0, 0, tiled=True)]
  transfers between devices with their start and end apart: 11 -> 11, of which waited for: 7 -> 7; matrix products, arithmetic and copies ran while one was open for 0% -> 0% of each run, Pallas kernels for 10% -> 17%
where the time goes in v4:
time: 86.2 us; the launch traced here: 85.7 us
  waiting for transfers between devices  28 us (32%)
  starting transfers between devices  27.6 us (32%)
  Pallas kernels  24.9 us (29%)
  blocking collectives  2.03 us (2%)
  between operations  1.46 us (2%)
  local copies, waits for them, and re-layouts  1.09 us (1%)
    pallas_call x6, Pallas kernels, call(): pl.pallas_call(kernel, out_shape=out_shape, in_specs=in_specs, out_specs=...  24.9 us
    ppermute x7, waiting for transfers between devices, swap(): return lax.ppermute(value, 'rows', [(i, i ^ flip) for i in range(dests)])  13.1 us
    ppermute x7, starting transfers between devices, swap(): return lax.ppermute(value, 'rows', [(i, i ^ flip) for i in range(dests)])  12.6 us
    all_to_all x1, waiting for transfers between devices, local(): back = lax.all_to_all(outgoing, 'rows', 0, 0, tiled=True)  7.61 us
    all_to_all x1, waiting for transfers between devices, local(): arrived = lax.all_to_all(sending, 'rows', 0, 0, tiled=True)  7.23 us
    all_to_all x1, starting transfers between devices, local(): arrived = lax.all_to_all(sending, 'rows', 0, 0, tiled=True)  6.04 us
    all_to_all x1, starting transfers between devices, local(): early = lax.all_to_all(packed, 'rows', 0, 0, tiled=True)  5.31 us
    all_to_all x1, starting transfers between devices, local(): back = lax.all_to_all(outgoing, 'rows', 0, 0, tiled=True)  3.6 us
  transfers between devices with their start and end apart: 11, of which 7 were waited for; matrix products, arithmetic and copies ran while one was open for 0% of the time, Pallas kernels for 17%

profile of v4, /device:TPU:0, one launch (start us, length us, event | category | flops | bytes accessed | tf_op | source)
XLA Modules:
  0.0 85.7 jit_solution(7198429556638183152)
XLA Ops:
  0.6 0.0 copy-start.3
  0.6 0.0 copy-start.5
  0.7 0.0 copy-start.2
  0.7 0.0 copy-start.1
  0.7 3.0 %collective-permute-start = (bf16[1,2,128,256]{3,2,1,0:T(8,128)(2,1)}, bf16[1,2,128,256]{3,2,1,0:T(8,128)(2,1)S(1)}, u32[]{:S(2)}, u32[]{:S(2)}) collective-permute-start(bf16[1,2,128,256]{3,2,1,0:T(8,128)(2,1)} %bitcast.15), channel_id=1, source_target_pairs={{0,2},{2,0},{4,6},{6,4},{8,10},{10,8},{12,14},{14,12},{1,3},{3,1},... | collective-permute-start | bytes 393224 | tf_op jit(solution)/shard_map/ppermute | solution.py:509
  3.7 2.6 %collective-permute-start.3 = (bf16[1,2,128,256]{3,2,1,0:T(8,128)(2,1)}, bf16[1,2,128,256]{3,2,1,0:T(8,128)(2,1)S(1)}, u32[]{:S(2)}, u32[]{:S(2)}) collective-permute-start(bf16[1,2,128,256]{3,2,1,0:T(8,128)(2,1)} %bitcast.16), channel_id=1, source_target_pairs={{0,8},{2,10},{4,12},{6,14},{8,0},{10,2},{12,4},{14,6},{1,9},{3,11}... | collective-permute-start | bytes 393224 | tf_op jit(solution)/shard_map/ppermute | solution.py:509
  6.3 1.3 %collective-permute-start.2 = (bf16[1,2,128,256]{3,2,1,0:T(8,128)(2,1)}, bf16[1,2,128,256]{3,2,1,0:T(8,128)(2,1)S(1)}, u32[]{:S(2)}, u32[]{:S(2)}) collective-permute-start(bf16[1,2,128,256]{3,2,1,0:T(8,128)(2,1)} %bitcast.17), channel_id=1, source_target_pairs={{0,12},{2,14},{4,8},{6,10},{8,4},{10,6},{12,0},{14,2},{1,13},{3,15... | collective-permute-start | bytes 393224 | tf_op jit(solution)/shard_map/ppermute | solution.py:509
  7.6 0.2 collective-permute-start.1
  7.9 0.0 collective-permute-done.refs_1_
  7.9 3.4 %collective-permute-start.5 = (bf16[1,2,128,256]{3,2,1,0:T(8,128)(2,1)S(1)}, bf16[1,2,128,256]{3,2,1,0:T(8,128)(2,1)S(1)}, u32[]{:S(2)}, u32[]{:S(2)}) collective-permute-start(bf16[1,2,128,256]{3,2,1,0:T(8,128)(2,1)S(1)} %collective-permute-done.refs_1_), channel_id=1, source_target_pairs={{0,12},{2,14},{4,8},{6,10},{8,4},{10,6},{12,0},{14,2},{1,13},{3,15... | collective-permute-start | bytes 393224 | tf_op jit(solution)/shard_map/ppermute | solution.py:509
  11.2 0.0 collective-permute-start.4
  11.9 5.2 %shard_map.149 = bf16[8,272,128]{2,1,0:T(8,128)(2,1)} custom-call(s32[1]{0:T(128)S(6)} %copy.23.count_ref, s32[12,128]{1,0:T(8,128)} %bitcast.25, bf16[2,1536]{1,0:T(2,128)(2,1)} %bitcast.26, bf16[1536,128]{1,0:T(8,128)(2,1)} %hidden_ref.1, bf16[2,256,128]{2,1,0:T(8,128)(2,1)} %context_ref.1), custom_call_target="tpu_custom_call" | custom-call | flops 603979776 | bytes 1048576 | tf_op jit(solution)/shard_map/pallas_call | solution.py:52
  17.1 1.4 %collective-permute-done.3.refs_4_ = bf16[1,2,128,256]{3,2,1,0:T(8,128)(2,1)S(1)} collective-permute-done((bf16[1,2,128,256]{3,2,1,0:T(8,128)(2,1)}, bf16[1,2,128,256]{3,2,1,0:T(8,128)(2,1)S(1)}, u32[]{:S(2)}, u32[]{:S(2)}) %collective-permute-start.3) | collective-permute-done | bytes 131104 | tf_op jit(solution)/shard_map/ppermute | solution.py:509
  18.5 0.0 collective-permute-done.2.refs_6_
  18.5 2.4 %collective-permute-done.1.refs_2_ = bf16[1,2,128,256]{3,2,1,0:T(8,128)(2,1)S(1)} collective-permute-done((bf16[1,2,128,256]{3,2,1,0:T(8,128)(2,1)}, bf16[1,2,128,256]{3,2,1,0:T(8,128)(2,1)S(1)}, u32[]{:S(2)}, u32[]{:S(2)}) %collective-permute-start.1) | collective-permute-done | bytes 131104 | tf_op jit(solution)/shard_map/ppermute | solution.py:509
  20.9 0.0 collective-permute-done.5.refs_7_
  20.9 1.5 %collective-permute-done.4.refs_3_ = bf16[1,2,128,256]{3,2,1,0:T(8,128)(2,1)S(1)} collective-permute-done((bf16[1,2,128,256]{3,2,1,0:T(8,128)(2,1)S(1)}, bf16[1,2,128,256]{3,2,1,0:T(8,128)(2,1)S(1)}, u32[]{:S(2)}, u32[]{:S(2)}) %collective-permute-start.4) | collective-permute-done | bytes 131104 | tf_op jit(solution)/shard_map/ppermute | solution.py:509
  22.4 5.3 %all-to-all-start = ((bf16[8,272,128]{2,1,0:T(8,128)(2,1)}), bf16[8,272,128]{2,1,0:T(8,128)(2,1)S(1)}, u32[]{:S(2)}, u32[]{:S(2)}) async-start(bf16[8,272,128]{2,1,0:T(8,128)(2,1)} %shard_map.149), calls=%async_computation | async-start | bytes 1114112 | tf_op jit(solution)/shard_map/all_to_all | solution.py:536
  27.7 2.0 %collective-permute-start.6 = (bf16[1,2,128,256]{3,2,1,0:T(8,128)(2,1)S(1)}, bf16[1,2,128,256]{3,2,1,0:T(8,128)(2,1)S(1)}, u32[]{:S(2)}, u32[]{:S(2)}) collective-permute-start(bf16[1,2,128,256]{3,2,1,0:T(8,128)(2,1)S(1)} %collective-permute-done.3.refs_4_), channel_id=1, source_target_pairs={{0,2},{2,0},{4,6},{6,4},{8,10},{10,8},{12,14},{14,12},{1,3},{3,1},... | collective-permute-start | bytes 393224 | tf_op jit(solution)/shard_map/ppermute | solution.py:509
  29.7 0.0 copy-done.5
  29.7 7.8 %collective-permute-done.6.refs_5_ = bf16[1,2,128,256]{3,2,1,0:T(8,128)(2,1)S(1)} collective-permute-done((bf16[1,2,128,256]{3,2,1,0:T(8,128)(2,1)S(1)}, bf16[1,2,128,256]{3,2,1,0:T(8,128)(2,1)S(1)}, u32[]{:S(2)}, u32[]{:S(2)}) %collective-permute-start.6) | collective-permute-done | bytes 131104 | tf_op jit(solution)/shard_map/ppermute | solution.py:509
  37.5 0.0 copy-done.3
  37.5 0.0 copy-done.2
  37.5 0.0 copy-done.1
  37.5 5.5 %shard_map.150 = (f32[2,144,384]{2,1,0:T(8,128)S(1)}, f32[2,144,384]{2,1,0:T(8,128)S(1)}) custom-call(bf16[512,256]{1,0:T(8,128)(2,1)S(1)} %bitcast.14, bf16[512,128]{1,0:T(8,128)(2,1)S(1)} %copy-done.2, f32[8,128]{1,0:T(8,128)S(1)} %pad.8.ow_ref, bf16[1,2,128,256]{3,2,1,0:T(8,128)(2,1)S(1)} %bitcast.19, ...), custom_call_target="tpu_custom_call" | custom-call | flops 1073741824 | bytes 2097152 | tf_op jit(solution)/shard_map/pallas_call | solution.py:52
  43.0 0.0 copy-start.6
  43.1 0.0 copy-start
  43.1 0.1 collective-permute-start.7
  43.1 0.0 all-to-all-done.got_ref.early_ref
  43.2 1.6 %shard_map.151 = (bf16[2,144,128]{2,1,0:T(8,128)(2,1)S(1)}, f32[8,512]{1,0:T(8,128)S(1)}, f32[2,144,128]{2,1,0:T(8,128)S(1)}) custom-call(bf16[8,272,128]{2,1,0:T(8,128)(2,1)S(1)} %all-to-all-done.got_ref.early_ref, f32[8,128]{1,0:T(8,128)S(1)} %pad.8.ow_ref), custom_call_target="tpu_custom_call" | custom-call | flops 201326592 | bytes 1048576 | tf_op jit(solution)/shard_map/pallas_call | solution.py:52
  44.8 0.1 collective-permute-done.7.got_ref
  44.9 0.9 %shard_map.152 = bf16[8,64,256]{2,1,0:T(8,128)(2,1)} custom-call(f32[2,144,384]{2,1,0:T(8,128)S(1)} %get-tuple-element.22.keep_ref, f32[2,144,384]{2,1,0:T(8,128)S(1)} %collective-permute-done.7.got_ref, f32[2,144,128]{2,1,0:T(8,128)S(1)} %get-tuple-element.25.term_ref, bf16[2,144,128]{2,1,0:T(8,128)(2,1)S(1)} %get-tuple-element.26.hidden_ref), custom_call_target="tpu_custom_call" | custom-call | bytes 1048576 | tf_op jit(solution)/shard_map/pallas_call | solution.py:52
  45.8 6.0 %all-to-all-start.1 = ((bf16[8,64,256]{2,1,0:T(8,128)(2,1)}), bf16[8,64,256]{2,1,0:T(8,128)(2,1)S(1)}, u32[]{:S(2)}, u32[]{:S(2)}) async-start(bf16[8,64,256]{2,1,0:T(8,128)(2,1)} %shard_map.152), calls=%async_computation.1 | async-start | bytes 524288 | tf_op jit(solution)/shard_map/all_to_all | solution.py:586
  51.8 0.0 copy-done.6
  51.9 0.0 copy-done
  51.9 0.0 copy-start.4
  51.9 2.2 %shard_map.153.fixed_ref = f32[2,512,384]{2,1,0:T(8,128)S(1)} custom-call(bf16[8,272,128]{2,1,0:T(8,128)(2,1)S(1)} %all-to-all-done.got_ref.early_ref, bf16[2,5,384,256]{3,2,1,0:T(8,128)(2,1)} %gate_hbm.3, bf16[2,5,384,128]{3,2,1,0:T(8,128)(2,1)} %state_hbm.3, f32[2,384]{1,0:T(2,128)S(1)} %copy-done), custom_call_target="tpu_custom_call" | custom-call | flops 503316480 | bytes 4194304 | tf_op jit(solution)/shard_map/pallas_call | solution.py:52
  54.1 7.2 %all-to-all-done.1.got_ref = bf16[8,64,256]{2,1,0:T(8,128)(2,1)S(1)} async-done(((bf16[8,64,256]{2,1,0:T(8,128)(2,1)}), bf16[8,64,256]{2,1,0:T(8,128)(2,1)S(1)}, u32[]{:S(2)}, u32[]{:S(2)}) %all-to-all-start.1) | async-done | bytes 262176 | tf_op jit(solution)/shard_map/all_to_all | solution.py:586
  61.3 0.0 copy-done.4
  61.3 9.5 %shard_map.154 = f32[8,40,128]{2,1,0:T(8,128)} custom-call(bf16[8,64,256]{2,1,0:T(8,128)(2,1)S(1)} %all-to-all-done.1.got_ref, f32[2,512,384]{2,1,0:T(8,128)S(1)} %shard_map.153.fixed_ref, f32[8,128]{1,0:T(8,128)S(1)} %pad.8.ow_ref, bf16[2,5,384,256]{3,2,1,0:T(8,128)(2,1)} %gate_hbm.3, bf16[2,5,384,128]{3,2,1,0:T(8,128)(2,1)} %state_hbm.3, ...), custom_call_target="tpu_custom_call" | custom-call | flops 2013265920 | bytes 4194304 | tf_op jit(solution)/shard_map/pallas_call | solution.py:52
  70.8 3.6 %all-to-all-start.2 = ((f32[8,40,128]{2,1,0:T(8,128)}), f32[8,40,128]{2,1,0:T(8,128)S(1)}, u32[]{:S(2)}, u32[]{:S(2)}) async-start(f32[8,40,128]{2,1,0:T(8,128)} %shard_map.154), calls=%async_computation.2 | async-start | bytes 327680 | tf_op jit(solution)/shard_map/all_to_all | solution.py:638
  74.4 7.6 %all-to-all-done.2 = f32[8,40,128]{2,1,0:T(8,128)S(1)} async-done(((f32[8,40,128]{2,1,0:T(8,128)}), f32[8,40,128]{2,1,0:T(8,128)S(1)}, u32[]{:S(2)}, u32[]{:S(2)}) %all-to-all-start.2) | async-done | bytes 163872 | tf_op jit(solution)/shard_map/all_to_all | solution.py:638
  82.0 2.0 %all-gather = f32[16,40,128]{2,1,0:T(8,128)S(1)} all-gather(f32[8,40,128]{2,1,0:T(8,128)S(1)} %all-to-all-done.2), channel_id=2, replica_groups=mesh['groups'=2,'rows'=8,'loop'=2] {'loop'}, dimensions={0}, use_global_device_ids=true | all-gather | bytes 491520 | tf_op jit(solution)/shard_map/all_gather | solution.py:639
  84.1 0.7 copy.18
  84.8 0.1 reshape.34
  84.9 0.1 slice.18
  85.0 0.1 reshape.35
  85.1 0.6 add.7
  (7 shorter events, 0.1 us)
Async XLA Ops:
  0.6 36.9 %copy-start.3 = (bf16[2,128,256]{2,1,0:T(8,128)(2,1)S(1)}, bf16[2,128,256]{2,1,0:T(8,128)(2,1)}, u32[]{:S(2)}) copy-start(bf16[2,128,256]{2,1,0:T(8,128)(2,1)} %param.15) | copy-start | bytes 393220
  0.6 29.1 %copy-start.5 = (f32[6,128]{1,0:T(8,128)S(1)}, f32[6,128]{1,0:T(8,128)}, u32[]{:S(2)}) copy-start(f32[6,128]{1,0:T(8,128)} %param.22) | copy-start | bytes 9220
  0.7 36.9 %copy-start.2 = (bf16[512,128]{1,0:T(8,128)(2,1)S(1)}, bf16[512,128]{1,0:T(8,128)(2,1)}, u32[]{:S(2)}) copy-start(bf16[512,128]{1,0:T(8,128)(2,1)} %weight_ref.1) | copy-start | bytes 393220
  0.7 36.9 %copy-start.1 = (bf16[2,256,256]{2,1,0:T(8,128)(2,1)S(1)}, bf16[2,256,256]{2,1,0:T(8,128)(2,1)}, u32[]{:S(2)}) copy-start(bf16[2,256,256]{2,1,0:T(8,128)(2,1)} %param.14) | copy-start | bytes 786436
  0.7 7.2 %collective-permute-start = (bf16[1,2,128,256]{3,2,1,0:T(8,128)(2,1)}, bf16[1,2,128,256]{3,2,1,0:T(8,128)(2,1)S(1)}, u32[]{:S(2)}, u32[]{:S(2)}) collective-permute-start(bf16[1,2,128,256]{3,2,1,0:T(8,128)(2,1)} %bitcast.15), channel_id=1, source_target_pairs={{0,2},{2,0},{4,6},{6,4},{8,10},{10,8},{12,14},{14,12},{1,3},{3,1},... | collective-permute-start | bytes 393224 | tf_op jit(solution)/shard_map/ppermute | solution.py:509
  3.7 14.7 %collective-permute-start.3 = (bf16[1,2,128,256]{3,2,1,0:T(8,128)(2,1)}, bf16[1,2,128,256]{3,2,1,0:T(8,128)(2,1)S(1)}, u32[]{:S(2)}, u32[]{:S(2)}) collective-permute-start(bf16[1,2,128,256]{3,2,1,0:T(8,128)(2,1)} %bitcast.16), channel_id=1, source_target_pairs={{0,8},{2,10},{4,12},{6,14},{8,0},{10,2},{12,4},{14,6},{1,9},{3,11}... | collective-permute-start | bytes 393224 | tf_op jit(solution)/shard_map/ppermute | solution.py:509
  6.3 12.2 %collective-permute-start.2 = (bf16[1,2,128,256]{3,2,1,0:T(8,128)(2,1)}, bf16[1,2,128,256]{3,2,1,0:T(8,128)(2,1)S(1)}, u32[]{:S(2)}, u32[]{:S(2)}) collective-permute-start(bf16[1,2,128,256]{3,2,1,0:T(8,128)(2,1)} %bitcast.17), channel_id=1, source_target_pairs={{0,12},{2,14},{4,8},{6,10},{8,4},{10,6},{12,0},{14,2},{1,13},{3,15... | collective-permute-start | bytes 393224 | tf_op jit(solution)/shard_map/ppermute | solution.py:509
  7.6 13.2 %collective-permute-start.1 = (bf16[1,2,128,256]{3,2,1,0:T(8,128)(2,1)}, bf16[1,2,128,256]{3,2,1,0:T(8,128)(2,1)S(1)}, u32[]{:S(2)}, u32[]{:S(2)}) collective-permute-start(bf16[1,2,128,256]{3,2,1,0:T(8,128)(2,1)} %bitcast.18), channel_id=1, source_target_pairs={{0,4},{2,6},{4,0},{6,2},{8,12},{10,14},{12,8},{14,10},{1,5},{3,7},... | collective-permute-start | bytes 393224 | tf_op jit(solution)/shard_map/ppermute | solution.py:509
  7.9 13.0 %collective-permute-start.5 = (bf16[1,2,128,256]{3,2,1,0:T(8,128)(2,1)S(1)}, bf16[1,2,128,256]{3,2,1,0:T(8,128)(2,1)S(1)}, u32[]{:S(2)}, u32[]{:S(2)}) collective-permute-start(bf16[1,2,128,256]{3,2,1,0:T(8,128)(2,1)S(1)} %collective-permute-done.refs_1_), channel_id=1, source_target_pairs={{0,12},{2,14},{4,8},{6,10},{8,4},{10,6},{12,0},{14,2},{1,13},{3,15... | collective-permute-start | bytes 393224 | tf_op jit(solution)/shard_map/ppermute | solution.py:509
  11.2 11.1 %collective-permute-start.4 = (bf16[1,2,128,256]{3,2,1,0:T(8,128)(2,1)S(1)}, bf16[1,2,128,256]{3,2,1,0:T(8,128)(2,1)S(1)}, u32[]{:S(2)}, u32[]{:S(2)}) collective-permute-start(bf16[1,2,128,256]{3,2,1,0:T(8,128)(2,1)S(1)} %collective-permute-done.refs_1_), channel_id=1, source_target_pairs={{0,4},{2,6},{4,0},{6,2},{8,12},{10,14},{12,8},{14,10},{1,5},{3,7},... | collective-permute-start | bytes 393224 | tf_op jit(solution)/shard_map/ppermute | solution.py:509
  22.4 20.8 %all-to-all-start = ((bf16[8,272,128]{2,1,0:T(8,128)(2,1)}), bf16[8,272,128]{2,1,0:T(8,128)(2,1)S(1)}, u32[]{:S(2)}, u32[]{:S(2)}) async-start(bf16[8,272,128]{2,1,0:T(8,128)(2,1)} %shard_map.149), calls=%async_computation | async-start | bytes 1114112 | tf_op jit(solution)/shard_map/all_to_all | solution.py:536
  27.7 9.8 %collective-permute-start.6 = (bf16[1,2,128,256]{3,2,1,0:T(8,128)(2,1)S(1)}, bf16[1,2,128,256]{3,2,1,0:T(8,128)(2,1)S(1)}, u32[]{:S(2)}, u32[]{:S(2)}) collective-permute-start(bf16[1,2,128,256]{3,2,1,0:T(8,128)(2,1)S(1)} %collective-permute-done.3.refs_4_), channel_id=1, source_target_pairs={{0,2},{2,0},{4,6},{6,4},{8,10},{10,8},{12,14},{14,12},{1,3},{3,1},... | collective-permute-start | bytes 393224 | tf_op jit(solution)/shard_map/ppermute | solution.py:509
  43.0 8.8 %copy-start.6 = (bf16[2,256]{1,0:T(2,128)(2,1)S(1)}, bf16[2,256]{1,0:T(2,128)(2,1)}, u32[]{:S(2)}) copy-start(bf16[2,256]{1,0:T(2,128)(2,1)} %param.27) | copy-start | bytes 3076
  43.1 8.8 %copy-start = (f32[2,384]{1,0:T(2,128)S(1)}, f32[2,384]{1,0:T(2,128)}, u32[]{:S(2)}) copy-start(f32[2,384]{1,0:T(2,128)} %bias_ref.1) | copy-start | bytes 9220
  43.1 1.9 %collective-permute-start.7 = (f32[2,144,384]{2,1,0:T(8,128)S(1)}, f32[2,144,384]{2,1,0:T(8,128)S(1)}, u32[]{:S(2)}, u32[]{:S(2)}) collective-permute-start(f32[2,144,384]{2,1,0:T(8,128)S(1)} %get-tuple-element.23), channel_id=1, source_target_pairs={{0,1},{1,0},{2,3},{3,2},{4,5},{5,4},{6,7},{7,6},{8,9},{9,8},{10,11... | collective-permute-start | bytes 1327112 | tf_op jit(solution)/shard_map/ppermute | solution.py:573
  45.8 15.5 %all-to-all-start.1 = ((bf16[8,64,256]{2,1,0:T(8,128)(2,1)}), bf16[8,64,256]{2,1,0:T(8,128)(2,1)S(1)}, u32[]{:S(2)}, u32[]{:S(2)}) async-start(bf16[8,64,256]{2,1,0:T(8,128)(2,1)} %shard_map.152), calls=%async_computation.1 | async-start | bytes 524288 | tf_op jit(solution)/shard_map/all_to_all | solution.py:586
  51.9 9.5 %copy-start.4 = (bf16[128,256]{1,0:T(8,128)(2,1)S(1)}, bf16[128,256]{1,0:T(8,128)(2,1)}, u32[]{:S(2)}) copy-start(bf16[128,256]{1,0:T(8,128)(2,1)} %head_ref.1) | copy-start | bytes 196612
  70.8 11.2 %all-to-all-start.2 = ((f32[8,40,128]{2,1,0:T(8,128)}), f32[8,40,128]{2,1,0:T(8,128)S(1)}, u32[]{:S(2)}, u32[]{:S(2)}) async-start(f32[8,40,128]{2,1,0:T(8,128)} %shard_map.154), calls=%async_computation.2 | async-start | bytes 327680 | tf_op jit(solution)/shard_map/all_to_all | solution.py:638

commit v5 on v4

--- a/solution.py
+++ b/solution.py
@@ -75,11 +75,13 @@
         running = dot(member[:, start : start + 128].astype(BF16), upper) + before
         before = running[:, 127:128]
         ranks.append(running)
-    rank = jnp.concatenate(ranks, axis=1) - 1.0
+    rank = jnp.concatenate(ranks, axis=1) - 1.0 - (lax.axis_index("loop") * cap).astype(F32)
+    belongs = belongs & (rank >= 0.0) & (rank < cap)
     place_at = jnp.sum(
         jnp.where(belongs, rank + iota((dests, slots), 0).astype(F32) * cap, 0.0), axis=0, keepdims=True
     )
-    landing = jnp.where(counted, place_at, -1.0).astype(jnp.int32)
+    taken = jnp.max(jnp.where(belongs, 1.0, 0.0), axis=0, keepdims=True)
+    landing = jnp.where(taken > 0.5, place_at, -1.0).astype(jnp.int32)
     row = iota((8, slots), 0)
     flow = flow_ref[...].astype(F32)
     side = jnp.where(row == 0, flow[0:1], 0.0)
@@ -115,15 +117,15 @@
             out_ref[j, top + r * WIN : top + (r + 1) * WIN, :] = part[j * own : j * own + WIN].astype(BF16)
 
 
-def place_kernel(cap, half_wide, rows_per, got_ref, ow_ref, hidden_ref, flow_ref, term_ref, wide_hidden, wide_term):
+def place_kernel(cap, half_wide, rows_per, first_ref, second_ref, ow_ref, hidden_ref, flow_ref, term_ref, wide_hidden, wide_term):
     half = lax.axis_index("loop")
-    dests = got_ref.shape[0]
+    dests = first_ref.shape[0]
     pixels = flow_ref.shape[1]
     width = pixels // rows_per
     rows_hidden = round_up(cap, 16)
     hidden = jnp.zeros((pixels, 128), F32)
     flow = jnp.zeros((8, pixels), F32)
-    for j in range(dests):
+    for j, got_ref in [(j, ref) for j in range(dests) for ref in (first_ref, second_ref)]:
         pieces = []
         for t in range(-(-cap // 128)):
             base = rows_hidden + 8 * t
@@ -494,7 +496,7 @@
     columns = frame_two.shape[1]
     pixels = rows_per * width
     slots, hidden_size = carry_hidden.shape
-    cap = slots // dests
+    cap = -(-slots // (dests * halves))
     own = columns // dests
     half_wide = round_up(columns - own + WIN, 8)
     padded = columns + half_wide
@@ -527,13 +529,17 @@
         context,
     )
     if dests == 8:
-        packed, near, wrap, across, near_beside, wrap_beside = lax.optimization_barrier(
-            (packed, near, wrap, across, near_beside, wrap_beside)
+        packed, across = lax.optimization_barrier((packed, across))
+        across_beside = swap(across, 1)
+        packed, near, wrap, near_beside, wrap_beside, across_beside = lax.optimization_barrier(
+            (packed, near, wrap, near_beside, wrap_beside, across_beside)
         )
-        keys = (shard, beside, near, near_beside, across, swap(across, 1), wrap, wrap_beside)
+        keys = (shard, beside, near, near_beside, across, across_beside, wrap, wrap_beside)
     else:
         keys = (beside,)
     early = lax.all_to_all(packed, "rows", 0, 0, tiled=True)
+    around = [(i, (i + 1) % halves) for i in range(halves)]
+    early_other = lax.ppermute(early, "loop", around)
     ow = jnp.pad(offset_weight, ((0, 2), (0, 0)))
     hidden_wide, flow_first, term = call(
         functools.partial(place_kernel, cap, half_wide, rows_per),
@@ -542,11 +548,12 @@
             jax.ShapeDtypeStruct((8, pixels), F32),
             jax.ShapeDtypeStruct((rows_per, half_wide, 128), F32),
         ),
-        vmem_specs(2),
+        vmem_specs(3),
         [pltpu.VMEM((rows_per, padded, 128), F32)] * 2,
         (2 * slots * pixels * 128, 1 << 20, 0),
         room,
         early,
+        early_other,
         ow,
     )
     queries = frame_one.reshape(pixels, channels)
@@ -570,7 +577,7 @@
         ow,
         *keys,
     )
-    other = lax.ppermute(send, "loop", [(i, (i + 1) % halves) for i in range(halves)])
+    other = lax.ppermute(send, "loop", around)
     sending = call(
         functools.partial(merge_kernel, own),
         jax.ShapeDtypeStruct((dests, rows_per * WIN, 256), BF16),

time: 86.2 us -> 81.1 us (0.941)
  starting transfers between devices: 27.6 us -> 20.8 us
  waiting for transfers between devices: 28 us -> 31 us
  Pallas kernels: 24.9 us -> 23.6 us
    all_to_all x1, waiting for transfers between devices: 0.01 us -> 4.7 us  [local(): early = lax.all_to_all(packed, 'rows', 0, 0, tiled=True)]
    ppermute x7, waiting for transfers between devices: 13.1 us -> 10.1 us  [swap(): return lax.ppermute(value, 'rows', [(i, i ^ flip) for i in range(dests)])]
    ppermute x7, starting transfers between devices: 12.6 us -> 10.1 us  [swap(): return lax.ppermute(value, 'rows', [(i, i ^ flip) for i in range(dests)])]
    all_to_all x1, starting transfers between devices: 6.04 us -> 3.62 us  [local(): arrived = lax.all_to_all(sending, 'rows', 0, 0, tiled=True)]
    all_to_all x1, starting transfers between devices: 5.31 us -> 3.44 us  [local(): early = lax.all_to_all(packed, 'rows', 0, 0, tiled=True)]
    ppermute x1 -> x2, waiting for transfers between devices: 0.14 us -> 1.68 us  [the longest x1 1.67 us: local(): early_other = lax.ppermute(early, 'loop', around)]
    pallas_call x6, Pallas kernels: 24.9 us -> 23.6 us  [call(): pl.pallas_call(kernel, out_shape=out_shape, in_specs=in_specs, out_specs=...]
  transfers between devices with their start and end apart: 11 -> 12, of which waited for: 7 -> 7; matrix products, arithmetic and copies ran while one was open for 0% -> 0% of each run, Pallas kernels for 17% -> 16%
where the time goes in v5:
time: 81.1 us; the launch traced here: 80.6 us
  waiting for transfers between devices  31 us (38%)
  Pallas kernels  23.6 us (29%)
  starting transfers between devices  20.8 us (26%)
  blocking collectives  2.03 us (3%)
  between operations  1.5 us (2%)
  local copies, waits for them, and re-layouts  1.09 us (1%)
    pallas_call x6, Pallas kernels, call(): pl.pallas_call(kernel, out_shape=out_shape, in_specs=in_specs, out_specs=...  23.6 us
    ppermute x7, starting transfers between devices, swap(): return lax.ppermute(value, 'rows', [(i, i ^ flip) for i in range(dests)])  10.1 us
    ppermute x7, waiting for transfers between devices, swap(): return lax.ppermute(value, 'rows', [(i, i ^ flip) for i in range(dests)])  10.1 us
    all_to_all x1, waiting for transfers between devices, local(): back = lax.all_to_all(outgoing, 'rows', 0, 0, tiled=True)  7.54 us
    all_to_all x1, waiting for transfers between devices, local(): arrived = lax.all_to_all(sending, 'rows', 0, 0, tiled=True)  7.01 us
    all_to_all x1, waiting for transfers between devices, local(): early = lax.all_to_all(packed, 'rows', 0, 0, tiled=True)  4.7 us
    all_to_all x1, starting transfers between devices, local(): arrived = lax.all_to_all(sending, 'rows', 0, 0, tiled=True)  3.62 us
    all_to_all x1, starting transfers between devices, local(): back = lax.all_to_all(outgoing, 'rows', 0, 0, tiled=True)  3.58 us
  transfers between devices with their start and end apart: 12, of which 7 were waited for; matrix products, arithmetic and copies ran while one was open for 0% of the time, Pallas kernels for 16%

profile of v5, /device:TPU:0, one launch (start us, length us, event | category | flops | bytes accessed | tf_op | source)
XLA Modules:
  0.0 80.6 jit_solution(887252372634799982)
XLA Ops:
  0.6 0.0 copy-start.3
  0.6 0.0 copy-start.5
  0.7 0.0 copy-start.2
  0.7 0.0 copy-start.1
  0.7 3.0 %collective-permute-start = (bf16[1,2,128,256]{3,2,1,0:T(8,128)(2,1)}, bf16[1,2,128,256]{3,2,1,0:T(8,128)(2,1)S(1)}, u32[]{:S(2)}, u32[]{:S(2)}) collective-permute-start(bf16[1,2,128,256]{3,2,1,0:T(8,128)(2,1)} %bitcast.15), channel_id=1, source_target_pairs={{0,2},{2,0},{4,6},{6,4},{8,10},{10,8},{12,14},{14,12},{1,3},{3,1},... | collective-permute-start | bytes 393224 | tf_op jit(solution)/shard_map/ppermute | solution.py:511
  3.7 2.6 %collective-permute-start.1 = (bf16[1,2,128,256]{3,2,1,0:T(8,128)(2,1)}, bf16[1,2,128,256]{3,2,1,0:T(8,128)(2,1)S(1)}, u32[]{:S(2)}, u32[]{:S(2)}) collective-permute-start(bf16[1,2,128,256]{3,2,1,0:T(8,128)(2,1)} %bitcast.16), channel_id=1, source_target_pairs={{0,8},{2,10},{4,12},{6,14},{8,0},{10,2},{12,4},{14,6},{1,9},{3,11}... | collective-permute-start | bytes 393224 | tf_op jit(solution)/shard_map/ppermute | solution.py:511
  6.3 1.3 %collective-permute-start.3 = (bf16[1,2,128,256]{3,2,1,0:T(8,128)(2,1)}, bf16[1,2,128,256]{3,2,1,0:T(8,128)(2,1)S(1)}, u32[]{:S(2)}, u32[]{:S(2)}) collective-permute-start(bf16[1,2,128,256]{3,2,1,0:T(8,128)(2,1)} %bitcast.17), channel_id=1, source_target_pairs={{0,12},{2,14},{4,8},{6,10},{8,4},{10,6},{12,0},{14,2},{1,13},{3,15... | collective-permute-start | bytes 393224 | tf_op jit(solution)/shard_map/ppermute | solution.py:511
  7.6 0.2 collective-permute-start.2
  8.5 0.0 collective-permute-done.refs_1_
  8.5 3.9 %shard_map.149 = bf16[8,176,128]{2,1,0:T(8,128)(2,1)} custom-call(s32[1]{0:T(128)S(6)} %copy.23.count_ref, s32[12,128]{1,0:T(8,128)} %bitcast.25, bf16[2,1536]{1,0:T(2,128)(2,1)} %bitcast.26, bf16[1536,128]{1,0:T(8,128)(2,1)} %hidden_ref.1, bf16[2,256,128]{2,1,0:T(8,128)(2,1)} %context_ref.1), custom_call_target="tpu_custom_call" | custom-call | flops 603979776 | bytes 1048576 | tf_op jit(solution)/shard_map/pallas_call | solution.py:52
  12.5 4.1 %collective-permute-done.1.refs_4_ = bf16[1,2,128,256]{3,2,1,0:T(8,128)(2,1)S(1)} collective-permute-done((bf16[1,2,128,256]{3,2,1,0:T(8,128)(2,1)}, bf16[1,2,128,256]{3,2,1,0:T(8,128)(2,1)S(1)}, u32[]{:S(2)}, u32[]{:S(2)}) %collective-permute-start.1) | collective-permute-done | bytes 131104 | tf_op jit(solution)/shard_map/ppermute | solution.py:511
  16.6 2.4 %collective-permute-start.5 = (bf16[1,2,128,256]{3,2,1,0:T(8,128)(2,1)S(1)}, bf16[1,2,128,256]{3,2,1,0:T(8,128)(2,1)S(1)}, u32[]{:S(2)}, u32[]{:S(2)}) collective-permute-start(bf16[1,2,128,256]{3,2,1,0:T(8,128)(2,1)S(1)} %collective-permute-done.refs_1_), channel_id=1, source_target_pairs={{0,12},{2,14},{4,8},{6,10},{8,4},{10,6},{12,0},{14,2},{1,13},{3,15... | collective-permute-start | bytes 393224 | tf_op jit(solution)/shard_map/ppermute | solution.py:511
  19.0 0.0 collective-permute-start.4
  19.0 0.5 collective-permute-start.6
  19.5 0.0 collective-permute-done.3.refs_6_
  19.5 0.0 collective-permute-done.2.refs_2_
  19.5 4.6 %collective-permute-done.5.refs_7_ = bf16[1,2,128,256]{3,2,1,0:T(8,128)(2,1)S(1)} collective-permute-done((bf16[1,2,128,256]{3,2,1,0:T(8,128)(2,1)S(1)}, bf16[1,2,128,256]{3,2,1,0:T(8,128)(2,1)S(1)}, u32[]{:S(2)}, u32[]{:S(2)}) %collective-permute-start.5) | collective-permute-done | bytes 131104 | tf_op jit(solution)/shard_map/ppermute | solution.py:511
  24.1 1.4 %collective-permute-done.4.refs_3_ = bf16[1,2,128,256]{3,2,1,0:T(8,128)(2,1)S(1)} collective-permute-done((bf16[1,2,128,256]{3,2,1,0:T(8,128)(2,1)S(1)}, bf16[1,2,128,256]{3,2,1,0:T(8,128)(2,1)S(1)}, u32[]{:S(2)}, u32[]{:S(2)}) %collective-permute-start.4) | collective-permute-done | bytes 131104 | tf_op jit(solution)/shard_map/ppermute | solution.py:511
  25.5 0.0 collective-permute-done.6.refs_5_
  25.5 3.4 %all-to-all-start = ((bf16[8,176,128]{2,1,0:T(8,128)(2,1)}), bf16[8,176,128]{2,1,0:T(8,128)(2,1)S(1)}, u32[]{:S(2)}, u32[]{:S(2)}) async-start(bf16[8,176,128]{2,1,0:T(8,128)(2,1)} %shard_map.149), calls=%async_computation | async-start | bytes 720896 | tf_op jit(solution)/shard_map/all_to_all | solution.py:540
  28.9 0.0 copy-done.5
  28.9 0.0 copy-done.3
  29.0 0.0 copy-done.2
  29.0 0.0 copy-done.1
  29.0 5.5 %shard_map.150 = (f32[2,144,384]{2,1,0:T(8,128)S(1)}, f32[2,144,384]{2,1,0:T(8,128)S(1)}) custom-call(bf16[512,256]{1,0:T(8,128)(2,1)S(1)} %bitcast.14, bf16[512,128]{1,0:T(8,128)(2,1)S(1)} %copy-done.2, f32[8,128]{1,0:T(8,128)S(1)} %pad.8.ow_ref, bf16[1,2,128,256]{3,2,1,0:T(8,128)(2,1)S(1)} %bitcast.19, ...), custom_call_target="tpu_custom_call" | custom-call | flops 1073741824 | bytes 2097152 | tf_op jit(solution)/shard_map/pallas_call | solution.py:52
  34.5 0.0 copy-start.6
  34.5 0.0 copy-start
  34.5 0.1 collective-permute-start.7
  34.6 4.7 %all-to-all-done.first_ref.early_ref = bf16[8,176,128]{2,1,0:T(8,128)(2,1)S(1)} async-done(((bf16[8,176,128]{2,1,0:T(8,128)(2,1)}), bf16[8,176,128]{2,1,0:T(8,128)(2,1)S(1)}, u32[]{:S(2)}, u32[]{:S(2)}) %all-to-all-start) | async-done | bytes 360480 | tf_op jit(solution)/shard_map/all_to_all | solution.py:540
  39.3 0.0 collective-permute-start.8
  39.3 1.7 %collective-permute-done.8.second_ref = bf16[8,176,128]{2,1,0:T(8,128)(2,1)S(1)} collective-permute-done((bf16[8,176,128]{2,1,0:T(8,128)(2,1)S(1)}, bf16[8,176,128]{2,1,0:T(8,128)(2,1)S(1)}, u32[]{:S(2)}, u32[]{:S(2)}) %collective-permute-start.8) | collective-permute-done | bytes 360480 | tf_op jit(solution)/shard_map/ppermute | solution.py:542
  41.0 1.6 %shard_map.151 = (bf16[2,144,128]{2,1,0:T(8,128)(2,1)S(1)}, f32[8,512]{1,0:T(8,128)S(1)}, f32[2,144,128]{2,1,0:T(8,128)S(1)}) custom-call(bf16[8,176,128]{2,1,0:T(8,128)(2,1)S(1)} %all-to-all-done.first_ref.early_ref, bf16[8,176,128]{2,1,0:T(8,128)(2,1)S(1)} %collective-permute-done.8.second_ref, f32[8,128]{1,0:T(8,128)S(1)} %pad.8.ow_ref), custom_call_target="tpu_custom_call" | custom-call | flops 201326592 | bytes 1048576 | tf_op jit(solution)/shard_map/pallas_call | solution.py:52
  42.6 0.0 collective-permute-done.7.got_ref
  42.6 0.9 %shard_map.152 = bf16[8,64,256]{2,1,0:T(8,128)(2,1)} custom-call(f32[2,144,384]{2,1,0:T(8,128)S(1)} %get-tuple-element.26.keep_ref, f32[2,144,384]{2,1,0:T(8,128)S(1)} %collective-permute-done.7.got_ref, f32[2,144,128]{2,1,0:T(8,128)S(1)} %get-tuple-element.29.term_ref, bf16[2,144,128]{2,1,0:T(8,128)(2,1)S(1)} %get-tuple-element.30.hidden_ref), custom_call_target="tpu_custom_call" | custom-call | bytes 1048576 | tf_op jit(solution)/shard_map/pallas_call | solution.py:52
  43.4 3.6 %all-to-all-start.1 = ((bf16[8,64,256]{2,1,0:T(8,128)(2,1)}), bf16[8,64,256]{2,1,0:T(8,128)(2,1)S(1)}, u32[]{:S(2)}, u32[]{:S(2)}) async-start(bf16[8,64,256]{2,1,0:T(8,128)(2,1)} %shard_map.152), calls=%async_computation.1 | async-start | bytes 524288 | tf_op jit(solution)/shard_map/all_to_all | solution.py:593
  47.1 0.0 copy-done.6
  47.1 0.0 copy-done
  47.1 0.0 copy-start.4
  47.1 2.2 %shard_map.153.fixed_ref = f32[2,512,384]{2,1,0:T(8,128)S(1)} custom-call(bf16[8,176,128]{2,1,0:T(8,128)(2,1)S(1)} %all-to-all-done.first_ref.early_ref, bf16[2,5,384,256]{3,2,1,0:T(8,128)(2,1)} %gate_hbm.3, bf16[2,5,384,128]{3,2,1,0:T(8,128)(2,1)} %state_hbm.3, f32[2,384]{1,0:T(2,128)S(1)} %copy-done), custom_call_target="tpu_custom_call" | custom-call | flops 503316480 | bytes 4194304 | tf_op jit(solution)/shard_map/pallas_call | solution.py:52
  49.3 7.0 %all-to-all-done.1.got_ref = bf16[8,64,256]{2,1,0:T(8,128)(2,1)S(1)} async-done(((bf16[8,64,256]{2,1,0:T(8,128)(2,1)}), bf16[8,64,256]{2,1,0:T(8,128)(2,1)S(1)}, u32[]{:S(2)}, u32[]{:S(2)}) %all-to-all-start.1) | async-done | bytes 262176 | tf_op jit(solution)/shard_map/all_to_all | solution.py:593
  56.3 0.0 copy-done.4
  56.3 9.5 %shard_map.154 = f32[8,40,128]{2,1,0:T(8,128)} custom-call(bf16[8,64,256]{2,1,0:T(8,128)(2,1)S(1)} %all-to-all-done.1.got_ref, f32[2,512,384]{2,1,0:T(8,128)S(1)} %shard_map.153.fixed_ref, f32[8,128]{1,0:T(8,128)S(1)} %pad.8.ow_ref, bf16[2,5,384,256]{3,2,1,0:T(8,128)(2,1)} %gate_hbm.3, bf16[2,5,384,128]{3,2,1,0:T(8,128)(2,1)} %state_hbm.3, ...), custom_call_target="tpu_custom_call" | custom-call | flops 2013265920 | bytes 4194304 | tf_op jit(solution)/shard_map/pallas_call | solution.py:52
  65.8 3.6 %all-to-all-start.2 = ((f32[8,40,128]{2,1,0:T(8,128)}), f32[8,40,128]{2,1,0:T(8,128)S(1)}, u32[]{:S(2)}, u32[]{:S(2)}) async-start(f32[8,40,128]{2,1,0:T(8,128)} %shard_map.154), calls=%async_computation.2 | async-start | bytes 327680 | tf_op jit(solution)/shard_map/all_to_all | solution.py:645
  69.4 7.5 %all-to-all-done.2 = f32[8,40,128]{2,1,0:T(8,128)S(1)} async-done(((f32[8,40,128]{2,1,0:T(8,128)}), f32[8,40,128]{2,1,0:T(8,128)S(1)}, u32[]{:S(2)}, u32[]{:S(2)}) %all-to-all-start.2) | async-done | bytes 163872 | tf_op jit(solution)/shard_map/all_to_all | solution.py:645
  77.0 2.0 %all-gather = f32[16,40,128]{2,1,0:T(8,128)S(1)} all-gather(f32[8,40,128]{2,1,0:T(8,128)S(1)} %all-to-all-done.2), channel_id=2, replica_groups=mesh['groups'=2,'rows'=8,'loop'=2] {'loop'}, dimensions={0}, use_global_device_ids=true | all-gather | bytes 491520 | tf_op jit(solution)/shard_map/all_gather | solution.py:646
  79.0 0.7 copy.18
  79.7 0.1 reshape.34
  79.8 0.1 slice.18
  79.9 0.1 reshape.35
  80.0 0.6 add.7
  (7 shorter events, 0.1 us)
Async XLA Ops:
  0.6 28.3 %copy-start.3 = (bf16[2,128,256]{2,1,0:T(8,128)(2,1)S(1)}, bf16[2,128,256]{2,1,0:T(8,128)(2,1)}, u32[]{:S(2)}) copy-start(bf16[2,128,256]{2,1,0:T(8,128)(2,1)} %param.15) | copy-start | bytes 393220
  0.6 28.3 %copy-start.5 = (f32[6,128]{1,0:T(8,128)S(1)}, f32[6,128]{1,0:T(8,128)}, u32[]{:S(2)}) copy-start(f32[6,128]{1,0:T(8,128)} %param.22) | copy-start | bytes 9220
  0.7 28.3 %copy-start.2 = (bf16[512,128]{1,0:T(8,128)(2,1)S(1)}, bf16[512,128]{1,0:T(8,128)(2,1)}, u32[]{:S(2)}) copy-start(bf16[512,128]{1,0:T(8,128)(2,1)} %weight_ref.1) | copy-start | bytes 393220
  0.7 28.3 %copy-start.1 = (bf16[2,256,256]{2,1,0:T(8,128)(2,1)S(1)}, bf16[2,256,256]{2,1,0:T(8,128)(2,1)}, u32[]{:S(2)}) copy-start(bf16[2,256,256]{2,1,0:T(8,128)(2,1)} %param.14) | copy-start | bytes 786436
  0.7 7.9 %collective-permute-start = (bf16[1,2,128,256]{3,2,1,0:T(8,128)(2,1)}, bf16[1,2,128,256]{3,2,1,0:T(8,128)(2,1)S(1)}, u32[]{:S(2)}, u32[]{:S(2)}) collective-permute-start(bf16[1,2,128,256]{3,2,1,0:T(8,128)(2,1)} %bitcast.15), channel_id=1, source_target_pairs={{0,2},{2,0},{4,6},{6,4},{8,10},{10,8},{12,14},{14,12},{1,3},{3,1},... | collective-permute-start | bytes 393224 | tf_op jit(solution)/shard_map/ppermute | solution.py:511
  3.7 12.9 %collective-permute-start.1 = (bf16[1,2,128,256]{3,2,1,0:T(8,128)(2,1)}, bf16[1,2,128,256]{3,2,1,0:T(8,128)(2,1)S(1)}, u32[]{:S(2)}, u32[]{:S(2)}) collective-permute-start(bf16[1,2,128,256]{3,2,1,0:T(8,128)(2,1)} %bitcast.16), channel_id=1, source_target_pairs={{0,8},{2,10},{4,12},{6,14},{8,0},{10,2},{12,4},{14,6},{1,9},{3,11}... | collective-permute-start | bytes 393224 | tf_op jit(solution)/shard_map/ppermute | solution.py:511
  6.3 13.2 %collective-permute-start.3 = (bf16[1,2,128,256]{3,2,1,0:T(8,128)(2,1)}, bf16[1,2,128,256]{3,2,1,0:T(8,128)(2,1)S(1)}, u32[]{:S(2)}, u32[]{:S(2)}) collective-permute-start(bf16[1,2,128,256]{3,2,1,0:T(8,128)(2,1)} %bitcast.17), channel_id=1, source_target_pairs={{0,12},{2,14},{4,8},{6,10},{8,4},{10,6},{12,0},{14,2},{1,13},{3,15... | collective-permute-start | bytes 393224 | tf_op jit(solution)/shard_map/ppermute | solution.py:511
  7.6 11.8 %collective-permute-start.2 = (bf16[1,2,128,256]{3,2,1,0:T(8,128)(2,1)}, bf16[1,2,128,256]{3,2,1,0:T(8,128)(2,1)S(1)}, u32[]{:S(2)}, u32[]{:S(2)}) collective-permute-start(bf16[1,2,128,256]{3,2,1,0:T(8,128)(2,1)} %bitcast.18), channel_id=1, source_target_pairs={{0,4},{2,6},{4,0},{6,2},{8,12},{10,14},{12,8},{14,10},{1,5},{3,7},... | collective-permute-start | bytes 393224 | tf_op jit(solution)/shard_map/ppermute | solution.py:511
  16.6 7.5 %collective-permute-start.5 = (bf16[1,2,128,256]{3,2,1,0:T(8,128)(2,1)S(1)}, bf16[1,2,128,256]{3,2,1,0:T(8,128)(2,1)S(1)}, u32[]{:S(2)}, u32[]{:S(2)}) collective-permute-start(bf16[1,2,128,256]{3,2,1,0:T(8,128)(2,1)S(1)} %collective-permute-done.refs_1_), channel_id=1, source_target_pairs={{0,12},{2,14},{4,8},{6,10},{8,4},{10,6},{12,0},{14,2},{1,13},{3,15... | collective-permute-start | bytes 393224 | tf_op jit(solution)/shard_map/ppermute | solution.py:511
  19.0 6.5 %collective-permute-start.4 = (bf16[1,2,128,256]{3,2,1,0:T(8,128)(2,1)S(1)}, bf16[1,2,128,256]{3,2,1,0:T(8,128)(2,1)S(1)}, u32[]{:S(2)}, u32[]{:S(2)}) collective-permute-start(bf16[1,2,128,256]{3,2,1,0:T(8,128)(2,1)S(1)} %collective-permute-done.refs_1_), channel_id=1, source_target_pairs={{0,4},{2,6},{4,0},{6,2},{8,12},{10,14},{12,8},{14,10},{1,5},{3,7},... | collective-permute-start | bytes 393224 | tf_op jit(solution)/shard_map/ppermute | solution.py:511
  19.0 6.5 %collective-permute-start.6 = (bf16[1,2,128,256]{3,2,1,0:T(8,128)(2,1)S(1)}, bf16[1,2,128,256]{3,2,1,0:T(8,128)(2,1)S(1)}, u32[]{:S(2)}, u32[]{:S(2)}) collective-permute-start(bf16[1,2,128,256]{3,2,1,0:T(8,128)(2,1)S(1)} %collective-permute-done.1.refs_4_), channel_id=1, source_target_pairs={{0,2},{2,0},{4,6},{6,4},{8,10},{10,8},{12,14},{14,12},{1,3},{3,1},... | collective-permute-start | bytes 393224 | tf_op jit(solution)/shard_map/ppermute | solution.py:511
  25.5 13.8 %all-to-all-start = ((bf16[8,176,128]{2,1,0:T(8,128)(2,1)}), bf16[8,176,128]{2,1,0:T(8,128)(2,1)S(1)}, u32[]{:S(2)}, u32[]{:S(2)}) async-start(bf16[8,176,128]{2,1,0:T(8,128)(2,1)} %shard_map.149), calls=%async_computation | async-start | bytes 720896 | tf_op jit(solution)/shard_map/all_to_all | solution.py:540
  34.5 12.6 %copy-start.6 = (bf16[2,256]{1,0:T(2,128)(2,1)S(1)}, bf16[2,256]{1,0:T(2,128)(2,1)}, u32[]{:S(2)}) copy-start(bf16[2,256]{1,0:T(2,128)(2,1)} %param.27) | copy-start | bytes 3076
  34.5 12.6 %copy-start = (f32[2,384]{1,0:T(2,128)S(1)}, f32[2,384]{1,0:T(2,128)}, u32[]{:S(2)}) copy-start(f32[2,384]{1,0:T(2,128)} %bias_ref.1) | copy-start | bytes 9220
  34.5 8.0 %collective-permute-start.7 = (f32[2,144,384]{2,1,0:T(8,128)S(1)}, f32[2,144,384]{2,1,0:T(8,128)S(1)}, u32[]{:S(2)}, u32[]{:S(2)}) collective-permute-start(f32[2,144,384]{2,1,0:T(8,128)S(1)} %get-tuple-element.27), channel_id=1, source_target_pairs={{0,1},{1,0},{2,3},{3,2},{4,5},{5,4},{6,7},{7,6},{8,9},{9,8},{10,11... | collective-permute-start | bytes 1327112 | tf_op jit(solution)/shard_map/ppermute | solution.py:580
  39.3 1.7 %collective-permute-start.8 = (bf16[8,176,128]{2,1,0:T(8,128)(2,1)S(1)}, bf16[8,176,128]{2,1,0:T(8,128)(2,1)S(1)}, u32[]{:S(2)}, u32[]{:S(2)}) collective-permute-start(bf16[8,176,128]{2,1,0:T(8,128)(2,1)S(1)} %all-to-all-done.first_ref.early_ref), channel_id=1, source_target_pairs={{0,1},{1,0},{2,3},{3,2},{4,5},{5,4},{6,7},{7,6},{8,9},{9,8},{10,11... | collective-permute-start | bytes 1081352 | tf_op jit(solution)/shard_map/ppermute | solution.py:542
  43.4 12.9 %all-to-all-start.1 = ((bf16[8,64,256]{2,1,0:T(8,128)(2,1)}), bf16[8,64,256]{2,1,0:T(8,128)(2,1)S(1)}, u32[]{:S(2)}, u32[]{:S(2)}) async-start(bf16[8,64,256]{2,1,0:T(8,128)(2,1)} %shard_map.152), calls=%async_computation.1 | async-start | bytes 524288 | tf_op jit(solution)/shard_map/all_to_all | solution.py:593
  47.1 9.3 %copy-start.4 = (bf16[128,256]{1,0:T(8,128)(2,1)S(1)}, bf16[128,256]{1,0:T(8,128)(2,1)}, u32[]{:S(2)}) copy-start(bf16[128,256]{1,0:T(8,128)(2,1)} %head_ref.1) | copy-start | bytes 196612
  65.8 11.1 %all-to-all-start.2 = ((f32[8,40,128]{2,1,0:T(8,128)}), f32[8,40,128]{2,1,0:T(8,128)S(1)}, u32[]{:S(2)}, u32[]{:S(2)}) async-start(f32[8,40,128]{2,1,0:T(8,128)} %shard_map.154), calls=%async_computation.2 | async-start | bytes 327680 | tf_op jit(solution)/shard_map/all_to_all | solution.py:645

commit v6 on v5

--- a/solution.py
+++ b/solution.py
@@ -10,8 +10,10 @@
 
 ITERS = 2
 WIN = 32
+SLIM = 16
 HALO = 8
 TILE = 512
+SLIM_TILE = TILE * SLIM // WIN
 OFFSET_SCALE = 0.03125
 F32 = jnp.float32
 BF16 = jnp.bfloat16
@@ -362,7 +364,8 @@
 
 def update_kernel(
     own, width, got_ref, fixed_ref, ow_ref, gate_hbm, state_hbm, head_ref, delta_ref,
-    out_ref, base, hidden, motions, states, resets, updates, taps, flow, flow_cols, gate_ref, state_ref, sems,
+    out_ref, base, hidden, motions, states, resets, updates, taps, flow, flow_cols, gate_ref, state_ref,
+    slim_taps, slim_states, slim_motions, slim_resets, slim_hidden, sems,
 ):
     handles = []
     for p in range(2):
@@ -392,6 +395,10 @@
     for ref in (motions, states, resets):
         ref[0:pad, :] = jnp.zeros((pad, 128), BF16)
         ref[pad + count : pad + count + pad, :] = jnp.zeros((pad, 128), BF16)
+    slim_pad = 2 * SLIM
+    for ref in (slim_motions, slim_states, slim_resets):
+        ref[0:slim_pad, :] = jnp.zeros((slim_pad, 128), BF16)
+        ref[slim_pad + count // 2 :, :] = jnp.zeros((slim_pad, 128), BF16)
     for j in range(dests):
         at = j * per_dest
         base[at : at + per_dest, :] = got_ref[j, :, 0:128]
@@ -403,7 +410,12 @@
         hidden[pl.ds(at, TILE), :] = new
         return new
 
+    def slim(value):
+        cube = value.reshape(TILE // WIN, WIN, value.shape[1])
+        return cube[:, HALO : HALO + SLIM, :].reshape(SLIM_TILE, value.shape[1])
+
     for iteration in range(ITERS):
+        last = iteration == ITERS - 1
 
         def columns_pass(at):
             motion = base[pl.ds(at, TILE), :].astype(F32)
@@ -412,7 +424,8 @@
                 motion = (motion + moved[:, 0:1] * add_row + moved[:, 1:2] * add_col) * mask
             motion = jnp.maximum(motion, 0.0)
             rounded = motion.astype(BF16)
-            motions[pl.ds(pad + at, TILE), :] = rounded
+            if not last:
+                motions[pl.ds(pad + at, TILE), :] = rounded
             motion = rounded.astype(F32)
             state = hidden[pl.ds(at, TILE), :].astype(BF16).astype(F32)
             for tap in range(5):
@@ -422,6 +435,20 @@
                 ready(0)
             gates = sigmoid(dot(taps[...], gate_ref[0].reshape(1280, 256)) + fixed_ref[0, pl.ds(at, TILE), 0:256])
             reset = (gates[:, 128:256] * state).astype(BF16).astype(F32)
+            if last:
+                to = pl.multiple_of(at // 2, SLIM_TILE)
+                for tap in range(5):
+                    slim_taps[:, tap * 256 : tap * 256 + 128] = slim(shifted(reset, tap)).astype(BF16)
+                    slim_taps[:, tap * 256 + 128 : tap * 256 + 256] = slim(shifted(motion, tap)).astype(BF16)
+                candidate = jnp.tanh(
+                    dot(slim_taps[...], state_ref[0].reshape(1280, 128)) + slim(fixed_ref[0, pl.ds(at, TILE), 256:384])
+                )
+                old = slim(hidden[pl.ds(at, TILE), :])
+                new = old + slim(gates[:, 0:128]) * (candidate - old)
+                slim_hidden[pl.ds(to, SLIM_TILE), :] = new
+                slim_states[pl.ds(slim_pad + to, SLIM_TILE), :] = new.astype(BF16)
+                slim_motions[pl.ds(slim_pad + to, SLIM_TILE), :] = slim(motion).astype(BF16)
+                return
             for tap in range(5):
                 taps[:, tap * 256 : tap * 256 + 128] = shifted(reset, tap).astype(BF16)
             if iteration == 0 and count == TILE:
@@ -429,30 +456,52 @@
             candidate = jnp.tanh(dot(taps[...], state_ref[0].reshape(1280, 128)) + fixed_ref[0, pl.ds(at, TILE), 256:384])
             states[pl.ds(pad + at, TILE), :] = finish(at, gates[:, 0:128], candidate).astype(BF16)
 
-        def fill(first, at):
+        def fill(out, first, second, at, stride, size):
             for tap in range(5):
-                taps[:, tap * 256 : tap * 256 + 128] = first[pl.ds(at + tap * WIN, TILE), :]
-                taps[:, tap * 256 + 128 : tap * 256 + 256] = motions[pl.ds(at + tap * WIN, TILE), :]
+                out[:, tap * 256 : tap * 256 + 128] = first[pl.ds(at + tap * stride, size), :]
+                out[:, tap * 256 + 128 : tap * 256 + 256] = second[pl.ds(at + tap * stride, size), :]
 
         def gate_rows(at):
-            fill(states, at)
+            fill(taps, states, motions, at, WIN, TILE)
             gates = sigmoid(dot(taps[...], gate_ref[1].reshape(1280, 256)) + fixed_ref[1, pl.ds(at, TILE), 0:256])
             updates[pl.ds(at, TILE), :] = gates[:, 0:128]
             resets[pl.ds(pad + at, TILE), :] = (
                 gates[:, 128:256] * states[pl.ds(pad + at, TILE), :].astype(F32)
             ).astype(BF16)
 
+        def head(new):
+            lifted = jnp.maximum(dot(new.astype(BF16), head_ref[...]), 0.0).astype(BF16)
+            return dot_nt(delta_ref[...], lifted)
+
         def state_rows(at):
-            fill(resets, at)
-            candidate = jnp.tanh(dot(taps[...], state_ref[1].reshape(1280, 128)) + fixed_ref[1, pl.ds(at, TILE), 256:384])
+            fill(taps, resets, motions, at, WIN, TILE)
+            candidate = jnp.tanh(
+                dot(taps[...], state_ref[1].reshape(1280, 128)) + fixed_ref[1, pl.ds(at, TILE), 256:384]
+            )
             new = finish(at, updates[pl.ds(at, TILE), :], candidate)
-            lifted = jnp.maximum(dot(new.astype(BF16), head_ref[...]), 0.0).astype(BF16)
-            step = dot_nt(delta_ref[...], lifted)
-            if iteration == 0:
-                flow[:, pl.ds(at, TILE)] = step
-                flow_cols[pl.ds(at, TILE), :] = step.T
-            else:
-                flow[:, pl.ds(at, TILE)] = flow[:, pl.ds(at, TILE)] + step
+            flow_cols[pl.ds(at, TILE), :] = head(new).T
+
+        def slim_gate_rows(at):
+            to = pl.multiple_of(at // 2, SLIM_TILE)
+            fill(slim_taps, slim_states, slim_motions, to, SLIM, SLIM_TILE)
+            gates = sigmoid(
+                dot(slim_taps[...], gate_ref[1].reshape(1280, 256)) + slim(fixed_ref[1, pl.ds(at, TILE), 0:256])
+            )
+            updates[pl.ds(to, SLIM_TILE), :] = gates[:, 0:128]
+            slim_resets[pl.ds(slim_pad + to, SLIM_TILE), :] = (
+                gates[:, 128:256] * slim_states[pl.ds(slim_pad + to, SLIM_TILE), :].astype(F32)
+            ).astype(BF16)
+
+        def slim_state_rows(at):
+            to = pl.multiple_of(at // 2, SLIM_TILE)
+            fill(slim_taps, slim_resets, slim_motions, to, SLIM, SLIM_TILE)
+            candidate = jnp.tanh(
+                dot(slim_taps[...], state_ref[1].reshape(1280, 128)) + slim(fixed_ref[1, pl.ds(at, TILE), 256:384])
+            )
+            old = slim_hidden[pl.ds(to, SLIM_TILE), :]
+            new = old + updates[pl.ds(to, SLIM_TILE), :] * (candidate - old)
+            slim_hidden[pl.ds(to, SLIM_TILE), :] = new
+            flow[:, pl.ds(to, SLIM_TILE)] = head(new) + slim(flow_cols[pl.ds(at, TILE), :]).T
 
         if iteration == 0 and count != TILE:
             ready(0)
@@ -461,17 +510,39 @@
         if iteration == 0:
             ready(2)
             ready(3)
-        each_tile(count, gate_rows)
-        each_tile(count, state_rows)
+            each_tile(count, gate_rows)
+            each_tile(count, state_rows)
+        else:
+            each_tile(count, slim_gate_rows)
+            each_tile(count, slim_state_rows)
 
     for j in range(dests):
         for r in range(rows_per):
-            at = j * per_dest + r * WIN + HALO
-            out_ref[j, r * own : (r + 1) * own, :] = hidden[at : at + own, :]
-        moved = flow[:, j * per_dest : (j + 1) * per_dest]
+            at = j * rows_per * SLIM + r * SLIM
+            out_ref[j, r * own : (r + 1) * own, :] = slim_hidden[at : at + own, :]
+        moved = flow[:, j * rows_per * SLIM : (j + 1) * rows_per * SLIM]
         out_ref[j, rows_per * own : rows_per * own + 8, :] = jnp.concatenate(
-            [moved, jnp.zeros((8, 128 - per_dest), F32)], axis=1
+            [moved, jnp.zeros((8, 128 - rows_per * SLIM), F32)], axis=1
         )
+
+
+def finish_kernel(own, mine_ref, other_ref, first_ref, hidden_ref, flow_ref):
+    half = lax.axis_index("loop")
+    rows_per, width, _ = hidden_ref.shape
+    columns = width // 2
+    dests = mine_ref.shape[0]
+    for ref, side in ((mine_ref, half), (other_ref, 1 - half)):
+        start = pl.multiple_of(side * columns, 128)
+        for r in range(rows_per):
+            cells = [ref[j, r * own : (r + 1) * own, :] for j in range(dests)]
+            hidden_ref[r, pl.ds(start, columns), :] = jnp.concatenate(cells, axis=0)
+            moved = jnp.concatenate(
+                [ref[j, rows_per * own : rows_per * own + 8, r * SLIM : r * SLIM + own] for j in range(dests)], axis=1
+            )
+            at = pl.multiple_of(r * width + side * columns, 128)
+            total = first_ref[:, pl.ds(at, columns)] + moved
+            for k in range(2):
+                flow_ref[k, r : r + 1, pl.ds(start, columns)] = total[k : k + 1]
 
 
 def local(
@@ -626,10 +697,15 @@
             pltpu.VMEM((count + 4 * WIN, 128), BF16),
             pltpu.VMEM((count, 128), F32),
             pltpu.VMEM((TILE, 1280), BF16),
-            pltpu.VMEM((8, count), F32),
+            pltpu.VMEM((8, count // 2), F32),
             pltpu.VMEM((count, 8), F32),
             pltpu.VMEM((2, 5, 256, 256), BF16),
             pltpu.VMEM((2, 5, 256, 128), BF16),
+            pltpu.VMEM((SLIM_TILE, 1280), BF16),
+            pltpu.VMEM((count // 2 + 4 * SLIM, 128), BF16),
+            pltpu.VMEM((count // 2 + 4 * SLIM, 128), BF16),
+            pltpu.VMEM((count // 2 + 4 * SLIM, 128), BF16),
+            pltpu.VMEM((count // 2, 128), F32),
             pltpu.SemaphoreType.DMA((8,)),
         ],
         (8 * count * 5 * 256 * 384, 1 << 22, 8 * count * 384),
@@ -643,13 +719,20 @@
         jnp.pad(delta_weight, ((0, 6), (0, 0))),
     )
     back = lax.all_to_all(outgoing, "rows", 0, 0, tiled=True)
-    both = lax.all_gather(back, "loop", axis=0)
-    cells = both[:, :, : rows_per * own, :].reshape(halves, dests, rows_per, own, hidden_size)
-    hidden_out = cells.transpose(2, 0, 1, 3, 4).reshape(rows_per, width, hidden_size)
-    moved = both[:, :, rows_per * own : rows_per * own + 2, : rows_per * WIN]
-    moved = moved.reshape(halves, dests, 2, rows_per, WIN)[..., HALO : HALO + own]
-    moved = moved.transpose(2, 3, 0, 1, 4).reshape(2, rows_per, width)
-    flow_out = flow_first[:2].reshape(2, rows_per, width) + moved
+    hidden_out, flow_out = call(
+        functools.partial(finish_kernel, own),
+        (
+            jax.ShapeDtypeStruct((rows_per, width, hidden_size), F32),
+            jax.ShapeDtypeStruct((2, rows_per, width), F32),
+        ),
+        vmem_specs(3),
+        [],
+        (0, 1 << 20, 0),
+        room,
+        back,
+        lax.ppermute(back, "loop", around),
+        flow_first,
+    )
     return (hidden_out, flow_out)
 
 

time: 81.1 us -> 75 us (0.925)
  waiting for transfers between devices: 31 us -> 22 us
  blocking collectives: 2.03 us -> 10.9 us
  starting transfers between devices: 20.8 us -> 17.6 us
  Pallas kernels: 23.6 us -> 22.5 us
  local copies, waits for them, and re-layouts: 1.09 us -> 0.05 us
    all_to_all x0 -> x1, blocking collectives: none -> 10.9 us  [local(): back = lax.all_to_all(outgoing, 'rows', 0, 0, tiled=True)]
    all_to_all x1 -> x0, waiting for transfers between devices: 7.54 us -> none  [local(): back = lax.all_to_all(outgoing, 'rows', 0, 0, tiled=True)]
    all_to_all x1 -> x0, starting transfers between devices: 3.58 us -> none  [local(): back = lax.all_to_all(outgoing, 'rows', 0, 0, tiled=True)]
    all_gather x1 -> x0, blocking collectives: 2.03 us -> none  [local(): both = lax.all_gather(back, 'loop', axis=0)]
    ppermute x7, waiting for transfers between devices: 10.1 us -> 8.55 us  [swap(): return lax.ppermute(value, 'rows', [(i, i ^ flip) for i in range(dests)])]
    ppermute x0 -> x1, waiting for transfers between devices: none -> 1.39 us  [local(): lax.ppermute(back, 'loop', around)]
    all_to_all x1, waiting for transfers between devices: 4.7 us -> 3.42 us  [local(): early = lax.all_to_all(packed, 'rows', 0, 0, tiled=True)]
    pallas_call x6 -> x7, Pallas kernels: 23.6 us -> 22.5 us  [call(): pl.pallas_call(kernel, out_shape=out_shape, in_specs=in_specs, out_specs=...]
  transfers between devices with their start and end apart: 12 -> 12, of which waited for: 7 -> 7; matrix products, arithmetic and copies ran while one was open for 0% -> 0% of each run, Pallas kernels for 16% -> 18%
where the time goes in v6:
time: 75 us; the launch traced here: 74.6 us
  Pallas kernels  22.5 us (30%)
  waiting for transfers between devices  22 us (29%)
  starting transfers between devices  17.6 us (23%)
  blocking collectives  10.9 us (15%)
  between operations  1.46 us (2%)
    pallas_call x7, Pallas kernels, call(): pl.pallas_call(kernel, out_shape=out_shape, in_specs=in_specs, out_specs=...  22.5 us
    all_to_all x1, blocking collectives, local(): back = lax.all_to_all(outgoing, 'rows', 0, 0, tiled=True)  10.9 us
    ppermute x7, starting transfers between devices, swap(): return lax.ppermute(value, 'rows', [(i, i ^ flip) for i in range(dests)])  10.2 us
    ppermute x7, waiting for transfers between devices, swap(): return lax.ppermute(value, 'rows', [(i, i ^ flip) for i in range(dests)])  8.55 us
    all_to_all x1, waiting for transfers between devices, local(): arrived = lax.all_to_all(sending, 'rows', 0, 0, tiled=True)  6.99 us
    all_to_all x1, starting transfers between devices, local(): early = lax.all_to_all(packed, 'rows', 0, 0, tiled=True)  3.66 us
    all_to_all x1, starting transfers between devices, local(): arrived = lax.all_to_all(sending, 'rows', 0, 0, tiled=True)  3.64 us
    all_to_all x1, waiting for transfers between devices, local(): early = lax.all_to_all(packed, 'rows', 0, 0, tiled=True)  3.42 us
  transfers between devices with their start and end apart: 12, of which 7 were waited for; matrix products, arithmetic and copies ran while one was open for 0% of the time, Pallas kernels for 18%

profile of v6, /device:TPU:0, one launch (start us, length us, event | category | flops | bytes accessed | tf_op | source)
XLA Modules:
  0.0 74.6 jit_solution(15578186214913430844)
XLA Ops:
  0.6 0.0 copy-start.3
  0.6 0.0 copy-start.5
  0.7 0.0 copy-start.1
  0.7 0.0 copy-start.2
  0.7 3.0 %collective-permute-start = (bf16[1,2,128,256]{3,2,1,0:T(8,128)(2,1)}, bf16[1,2,128,256]{3,2,1,0:T(8,128)(2,1)S(1)}, u32[]{:S(2)}, u32[]{:S(2)}) collective-permute-start(bf16[1,2,128,256]{3,2,1,0:T(8,128)(2,1)} %bitcast.5), channel_id=1, source_target_pairs={{0,2},{2,0},{4,6},{6,4},{8,10},{10,8},{12,14},{14,12},{1,3},{3,1},... | collective-permute-start | bytes 393224 | tf_op jit(solution)/shard_map/ppermute | solution.py:582
  3.7 2.6 %collective-permute-start.1 = (bf16[1,2,128,256]{3,2,1,0:T(8,128)(2,1)}, bf16[1,2,128,256]{3,2,1,0:T(8,128)(2,1)S(1)}, u32[]{:S(2)}, u32[]{:S(2)}) collective-permute-start(bf16[1,2,128,256]{3,2,1,0:T(8,128)(2,1)} %bitcast.6), channel_id=1, source_target_pairs={{0,8},{2,10},{4,12},{6,14},{8,0},{10,2},{12,4},{14,6},{1,9},{3,11}... | collective-permute-start | bytes 393224 | tf_op jit(solution)/shard_map/ppermute | solution.py:582
  6.3 1.6 %collective-permute-start.2 = (bf16[1,2,128,256]{3,2,1,0:T(8,128)(2,1)}, bf16[1,2,128,256]{3,2,1,0:T(8,128)(2,1)S(1)}, u32[]{:S(2)}, u32[]{:S(2)}) collective-permute-start(bf16[1,2,128,256]{3,2,1,0:T(8,128)(2,1)} %bitcast.7), channel_id=1, source_target_pairs={{0,4},{2,6},{4,0},{6,2},{8,12},{10,14},{12,8},{14,10},{1,5},{3,7},... | collective-permute-start | bytes 393224 | tf_op jit(solution)/shard_map/ppermute | solution.py:582
  7.9 0.2 collective-permute-start.3
  8.7 0.0 collective-permute-done.refs_1_
  8.8 4.0 %shard_map.149 = bf16[8,176,128]{2,1,0:T(8,128)(2,1)} custom-call(s32[1]{0:T(128)S(6)} %copy.16.count_ref, s32[12,128]{1,0:T(8,128)} %bitcast.10, bf16[2,1536]{1,0:T(2,128)(2,1)} %bitcast.11, bf16[1536,128]{1,0:T(8,128)(2,1)} %hidden_ref.1, bf16[2,256,128]{2,1,0:T(8,128)(2,1)} %context_ref.1), custom_call_target="tpu_custom_call" | custom-call | flops 603979776 | bytes 1048576 | tf_op jit(solution)/shard_map/pallas_call | solution.py:54
  12.7 3.9 %collective-permute-done.1.refs_4_ = bf16[1,2,128,256]{3,2,1,0:T(8,128)(2,1)S(1)} collective-permute-done((bf16[1,2,128,256]{3,2,1,0:T(8,128)(2,1)}, bf16[1,2,128,256]{3,2,1,0:T(8,128)(2,1)S(1)}, u32[]{:S(2)}, u32[]{:S(2)}) %collective-permute-start.1) | collective-permute-done | bytes 131104 | tf_op jit(solution)/shard_map/ppermute | solution.py:582
  16.6 0.0 collective-permute-start.4
  16.6 2.3 %collective-permute-start.5 = (bf16[1,2,128,256]{3,2,1,0:T(8,128)(2,1)S(1)}, bf16[1,2,128,256]{3,2,1,0:T(8,128)(2,1)S(1)}, u32[]{:S(2)}, u32[]{:S(2)}) collective-permute-start(bf16[1,2,128,256]{3,2,1,0:T(8,128)(2,1)S(1)} %collective-permute-done.refs_1_), channel_id=1, source_target_pairs={{0,12},{2,14},{4,8},{6,10},{8,4},{10,6},{12,0},{14,2},{1,13},{3,15... | collective-permute-start | bytes 393224 | tf_op jit(solution)/shard_map/ppermute | solution.py:582
  18.9 0.5 collective-permute-start.6
  19.4 0.0 collective-permute-done.2.refs_2_
  19.4 0.0 collective-permute-done.3.refs_6_
  19.4 3.2 %collective-permute-done.4.refs_3_ = bf16[1,2,128,256]{3,2,1,0:T(8,128)(2,1)S(1)} collective-permute-done((bf16[1,2,128,256]{3,2,1,0:T(8,128)(2,1)S(1)}, bf16[1,2,128,256]{3,2,1,0:T(8,128)(2,1)S(1)}, u32[]{:S(2)}, u32[]{:S(2)}) %collective-permute-start.4) | collective-permute-done | bytes 131104 | tf_op jit(solution)/shard_map/ppermute | solution.py:582
  22.6 1.4 %collective-permute-done.5.refs_7_ = bf16[1,2,128,256]{3,2,1,0:T(8,128)(2,1)S(1)} collective-permute-done((bf16[1,2,128,256]{3,2,1,0:T(8,128)(2,1)S(1)}, bf16[1,2,128,256]{3,2,1,0:T(8,128)(2,1)S(1)}, u32[]{:S(2)}, u32[]{:S(2)}) %collective-permute-start.5) | collective-permute-done | bytes 131104 | tf_op jit(solution)/shard_map/ppermute | solution.py:582
  24.0 0.0 collective-permute-done.6.refs_5_
  24.0 3.7 %all-to-all-start = ((bf16[8,176,128]{2,1,0:T(8,128)(2,1)}), bf16[8,176,128]{2,1,0:T(8,128)(2,1)S(1)}, u32[]{:S(2)}, u32[]{:S(2)}) async-start(bf16[8,176,128]{2,1,0:T(8,128)(2,1)} %shard_map.149), calls=%async_computation | async-start | bytes 720896 | tf_op jit(solution)/shard_map/all_to_all | solution.py:611
  27.7 0.0 copy-done.5
  27.7 0.0 copy-done.3
  27.7 0.0 copy-done.1
  27.7 0.0 copy-done.2
  27.7 5.5 %shard_map.150 = (f32[2,144,384]{2,1,0:T(8,128)S(1)}, f32[2,144,384]{2,1,0:T(8,128)S(1)}) custom-call(bf16[512,256]{1,0:T(8,128)(2,1)S(1)} %bitcast.4, bf16[512,128]{1,0:T(8,128)(2,1)S(1)} %copy-done.2, f32[8,128]{1,0:T(8,128)S(1)} %pad.8.ow_ref, bf16[1,2,128,256]{3,2,1,0:T(8,128)(2,1)S(1)} %bitcast.9, ...), custom_call_target="tpu_custom_call" | custom-call | flops 1073741824 | bytes 2097152 | tf_op jit(solution)/shard_map/pallas_call | solution.py:54
  33.3 0.0 copy-start.6
  33.3 0.0 copy-start
  33.3 0.1 collective-permute-start.7
  33.4 3.4 %all-to-all-done.first_ref.early_ref = bf16[8,176,128]{2,1,0:T(8,128)(2,1)S(1)} async-done(((bf16[8,176,128]{2,1,0:T(8,128)(2,1)}), bf16[8,176,128]{2,1,0:T(8,128)(2,1)S(1)}, u32[]{:S(2)}, u32[]{:S(2)}) %all-to-all-start) | async-done | bytes 360480 | tf_op jit(solution)/shard_map/all_to_all | solution.py:611
  36.8 0.0 collective-permute-start.8
  36.8 1.7 %collective-permute-done.8.second_ref = bf16[8,176,128]{2,1,0:T(8,128)(2,1)S(1)} collective-permute-done((bf16[8,176,128]{2,1,0:T(8,128)(2,1)S(1)}, bf16[8,176,128]{2,1,0:T(8,128)(2,1)S(1)}, u32[]{:S(2)}, u32[]{:S(2)}) %collective-permute-start.8) | collective-permute-done | bytes 360480 | tf_op jit(solution)/shard_map/ppermute | solution.py:613
  38.5 1.6 %shard_map.151 = (bf16[2,144,128]{2,1,0:T(8,128)(2,1)S(1)}, f32[8,512]{1,0:T(8,128)S(1)}, f32[2,144,128]{2,1,0:T(8,128)S(1)}) custom-call(bf16[8,176,128]{2,1,0:T(8,128)(2,1)S(1)} %all-to-all-done.first_ref.early_ref, bf16[8,176,128]{2,1,0:T(8,128)(2,1)S(1)} %collective-permute-done.8.second_ref, f32[8,128]{1,0:T(8,128)S(1)} %pad.8.ow_ref), custom_call_target="tpu_custom_call" | custom-call | flops 201326592 | bytes 1048576 | tf_op jit(solution)/shard_map/pallas_call | solution.py:54
  40.0 0.0 collective-permute-done.7.got_ref
  40.1 0.9 %shard_map.152 = bf16[8,64,256]{2,1,0:T(8,128)(2,1)} custom-call(f32[2,144,384]{2,1,0:T(8,128)S(1)} %get-tuple-element.26.keep_ref, f32[2,144,384]{2,1,0:T(8,128)S(1)} %collective-permute-done.7.got_ref, f32[2,144,128]{2,1,0:T(8,128)S(1)} %get-tuple-element.29.term_ref, bf16[2,144,128]{2,1,0:T(8,128)(2,1)S(1)} %get-tuple-element.30.hidden_ref), custom_call_target="tpu_custom_call" | custom-call | bytes 1048576 | tf_op jit(solution)/shard_map/pallas_call | solution.py:54
  40.9 3.6 %all-to-all-start.1 = ((bf16[8,64,256]{2,1,0:T(8,128)(2,1)}), bf16[8,64,256]{2,1,0:T(8,128)(2,1)S(1)}, u32[]{:S(2)}, u32[]{:S(2)}) async-start(bf16[8,64,256]{2,1,0:T(8,128)(2,1)} %shard_map.152), calls=%async_computation.1 | async-start | bytes 524288 | tf_op jit(solution)/shard_map/all_to_all | solution.py:664
  44.6 0.0 copy-done.6
  44.6 0.0 copy-done
  44.6 0.0 copy-start.4
  44.6 2.2 %shard_map.153.fixed_ref = f32[2,512,384]{2,1,0:T(8,128)S(1)} custom-call(bf16[8,176,128]{2,1,0:T(8,128)(2,1)S(1)} %all-to-all-done.first_ref.early_ref, bf16[2,5,384,256]{3,2,1,0:T(8,128)(2,1)} %gate_hbm.3, bf16[2,5,384,128]{3,2,1,0:T(8,128)(2,1)} %state_hbm.3, f32[2,384]{1,0:T(2,128)S(1)} %copy-done), custom_call_target="tpu_custom_call" | custom-call | flops 503316480 | bytes 4194304 | tf_op jit(solution)/shard_map/pallas_call | solution.py:54
  46.8 7.0 %all-to-all-done.1.got_ref = bf16[8,64,256]{2,1,0:T(8,128)(2,1)S(1)} async-done(((bf16[8,64,256]{2,1,0:T(8,128)(2,1)}), bf16[8,64,256]{2,1,0:T(8,128)(2,1)S(1)}, u32[]{:S(2)}, u32[]{:S(2)}) %all-to-all-start.1) | async-done | bytes 262176 | tf_op jit(solution)/shard_map/all_to_all | solution.py:664
  53.8 0.0 copy-done.4
  53.8 7.6 %shard_map.154 = f32[8,40,128]{2,1,0:T(8,128)S(1)} custom-call(bf16[8,64,256]{2,1,0:T(8,128)(2,1)S(1)} %all-to-all-done.1.got_ref, f32[2,512,384]{2,1,0:T(8,128)S(1)} %shard_map.153.fixed_ref, f32[8,128]{1,0:T(8,128)S(1)} %pad.8.ow_ref, bf16[2,5,384,256]{3,2,1,0:T(8,128)(2,1)} %gate_hbm.3, bf16[2,5,384,128]{3,2,1,0:T(8,128)(2,1)} %state_hbm.3, ...), custom_call_target="tpu_custom_call" | custom-call | flops 2013265920 | bytes 4194304 | tf_op jit(solution)/shard_map/pallas_call | solution.py:54
  61.5 10.9 %all_to_all.15.mine_ref = f32[8,40,128]{2,1,0:T(8,128)S(1)} all-to-all(f32[8,40,128]{2,1,0:T(8,128)S(1)} %shard_map.154), channel_id=1, replica_groups=mesh['groups'=2,'rows'=8,'loop'=2] {'rows'}, dimensions={0} | all-to-all | bytes 327680 | tf_op jit(solution)/shard_map/all_to_all | solution.py:721
  72.4 0.0 collective-permute-start.9
  72.4 1.4 %collective-permute-done.9.other_ref = f32[8,40,128]{2,1,0:T(8,128)S(1)} collective-permute-done((f32[8,40,128]{2,1,0:T(8,128)S(1)}, f32[8,40,128]{2,1,0:T(8,128)S(1)}, u32[]{:S(2)}, u32[]{:S(2)}) %collective-permute-start.9) | collective-permute-done | bytes 163872 | tf_op jit(solution)/shard_map/ppermute | solution.py:733
  73.8 0.7 shard_map.155
  (2 shorter events, 0.0 us)
Async XLA Ops:
  0.6 27.1 %copy-start.3 = (bf16[2,128,256]{2,1,0:T(8,128)(2,1)S(1)}, bf16[2,128,256]{2,1,0:T(8,128)(2,1)}, u32[]{:S(2)}) copy-start(bf16[2,128,256]{2,1,0:T(8,128)(2,1)} %param.15) | copy-start | bytes 393220
  0.6 27.0 %copy-start.5 = (f32[6,128]{1,0:T(8,128)S(1)}, f32[6,128]{1,0:T(8,128)}, u32[]{:S(2)}) copy-start(f32[6,128]{1,0:T(8,128)} %param.22) | copy-start | bytes 9220
  0.7 27.1 %copy-start.1 = (bf16[2,256,256]{2,1,0:T(8,128)(2,1)S(1)}, bf16[2,256,256]{2,1,0:T(8,128)(2,1)}, u32[]{:S(2)}) copy-start(bf16[2,256,256]{2,1,0:T(8,128)(2,1)} %param.14) | copy-start | bytes 786436
  0.7 27.1 %copy-start.2 = (bf16[512,128]{1,0:T(8,128)(2,1)S(1)}, bf16[512,128]{1,0:T(8,128)(2,1)}, u32[]{:S(2)}) copy-start(bf16[512,128]{1,0:T(8,128)(2,1)} %weight_ref.1) | copy-start | bytes 393220
  0.7 8.1 %collective-permute-start = (bf16[1,2,128,256]{3,2,1,0:T(8,128)(2,1)}, bf16[1,2,128,256]{3,2,1,0:T(8,128)(2,1)S(1)}, u32[]{:S(2)}, u32[]{:S(2)}) collective-permute-start(bf16[1,2,128,256]{3,2,1,0:T(8,128)(2,1)} %bitcast.5), channel_id=1, source_target_pairs={{0,2},{2,0},{4,6},{6,4},{8,10},{10,8},{12,14},{14,12},{1,3},{3,1},... | collective-permute-start | bytes 393224 | tf_op jit(solution)/shard_map/ppermute | solution.py:582
  3.7 12.9 %collective-permute-start.1 = (bf16[1,2,128,256]{3,2,1,0:T(8,128)(2,1)}, bf16[1,2,128,256]{3,2,1,0:T(8,128)(2,1)S(1)}, u32[]{:S(2)}, u32[]{:S(2)}) collective-permute-start(bf16[1,2,128,256]{3,2,1,0:T(8,128)(2,1)} %bitcast.6), channel_id=1, source_target_pairs={{0,8},{2,10},{4,12},{6,14},{8,0},{10,2},{12,4},{14,6},{1,9},{3,11}... | collective-permute-start | bytes 393224 | tf_op jit(solution)/shard_map/ppermute | solution.py:582
  6.3 13.1 %collective-permute-start.2 = (bf16[1,2,128,256]{3,2,1,0:T(8,128)(2,1)}, bf16[1,2,128,256]{3,2,1,0:T(8,128)(2,1)S(1)}, u32[]{:S(2)}, u32[]{:S(2)}) collective-permute-start(bf16[1,2,128,256]{3,2,1,0:T(8,128)(2,1)} %bitcast.7), channel_id=1, source_target_pairs={{0,4},{2,6},{4,0},{6,2},{8,12},{10,14},{12,8},{14,10},{1,5},{3,7},... | collective-permute-start | bytes 393224 | tf_op jit(solution)/shard_map/ppermute | solution.py:582
  7.9 11.5 %collective-permute-start.3 = (bf16[1,2,128,256]{3,2,1,0:T(8,128)(2,1)}, bf16[1,2,128,256]{3,2,1,0:T(8,128)(2,1)S(1)}, u32[]{:S(2)}, u32[]{:S(2)}) collective-permute-start(bf16[1,2,128,256]{3,2,1,0:T(8,128)(2,1)} %bitcast.8), channel_id=1, source_target_pairs={{0,12},{2,14},{4,8},{6,10},{8,4},{10,6},{12,0},{14,2},{1,13},{3,15... | collective-permute-start | bytes 393224 | tf_op jit(solution)/shard_map/ppermute | solution.py:582
  16.6 6.0 %collective-permute-start.4 = (bf16[1,2,128,256]{3,2,1,0:T(8,128)(2,1)S(1)}, bf16[1,2,128,256]{3,2,1,0:T(8,128)(2,1)S(1)}, u32[]{:S(2)}, u32[]{:S(2)}) collective-permute-start(bf16[1,2,128,256]{3,2,1,0:T(8,128)(2,1)S(1)} %collective-permute-done.refs_1_), channel_id=1, source_target_pairs={{0,4},{2,6},{4,0},{6,2},{8,12},{10,14},{12,8},{14,10},{1,5},{3,7},... | collective-permute-start | bytes 393224 | tf_op jit(solution)/shard_map/ppermute | solution.py:582
  16.6 7.4 %collective-permute-start.5 = (bf16[1,2,128,256]{3,2,1,0:T(8,128)(2,1)S(1)}, bf16[1,2,128,256]{3,2,1,0:T(8,128)(2,1)S(1)}, u32[]{:S(2)}, u32[]{:S(2)}) collective-permute-start(bf16[1,2,128,256]{3,2,1,0:T(8,128)(2,1)S(1)} %collective-permute-done.refs_1_), channel_id=1, source_target_pairs={{0,12},{2,14},{4,8},{6,10},{8,4},{10,6},{12,0},{14,2},{1,13},{3,15... | collective-permute-start | bytes 393224 | tf_op jit(solution)/shard_map/ppermute | solution.py:582
  18.9 5.1 %collective-permute-start.6 = (bf16[1,2,128,256]{3,2,1,0:T(8,128)(2,1)S(1)}, bf16[1,2,128,256]{3,2,1,0:T(8,128)(2,1)S(1)}, u32[]{:S(2)}, u32[]{:S(2)}) collective-permute-start(bf16[1,2,128,256]{3,2,1,0:T(8,128)(2,1)S(1)} %collective-permute-done.1.refs_4_), channel_id=1, source_target_pairs={{0,2},{2,0},{4,6},{6,4},{8,10},{10,8},{12,14},{14,12},{1,3},{3,1},... | collective-permute-start | bytes 393224 | tf_op jit(solution)/shard_map/ppermute | solution.py:582
  24.0 12.8 %all-to-all-start = ((bf16[8,176,128]{2,1,0:T(8,128)(2,1)}), bf16[8,176,128]{2,1,0:T(8,128)(2,1)S(1)}, u32[]{:S(2)}, u32[]{:S(2)}) async-start(bf16[8,176,128]{2,1,0:T(8,128)(2,1)} %shard_map.149), calls=%async_computation | async-start | bytes 720896 | tf_op jit(solution)/shard_map/all_to_all | solution.py:611
  33.3 11.3 %copy-start.6 = (bf16[2,256]{1,0:T(2,128)(2,1)S(1)}, bf16[2,256]{1,0:T(2,128)(2,1)}, u32[]{:S(2)}) copy-start(bf16[2,256]{1,0:T(2,128)(2,1)} %param.27) | copy-start | bytes 3076
  33.3 11.3 %copy-start = (f32[2,384]{1,0:T(2,128)S(1)}, f32[2,384]{1,0:T(2,128)}, u32[]{:S(2)}) copy-start(f32[2,384]{1,0:T(2,128)} %bias_ref.1) | copy-start | bytes 9220
  33.3 6.8 %collective-permute-start.7 = (f32[2,144,384]{2,1,0:T(8,128)S(1)}, f32[2,144,384]{2,1,0:T(8,128)S(1)}, u32[]{:S(2)}, u32[]{:S(2)}) collective-permute-start(f32[2,144,384]{2,1,0:T(8,128)S(1)} %get-tuple-element.27), channel_id=1, source_target_pairs={{0,1},{1,0},{2,3},{3,2},{4,5},{5,4},{6,7},{7,6},{8,9},{9,8},{10,11... | collective-permute-start | bytes 1327112 | tf_op jit(solution)/shard_map/ppermute | solution.py:651
  36.8 1.7 %collective-permute-start.8 = (bf16[8,176,128]{2,1,0:T(8,128)(2,1)S(1)}, bf16[8,176,128]{2,1,0:T(8,128)(2,1)S(1)}, u32[]{:S(2)}, u32[]{:S(2)}) collective-permute-start(bf16[8,176,128]{2,1,0:T(8,128)(2,1)S(1)} %all-to-all-done.first_ref.early_ref), channel_id=1, source_target_pairs={{0,1},{1,0},{2,3},{3,2},{4,5},{5,4},{6,7},{7,6},{8,9},{9,8},{10,11... | collective-permute-start | bytes 1081352 | tf_op jit(solution)/shard_map/ppermute | solution.py:613
  40.9 12.9 %all-to-all-start.1 = ((bf16[8,64,256]{2,1,0:T(8,128)(2,1)}), bf16[8,64,256]{2,1,0:T(8,128)(2,1)S(1)}, u32[]{:S(2)}, u32[]{:S(2)}) async-start(bf16[8,64,256]{2,1,0:T(8,128)(2,1)} %shard_map.152), calls=%async_computation.1 | async-start | bytes 524288 | tf_op jit(solution)/shard_map/all_to_all | solution.py:664
  44.6 9.2 %copy-start.4 = (bf16[128,256]{1,0:T(8,128)(2,1)S(1)}, bf16[128,256]{1,0:T(8,128)(2,1)}, u32[]{:S(2)}) copy-start(bf16[128,256]{1,0:T(8,128)(2,1)} %head_ref.1) | copy-start | bytes 196612
  72.4 1.4 %collective-permute-start.9 = (f32[8,40,128]{2,1,0:T(8,128)S(1)}, f32[8,40,128]{2,1,0:T(8,128)S(1)}, u32[]{:S(2)}, u32[]{:S(2)}) collective-permute-start(f32[8,40,128]{2,1,0:T(8,128)S(1)} %all_to_all.15.mine_ref), channel_id=1, source_target_pairs={{0,1},{1,0},{2,3},{3,2},{4,5},{5,4},{6,7},{7,6},{8,9},{9,8},{10,11... | collective-permute-start | bytes 491528 | tf_op jit(solution)/shard_map/ppermute | solution.py:733

commit v7 on v6

--- a/solution.py
+++ b/solution.py
@@ -119,15 +119,10 @@
             out_ref[j, top + r * WIN : top + (r + 1) * WIN, :] = part[j * own : j * own + WIN].astype(BF16)
 
 
-def place_kernel(cap, half_wide, rows_per, first_ref, second_ref, ow_ref, hidden_ref, flow_ref, term_ref, wide_hidden, wide_term):
-    half = lax.axis_index("loop")
-    dests = first_ref.shape[0]
-    pixels = flow_ref.shape[1]
-    width = pixels // rows_per
+def gather_slots(cap, got_ref, hidden, flow):
     rows_hidden = round_up(cap, 16)
-    hidden = jnp.zeros((pixels, 128), F32)
-    flow = jnp.zeros((8, pixels), F32)
-    for j, got_ref in [(j, ref) for j in range(dests) for ref in (first_ref, second_ref)]:
+    pixels = flow.shape[1]
+    for j in range(got_ref.shape[0]):
         pieces = []
         for t in range(-(-cap // 128)):
             base = rows_hidden + 8 * t
@@ -137,6 +132,19 @@
         chosen = jnp.where(iota((pixels, cap), 0) == place, 1.0, 0.0).astype(BF16)
         hidden = hidden + dot(chosen, got_ref[j, 0:cap, :])
         flow = flow + dot_nt(side.astype(BF16), chosen)
+    return hidden, flow
+
+
+def own_slots_kernel(cap, got_ref, hidden_ref, flow_ref):
+    zeros = jnp.zeros(hidden_ref.shape, F32), jnp.zeros(flow_ref.shape, F32)
+    hidden_ref[...], flow_ref[...] = gather_slots(cap, got_ref, *zeros)
+
+
+def place_kernel(cap, half_wide, rows_per, got_ref, part_ref, flow_part_ref, ow_ref, hidden_ref, flow_ref, term_ref, wide_hidden, wide_term):
+    half = lax.axis_index("loop")
+    pixels = flow_ref.shape[1]
+    width = pixels // rows_per
+    hidden, flow = gather_slots(cap, got_ref, part_ref[...], flow_part_ref[...])
     flow_ref[...] = flow
     columns = flow.T
     ow = ow_ref[...]
@@ -612,6 +620,15 @@
     around = [(i, (i + 1) % halves) for i in range(halves)]
     early_other = lax.ppermute(early, "loop", around)
     ow = jnp.pad(offset_weight, ((0, 2), (0, 0)))
+    hidden_part, flow_part = call(
+        functools.partial(own_slots_kernel, cap),
+        (jax.ShapeDtypeStruct((pixels, 128), F32), jax.ShapeDtypeStruct((8, pixels), F32)),
+        vmem_specs(1),
+        [],
+        (slots * pixels * 128, 1 << 20, 0),
+        room,
+        early,
+    )
     hidden_wide, flow_first, term = call(
         functools.partial(place_kernel, cap, half_wide, rows_per),
         (
@@ -619,12 +636,13 @@
             jax.ShapeDtypeStruct((8, pixels), F32),
             jax.ShapeDtypeStruct((rows_per, half_wide, 128), F32),
         ),
-        vmem_specs(3),
+        vmem_specs(4),
         [pltpu.VMEM((rows_per, padded, 128), F32)] * 2,
-        (2 * slots * pixels * 128, 1 << 20, 0),
+        (slots * pixels * 128, 1 << 20, 0),
         room,
-        early,
         early_other,
+        hidden_part,
+        flow_part,
         ow,
     )
     queries = frame_one.reshape(pixels, channels)

time: 75 us -> 74.4 us (level)
    pallas_call x7 -> x8, Pallas kernels: 22.5 us -> 22.6 us  [call(): pl.pallas_call(kernel, out_shape=out_shape, in_specs=in_specs, out_specs=...]
where the time goes in v7:
time: 74.4 us; the launch traced here: 74 us
  Pallas kernels  22.6 us (30%)
  waiting for transfers between devices  21.4 us (29%)
  starting transfers between devices  17.6 us (24%)
  blocking collectives  10.9 us (15%)
  between operations  1.46 us (2%)
    pallas_call x8, Pallas kernels, call(): pl.pallas_call(kernel, out_shape=out_shape, in_specs=in_specs, out_specs=...  22.6 us
    all_to_all x1, blocking collectives, local(): back = lax.all_to_all(outgoing, 'rows', 0, 0, tiled=True)  10.9 us
    ppermute x7, starting transfers between devices, swap(): return lax.ppermute(value, 'rows', [(i, i ^ flip) for i in range(dests)])  10.2 us
    ppermute x7, waiting for transfers between devices, swap(): return lax.ppermute(value, 'rows', [(i, i ^ flip) for i in range(dests)])  8.55 us
    all_to_all x1, waiting for transfers between devices, local(): arrived = lax.all_to_all(sending, 'rows', 0, 0, tiled=True)  6.99 us
    all_to_all x1, starting transfers between devices, local(): early = lax.all_to_all(packed, 'rows', 0, 0, tiled=True)  3.66 us
    all_to_all x1, starting transfers between devices, local(): arrived = lax.all_to_all(sending, 'rows', 0, 0, tiled=True)  3.64 us
    all_to_all x1, waiting for transfers between devices, local(): early = lax.all_to_all(packed, 'rows', 0, 0, tiled=True)  3.42 us
  transfers between devices with their start and end apart: 12, of which 7 were waited for; matrix products, arithmetic and copies ran while one was open for 0% of the time, Pallas kernels for 18%

profile of v7, /device:TPU:0, one launch (start us, length us, event | category | flops | bytes accessed | tf_op | source)
XLA Modules:
  0.0 74.0 jit_solution(6735861587360582153)
XLA Ops:
  0.6 0.0 copy-start.3
  0.6 0.0 copy-start.5
  0.7 0.0 copy-start.1
  0.7 0.0 copy-start.2
  0.7 3.0 %collective-permute-start = (bf16[1,2,128,256]{3,2,1,0:T(8,128)(2,1)}, bf16[1,2,128,256]{3,2,1,0:T(8,128)(2,1)S(1)}, u32[]{:S(2)}, u32[]{:S(2)}) collective-permute-start(bf16[1,2,128,256]{3,2,1,0:T(8,128)(2,1)} %bitcast.5), channel_id=1, source_target_pairs={{0,2},{2,0},{4,6},{6,4},{8,10},{10,8},{12,14},{14,12},{1,3},{3,1},... | collective-permute-start | bytes 393224 | tf_op jit(solution)/shard_map/ppermute | solution.py:590
  3.7 2.6 %collective-permute-start.1 = (bf16[1,2,128,256]{3,2,1,0:T(8,128)(2,1)}, bf16[1,2,128,256]{3,2,1,0:T(8,128)(2,1)S(1)}, u32[]{:S(2)}, u32[]{:S(2)}) collective-permute-start(bf16[1,2,128,256]{3,2,1,0:T(8,128)(2,1)} %bitcast.6), channel_id=1, source_target_pairs={{0,8},{2,10},{4,12},{6,14},{8,0},{10,2},{12,4},{14,6},{1,9},{3,11}... | collective-permute-start | bytes 393224 | tf_op jit(solution)/shard_map/ppermute | solution.py:590
  6.3 1.6 %collective-permute-start.2 = (bf16[1,2,128,256]{3,2,1,0:T(8,128)(2,1)}, bf16[1,2,128,256]{3,2,1,0:T(8,128)(2,1)S(1)}, u32[]{:S(2)}, u32[]{:S(2)}) collective-permute-start(bf16[1,2,128,256]{3,2,1,0:T(8,128)(2,1)} %bitcast.7), channel_id=1, source_target_pairs={{0,4},{2,6},{4,0},{6,2},{8,12},{10,14},{12,8},{14,10},{1,5},{3,7},... | collective-permute-start | bytes 393224 | tf_op jit(solution)/shard_map/ppermute | solution.py:590
  7.9 0.2 collective-permute-start.3
  8.7 0.0 collective-permute-done.refs_1_
  8.8 3.9 %shard_map.149 = bf16[8,176,128]{2,1,0:T(8,128)(2,1)} custom-call(s32[1]{0:T(128)S(6)} %copy.16.count_ref, s32[12,128]{1,0:T(8,128)} %bitcast.10, bf16[2,1536]{1,0:T(2,128)(2,1)} %bitcast.11, bf16[1536,128]{1,0:T(8,128)(2,1)} %hidden_ref.1, bf16[2,256,128]{2,1,0:T(8,128)(2,1)} %context_ref.1), custom_call_target="tpu_custom_call" | custom-call | flops 603979776 | bytes 1048576 | tf_op jit(solution)/shard_map/pallas_call | solution.py:54
  12.7 3.9 %collective-permute-done.1.refs_4_ = bf16[1,2,128,256]{3,2,1,0:T(8,128)(2,1)S(1)} collective-permute-done((bf16[1,2,128,256]{3,2,1,0:T(8,128)(2,1)}, bf16[1,2,128,256]{3,2,1,0:T(8,128)(2,1)S(1)}, u32[]{:S(2)}, u32[]{:S(2)}) %collective-permute-start.1) | collective-permute-done | bytes 131104 | tf_op jit(solution)/shard_map/ppermute | solution.py:590
  16.6 0.0 collective-permute-start.4
  16.6 2.3 %collective-permute-start.5 = (bf16[1,2,128,256]{3,2,1,0:T(8,128)(2,1)S(1)}, bf16[1,2,128,256]{3,2,1,0:T(8,128)(2,1)S(1)}, u32[]{:S(2)}, u32[]{:S(2)}) collective-permute-start(bf16[1,2,128,256]{3,2,1,0:T(8,128)(2,1)S(1)} %collective-permute-done.refs_1_), channel_id=1, source_target_pairs={{0,12},{2,14},{4,8},{6,10},{8,4},{10,6},{12,0},{14,2},{1,13},{3,15... | collective-permute-start | bytes 393224 | tf_op jit(solution)/shard_map/ppermute | solution.py:590
  18.9 0.5 collective-permute-start.6
  19.4 0.0 collective-permute-done.2.refs_2_
  19.4 0.0 collective-permute-done.3.refs_6_
  19.4 3.2 %collective-permute-done.4.refs_3_ = bf16[1,2,128,256]{3,2,1,0:T(8,128)(2,1)S(1)} collective-permute-done((bf16[1,2,128,256]{3,2,1,0:T(8,128)(2,1)S(1)}, bf16[1,2,128,256]{3,2,1,0:T(8,128)(2,1)S(1)}, u32[]{:S(2)}, u32[]{:S(2)}) %collective-permute-start.4) | collective-permute-done | bytes 131104 | tf_op jit(solution)/shard_map/ppermute | solution.py:590
  22.6 1.4 %collective-permute-done.5.refs_7_ = bf16[1,2,128,256]{3,2,1,0:T(8,128)(2,1)S(1)} collective-permute-done((bf16[1,2,128,256]{3,2,1,0:T(8,128)(2,1)S(1)}, bf16[1,2,128,256]{3,2,1,0:T(8,128)(2,1)S(1)}, u32[]{:S(2)}, u32[]{:S(2)}) %collective-permute-start.5) | collective-permute-done | bytes 131104 | tf_op jit(solution)/shard_map/ppermute | solution.py:590
  24.0 0.0 collective-permute-done.6.refs_5_
  24.0 3.7 %all-to-all-start = ((bf16[8,176,128]{2,1,0:T(8,128)(2,1)}), bf16[8,176,128]{2,1,0:T(8,128)(2,1)S(1)}, u32[]{:S(2)}, u32[]{:S(2)}) async-start(bf16[8,176,128]{2,1,0:T(8,128)(2,1)} %shard_map.149), calls=%async_computation | async-start | bytes 720896 | tf_op jit(solution)/shard_map/all_to_all | solution.py:619
  27.7 0.0 copy-done.5
  27.7 0.0 copy-done.3
  27.7 0.0 copy-done.1
  27.7 0.0 copy-done.2
  27.7 5.5 %shard_map.150 = (f32[2,144,384]{2,1,0:T(8,128)S(1)}, f32[2,144,384]{2,1,0:T(8,128)S(1)}) custom-call(bf16[512,256]{1,0:T(8,128)(2,1)S(1)} %bitcast.4, bf16[512,128]{1,0:T(8,128)(2,1)S(1)} %copy-done.2, f32[8,128]{1,0:T(8,128)S(1)} %pad.8.ow_ref, bf16[1,2,128,256]{3,2,1,0:T(8,128)(2,1)S(1)} %bitcast.9, ...), custom_call_target="tpu_custom_call" | custom-call | flops 1073741824 | bytes 2097152 | tf_op jit(solution)/shard_map/pallas_call | solution.py:54
  33.3 0.0 copy-start.6
  33.3 0.0 copy-start
  33.3 0.1 collective-permute-start.7
  33.4 3.4 %all-to-all-done.got_ref.early_ref = bf16[8,176,128]{2,1,0:T(8,128)(2,1)S(1)} async-done(((bf16[8,176,128]{2,1,0:T(8,128)(2,1)}), bf16[8,176,128]{2,1,0:T(8,128)(2,1)S(1)}, u32[]{:S(2)}, u32[]{:S(2)}) %all-to-all-start) | async-done | bytes 360480 | tf_op jit(solution)/shard_map/all_to_all | solution.py:619
  36.8 0.0 collective-permute-start.8
  36.8 0.7 shard_map.151
  37.5 1.0 %collective-permute-done.8.got_ref = bf16[8,176,128]{2,1,0:T(8,128)(2,1)S(1)} collective-permute-done((bf16[8,176,128]{2,1,0:T(8,128)(2,1)S(1)}, bf16[8,176,128]{2,1,0:T(8,128)(2,1)S(1)}, u32[]{:S(2)}, u32[]{:S(2)}) %collective-permute-start.8) | collective-permute-done | bytes 360480 | tf_op jit(solution)/shard_map/ppermute | solution.py:621
  38.5 1.0 %shard_map.152 = (bf16[2,144,128]{2,1,0:T(8,128)(2,1)S(1)}, f32[8,512]{1,0:T(8,128)S(1)}, f32[2,144,128]{2,1,0:T(8,128)S(1)}) custom-call(bf16[8,176,128]{2,1,0:T(8,128)(2,1)S(1)} %collective-permute-done.8.got_ref, f32[512,128]{1,0:T(8,128)S(1)} %get-tuple-element.31.part_ref, f32[8,512]{1,0:T(8,128)S(1)} %get-tuple-element.32.flow_part_ref, ...), custom_call_target="tpu_custom_call" | custom-call | flops 100663296 | bytes 1048576 | tf_op jit(solution)/shard_map/pallas_call | solution.py:54
  39.5 0.0 collective-permute-done.7.got_ref
  39.5 0.9 %shard_map.153 = bf16[8,64,256]{2,1,0:T(8,128)(2,1)} custom-call(f32[2,144,384]{2,1,0:T(8,128)S(1)} %get-tuple-element.28.keep_ref, f32[2,144,384]{2,1,0:T(8,128)S(1)} %collective-permute-done.7.got_ref, f32[2,144,128]{2,1,0:T(8,128)S(1)} %get-tuple-element.33.term_ref, bf16[2,144,128]{2,1,0:T(8,128)(2,1)S(1)} %get-tuple-element.34.hidden_ref), custom_call_target="tpu_custom_call" | custom-call | bytes 1048576 | tf_op jit(solution)/shard_map/pallas_call | solution.py:54
  40.4 3.6 %all-to-all-start.1 = ((bf16[8,64,256]{2,1,0:T(8,128)(2,1)}), bf16[8,64,256]{2,1,0:T(8,128)(2,1)S(1)}, u32[]{:S(2)}, u32[]{:S(2)}) async-start(bf16[8,64,256]{2,1,0:T(8,128)(2,1)} %shard_map.153), calls=%async_computation.1 | async-start | bytes 524288 | tf_op jit(solution)/shard_map/all_to_all | solution.py:682
  44.0 0.0 copy-done.6
  44.1 0.0 copy-done
  44.1 0.0 copy-start.4
  44.1 2.2 %shard_map.154.fixed_ref = f32[2,512,384]{2,1,0:T(8,128)S(1)} custom-call(bf16[8,176,128]{2,1,0:T(8,128)(2,1)S(1)} %all-to-all-done.got_ref.early_ref, bf16[2,5,384,256]{3,2,1,0:T(8,128)(2,1)} %gate_hbm.3, bf16[2,5,384,128]{3,2,1,0:T(8,128)(2,1)} %state_hbm.3, f32[2,384]{1,0:T(2,128)S(1)} %copy-done), custom_call_target="tpu_custom_call" | custom-call | flops 503316480 | bytes 4194304 | tf_op jit(solution)/shard_map/pallas_call | solution.py:54
  46.3 7.0 %all-to-all-done.1.got_ref = bf16[8,64,256]{2,1,0:T(8,128)(2,1)S(1)} async-done(((bf16[8,64,256]{2,1,0:T(8,128)(2,1)}), bf16[8,64,256]{2,1,0:T(8,128)(2,1)S(1)}, u32[]{:S(2)}, u32[]{:S(2)}) %all-to-all-start.1) | async-done | bytes 262176 | tf_op jit(solution)/shard_map/all_to_all | solution.py:682
  53.3 0.0 copy-done.4
  53.3 7.6 %shard_map.155 = f32[8,40,128]{2,1,0:T(8,128)S(1)} custom-call(bf16[8,64,256]{2,1,0:T(8,128)(2,1)S(1)} %all-to-all-done.1.got_ref, f32[2,512,384]{2,1,0:T(8,128)S(1)} %shard_map.154.fixed_ref, f32[8,128]{1,0:T(8,128)S(1)} %pad.8.ow_ref, bf16[2,5,384,256]{3,2,1,0:T(8,128)(2,1)} %gate_hbm.3, bf16[2,5,384,128]{3,2,1,0:T(8,128)(2,1)} %state_hbm.3, ...), custom_call_target="tpu_custom_call" | custom-call | flops 2013265920 | bytes 4194304 | tf_op jit(solution)/shard_map/pallas_call | solution.py:54
  60.9 10.9 %all_to_all.15.mine_ref = f32[8,40,128]{2,1,0:T(8,128)S(1)} all-to-all(f32[8,40,128]{2,1,0:T(8,128)S(1)} %shard_map.155), channel_id=1, replica_groups=mesh['groups'=2,'rows'=8,'loop'=2] {'rows'}, dimensions={0} | all-to-all | bytes 327680 | tf_op jit(solution)/shard_map/all_to_all | solution.py:739
  71.9 0.0 collective-permute-start.9
  71.9 1.4 %collective-permute-done.9.other_ref = f32[8,40,128]{2,1,0:T(8,128)S(1)} collective-permute-done((f32[8,40,128]{2,1,0:T(8,128)S(1)}, f32[8,40,128]{2,1,0:T(8,128)S(1)}, u32[]{:S(2)}, u32[]{:S(2)}) %collective-permute-start.9) | collective-permute-done | bytes 163872 | tf_op jit(solution)/shard_map/ppermute | solution.py:751
  73.3 0.7 shard_map.156
  (2 shorter events, 0.0 us)
Async XLA Ops:
  0.6 27.1 %copy-start.3 = (bf16[2,128,256]{2,1,0:T(8,128)(2,1)S(1)}, bf16[2,128,256]{2,1,0:T(8,128)(2,1)}, u32[]{:S(2)}) copy-start(bf16[2,128,256]{2,1,0:T(8,128)(2,1)} %param.15) | copy-start | bytes 393220
  0.6 27.0 %copy-start.5 = (f32[6,128]{1,0:T(8,128)S(1)}, f32[6,128]{1,0:T(8,128)}, u32[]{:S(2)}) copy-start(f32[6,128]{1,0:T(8,128)} %param.22) | copy-start | bytes 9220
  0.7 27.1 %copy-start.1 = (bf16[2,256,256]{2,1,0:T(8,128)(2,1)S(1)}, bf16[2,256,256]{2,1,0:T(8,128)(2,1)}, u32[]{:S(2)}) copy-start(bf16[2,256,256]{2,1,0:T(8,128)(2,1)} %param.14) | copy-start | bytes 786436
  0.7 27.1 %copy-start.2 = (bf16[512,128]{1,0:T(8,128)(2,1)S(1)}, bf16[512,128]{1,0:T(8,128)(2,1)}, u32[]{:S(2)}) copy-start(bf16[512,128]{1,0:T(8,128)(2,1)} %weight_ref.1) | copy-start | bytes 393220
  0.7 8.1 %collective-permute-start = (bf16[1,2,128,256]{3,2,1,0:T(8,128)(2,1)}, bf16[1,2,128,256]{3,2,1,0:T(8,128)(2,1)S(1)}, u32[]{:S(2)}, u32[]{:S(2)}) collective-permute-start(bf16[1,2,128,256]{3,2,1,0:T(8,128)(2,1)} %bitcast.5), channel_id=1, source_target_pairs={{0,2},{2,0},{4,6},{6,4},{8,10},{10,8},{12,14},{14,12},{1,3},{3,1},... | collective-permute-start | bytes 393224 | tf_op jit(solution)/shard_map/ppermute | solution.py:590
  3.7 12.9 %collective-permute-start.1 = (bf16[1,2,128,256]{3,2,1,0:T(8,128)(2,1)}, bf16[1,2,128,256]{3,2,1,0:T(8,128)(2,1)S(1)}, u32[]{:S(2)}, u32[]{:S(2)}) collective-permute-start(bf16[1,2,128,256]{3,2,1,0:T(8,128)(2,1)} %bitcast.6), channel_id=1, source_target_pairs={{0,8},{2,10},{4,12},{6,14},{8,0},{10,2},{12,4},{14,6},{1,9},{3,11}... | collective-permute-start | bytes 393224 | tf_op jit(solution)/shard_map/ppermute | solution.py:590
  6.3 13.1 %collective-permute-start.2 = (bf16[1,2,128,256]{3,2,1,0:T(8,128)(2,1)}, bf16[1,2,128,256]{3,2,1,0:T(8,128)(2,1)S(1)}, u32[]{:S(2)}, u32[]{:S(2)}) collective-permute-start(bf16[1,2,128,256]{3,2,1,0:T(8,128)(2,1)} %bitcast.7), channel_id=1, source_target_pairs={{0,4},{2,6},{4,0},{6,2},{8,12},{10,14},{12,8},{14,10},{1,5},{3,7},... | collective-permute-start | bytes 393224 | tf_op jit(solution)/shard_map/ppermute | solution.py:590
  7.9 11.5 %collective-permute-start.3 = (bf16[1,2,128,256]{3,2,1,0:T(8,128)(2,1)}, bf16[1,2,128,256]{3,2,1,0:T(8,128)(2,1)S(1)}, u32[]{:S(2)}, u32[]{:S(2)}) collective-permute-start(bf16[1,2,128,256]{3,2,1,0:T(8,128)(2,1)} %bitcast.8), channel_id=1, source_target_pairs={{0,12},{2,14},{4,8},{6,10},{8,4},{10,6},{12,0},{14,2},{1,13},{3,15... | collective-permute-start | bytes 393224 | tf_op jit(solution)/shard_map/ppermute | solution.py:590
  16.6 6.0 %collective-permute-start.4 = (bf16[1,2,128,256]{3,2,1,0:T(8,128)(2,1)S(1)}, bf16[1,2,128,256]{3,2,1,0:T(8,128)(2,1)S(1)}, u32[]{:S(2)}, u32[]{:S(2)}) collective-permute-start(bf16[1,2,128,256]{3,2,1,0:T(8,128)(2,1)S(1)} %collective-permute-done.refs_1_), channel_id=1, source_target_pairs={{0,4},{2,6},{4,0},{6,2},{8,12},{10,14},{12,8},{14,10},{1,5},{3,7},... | collective-permute-start | bytes 393224 | tf_op jit(solution)/shard_map/ppermute | solution.py:590
  16.6 7.4 %collective-permute-start.5 = (bf16[1,2,128,256]{3,2,1,0:T(8,128)(2,1)S(1)}, bf16[1,2,128,256]{3,2,1,0:T(8,128)(2,1)S(1)}, u32[]{:S(2)}, u32[]{:S(2)}) collective-permute-start(bf16[1,2,128,256]{3,2,1,0:T(8,128)(2,1)S(1)} %collective-permute-done.refs_1_), channel_id=1, source_target_pairs={{0,12},{2,14},{4,8},{6,10},{8,4},{10,6},{12,0},{14,2},{1,13},{3,15... | collective-permute-start | bytes 393224 | tf_op jit(solution)/shard_map/ppermute | solution.py:590
  18.9 5.1 %collective-permute-start.6 = (bf16[1,2,128,256]{3,2,1,0:T(8,128)(2,1)S(1)}, bf16[1,2,128,256]{3,2,1,0:T(8,128)(2,1)S(1)}, u32[]{:S(2)}, u32[]{:S(2)}) collective-permute-start(bf16[1,2,128,256]{3,2,1,0:T(8,128)(2,1)S(1)} %collective-permute-done.1.refs_4_), channel_id=1, source_target_pairs={{0,2},{2,0},{4,6},{6,4},{8,10},{10,8},{12,14},{14,12},{1,3},{3,1},... | collective-permute-start | bytes 393224 | tf_op jit(solution)/shard_map/ppermute | solution.py:590
  24.0 12.8 %all-to-all-start = ((bf16[8,176,128]{2,1,0:T(8,128)(2,1)}), bf16[8,176,128]{2,1,0:T(8,128)(2,1)S(1)}, u32[]{:S(2)}, u32[]{:S(2)}) async-start(bf16[8,176,128]{2,1,0:T(8,128)(2,1)} %shard_map.149), calls=%async_computation | async-start | bytes 720896 | tf_op jit(solution)/shard_map/all_to_all | solution.py:619
  33.3 10.8 %copy-start.6 = (bf16[2,256]{1,0:T(2,128)(2,1)S(1)}, bf16[2,256]{1,0:T(2,128)(2,1)}, u32[]{:S(2)}) copy-start(bf16[2,256]{1,0:T(2,128)(2,1)} %param.27) | copy-start | bytes 3076
  33.3 10.8 %copy-start = (f32[2,384]{1,0:T(2,128)S(1)}, f32[2,384]{1,0:T(2,128)}, u32[]{:S(2)}) copy-start(f32[2,384]{1,0:T(2,128)} %bias_ref.1) | copy-start | bytes 9220
  33.3 6.2 %collective-permute-start.7 = (f32[2,144,384]{2,1,0:T(8,128)S(1)}, f32[2,144,384]{2,1,0:T(8,128)S(1)}, u32[]{:S(2)}, u32[]{:S(2)}) collective-permute-start(f32[2,144,384]{2,1,0:T(8,128)S(1)} %get-tuple-element.29), channel_id=1, source_target_pairs={{0,1},{1,0},{2,3},{3,2},{4,5},{5,4},{6,7},{7,6},{8,9},{9,8},{10,11... | collective-permute-start | bytes 1327112 | tf_op jit(solution)/shard_map/ppermute | solution.py:669
  36.8 1.7 %collective-permute-start.8 = (bf16[8,176,128]{2,1,0:T(8,128)(2,1)S(1)}, bf16[8,176,128]{2,1,0:T(8,128)(2,1)S(1)}, u32[]{:S(2)}, u32[]{:S(2)}) collective-permute-start(bf16[8,176,128]{2,1,0:T(8,128)(2,1)S(1)} %all-to-all-done.got_ref.early_ref), channel_id=1, source_target_pairs={{0,1},{1,0},{2,3},{3,2},{4,5},{5,4},{6,7},{7,6},{8,9},{9,8},{10,11... | collective-permute-start | bytes 1081352 | tf_op jit(solution)/shard_map/ppermute | solution.py:621
  40.4 12.9 %all-to-all-start.1 = ((bf16[8,64,256]{2,1,0:T(8,128)(2,1)}), bf16[8,64,256]{2,1,0:T(8,128)(2,1)S(1)}, u32[]{:S(2)}, u32[]{:S(2)}) async-start(bf16[8,64,256]{2,1,0:T(8,128)(2,1)} %shard_map.153), calls=%async_computation.1 | async-start | bytes 524288 | tf_op jit(solution)/shard_map/all_to_all | solution.py:682
  44.1 9.2 %copy-start.4 = (bf16[128,256]{1,0:T(8,128)(2,1)S(1)}, bf16[128,256]{1,0:T(8,128)(2,1)}, u32[]{:S(2)}) copy-start(bf16[128,256]{1,0:T(8,128)(2,1)} %head_ref.1) | copy-start | bytes 196612
  71.9 1.4 %collective-permute-start.9 = (f32[8,40,128]{2,1,0:T(8,128)S(1)}, f32[8,40,128]{2,1,0:T(8,128)S(1)}, u32[]{:S(2)}, u32[]{:S(2)}) collective-permute-start(f32[8,40,128]{2,1,0:T(8,128)S(1)} %all_to_all.15.mine_ref), channel_id=1, source_target_pairs={{0,1},{1,0},{2,3},{3,2},{4,5},{5,4},{6,7},{7,6},{8,9},{9,8},{10,11... | collective-permute-start | bytes 491528 | tf_op jit(solution)/shard_map/ppermute | solution.py:751

commit v8 on v7

--- a/solution.py
+++ b/solution.py
@@ -290,20 +290,23 @@
         send_ref[r] = wide[r, pl.ds(other, half_wide), :]
 
 
-def merge_kernel(own, keep_ref, got_ref, term_ref, hidden_ref, out_ref):
-    dests = out_ref.shape[0]
+def combine_kernel(keep_ref, got_ref, out_ref):
     for r in range(keep_ref.shape[0]):
         keep, got = keep_ref[r], got_ref[r]
         gap = got[:, 256:384] - keep[:, 256:384]
         share = 1.0 / (1.0 + jnp.exp(gap))
-        share_fine, share_coarse = share[:, 0:1], share[:, 64:65]
-        base = (
+        out_ref[r] = (
             got[:, 0:128]
-            + (keep[:, 0:128] - got[:, 0:128]) * share_fine
+            + (keep[:, 0:128] - got[:, 0:128]) * share[:, 0:1]
             + got[:, 128:256]
-            + (keep[:, 128:256] - got[:, 128:256]) * share_coarse
-            + term_ref[r]
+            + (keep[:, 128:256] - got[:, 128:256]) * share[:, 64:65]
         )
+
+
+def merge_kernel(own, base_ref, term_ref, hidden_ref, out_ref):
+    dests = out_ref.shape[0]
+    for r in range(base_ref.shape[0]):
+        base = base_ref[r] + term_ref[r]
         hidden = hidden_ref[r].astype(F32)
         for j in range(dests):
             out_ref[j, r * WIN : (r + 1) * WIN, 0:128] = base[j * own : j * own + WIN].astype(BF16)
@@ -582,7 +585,7 @@
     room = 16 if dests <= 8 else 56
 
     rows_hidden = round_up(cap, 16)
-    rows_slot = rows_hidden + round_up(8 * (-(-cap // 128)), 16)
+    rows_slot = rows_hidden + 8 * (-(-cap // 128))
     shard = frame_two.reshape(1, rows_per, columns, channels)
     if dests == 8:
 
@@ -667,15 +670,24 @@
         *keys,
     )
     other = lax.ppermute(send, "loop", around)
-    sending = call(
-        functools.partial(merge_kernel, own),
-        jax.ShapeDtypeStruct((dests, rows_per * WIN, 256), BF16),
-        vmem_specs(4),
+    combined = call(
+        combine_kernel,
+        jax.ShapeDtypeStruct((rows_per, half_wide, 128), F32),
+        vmem_specs(2),
         [],
         (0, 1 << 20, 0),
         room,
         keep,
         other,
+    )
+    sending = call(
+        functools.partial(merge_kernel, own),
+        jax.ShapeDtypeStruct((dests, rows_per * WIN, 256), BF16),
+        vmem_specs(3),
+        [],
+        (0, 1 << 20, 0),
+        room,
+        combined,
         term,
         hidden_wide,
     )

time: 74.4 us -> 74.2 us (level)
    pallas_call x8 -> x9, Pallas kernels: 22.6 us -> 22.7 us  [call(): pl.pallas_call(kernel, out_shape=out_shape, in_specs=in_specs, out_specs=...]
  transfers between devices with their start and end apart: 12 -> 12, of which waited for: 7 -> 7; matrix products, arithmetic and copies ran while one was open for 0% -> 0% of each run, Pallas kernels for 18% -> 17%
where the time goes in v8:
time: 74.2 us; the launch traced here: 73.8 us
  Pallas kernels  22.7 us (31%)
  waiting for transfers between devices  20.9 us (28%)
  starting transfers between devices  17.7 us (24%)
  blocking collectives  10.9 us (15%)
  between operations  1.46 us (2%)
    pallas_call x9, Pallas kernels, call(): pl.pallas_call(kernel, out_shape=out_shape, in_specs=in_specs, out_specs=...  22.7 us
    all_to_all x1, blocking collectives, local(): back = lax.all_to_all(outgoing, 'rows', 0, 0, tiled=True)  10.9 us
    ppermute x7, starting transfers between devices, swap(): return lax.ppermute(value, 'rows', [(i, i ^ flip) for i in range(dests)])  10.2 us
    ppermute x7, waiting for transfers between devices, swap(): return lax.ppermute(value, 'rows', [(i, i ^ flip) for i in range(dests)])  8.55 us
    all_to_all x1, waiting for transfers between devices, local(): arrived = lax.all_to_all(sending, 'rows', 0, 0, tiled=True)  6.99 us
    all_to_all x1, starting transfers between devices, local(): arrived = lax.all_to_all(sending, 'rows', 0, 0, tiled=True)  3.78 us
    all_to_all x1, starting transfers between devices, local(): early = lax.all_to_all(packed, 'rows', 0, 0, tiled=True)  3.66 us
    all_to_all x1, waiting for transfers between devices, local(): early = lax.all_to_all(packed, 'rows', 0, 0, tiled=True)  3.18 us
  transfers between devices with their start and end apart: 12, of which 7 were waited for; matrix products, arithmetic and copies ran while one was open for 0% of the time, Pallas kernels for 17%

profile of v8, /device:TPU:0, one launch (start us, length us, event | category | flops | bytes accessed | tf_op | source)
XLA Modules:
  0.0 73.8 jit_solution(13323417641521134412)
XLA Ops:
  0.6 0.0 copy-start.3
  0.6 0.0 copy-start.5
  0.7 0.0 copy-start.1
  0.7 0.0 copy-start.2
  0.7 3.0 %collective-permute-start = (bf16[1,2,128,256]{3,2,1,0:T(8,128)(2,1)}, bf16[1,2,128,256]{3,2,1,0:T(8,128)(2,1)S(1)}, u32[]{:S(2)}, u32[]{:S(2)}) collective-permute-start(bf16[1,2,128,256]{3,2,1,0:T(8,128)(2,1)} %bitcast.5), channel_id=1, source_target_pairs={{0,2},{2,0},{4,6},{6,4},{8,10},{10,8},{12,14},{14,12},{1,3},{3,1},... | collective-permute-start | bytes 393224 | tf_op jit(solution)/shard_map/ppermute | solution.py:593
  3.7 2.6 %collective-permute-start.1 = (bf16[1,2,128,256]{3,2,1,0:T(8,128)(2,1)}, bf16[1,2,128,256]{3,2,1,0:T(8,128)(2,1)S(1)}, u32[]{:S(2)}, u32[]{:S(2)}) collective-permute-start(bf16[1,2,128,256]{3,2,1,0:T(8,128)(2,1)} %bitcast.6), channel_id=1, source_target_pairs={{0,8},{2,10},{4,12},{6,14},{8,0},{10,2},{12,4},{14,6},{1,9},{3,11}... | collective-permute-start | bytes 393224 | tf_op jit(solution)/shard_map/ppermute | solution.py:593
  6.3 1.6 %collective-permute-start.2 = (bf16[1,2,128,256]{3,2,1,0:T(8,128)(2,1)}, bf16[1,2,128,256]{3,2,1,0:T(8,128)(2,1)S(1)}, u32[]{:S(2)}, u32[]{:S(2)}) collective-permute-start(bf16[1,2,128,256]{3,2,1,0:T(8,128)(2,1)} %bitcast.7), channel_id=1, source_target_pairs={{0,4},{2,6},{4,0},{6,2},{8,12},{10,14},{12,8},{14,10},{1,5},{3,7},... | collective-permute-start | bytes 393224 | tf_op jit(solution)/shard_map/ppermute | solution.py:593
  7.9 0.2 collective-permute-start.3
  8.7 0.0 collective-permute-done.refs_1_
  8.8 3.9 %shard_map.149 = bf16[8,168,128]{2,1,0:T(8,128)(2,1)} custom-call(s32[1]{0:T(128)S(6)} %copy.16.count_ref, s32[12,128]{1,0:T(8,128)} %bitcast.10, bf16[2,1536]{1,0:T(2,128)(2,1)} %bitcast.11, bf16[1536,128]{1,0:T(8,128)(2,1)} %hidden_ref.1, bf16[2,256,128]{2,1,0:T(8,128)(2,1)} %context_ref.1), custom_call_target="tpu_custom_call" | custom-call | flops 603979776 | bytes 1048576 | tf_op jit(solution)/shard_map/pallas_call | solution.py:54
  12.7 3.9 %collective-permute-done.1.refs_4_ = bf16[1,2,128,256]{3,2,1,0:T(8,128)(2,1)S(1)} collective-permute-done((bf16[1,2,128,256]{3,2,1,0:T(8,128)(2,1)}, bf16[1,2,128,256]{3,2,1,0:T(8,128)(2,1)S(1)}, u32[]{:S(2)}, u32[]{:S(2)}) %collective-permute-start.1) | collective-permute-done | bytes 131104 | tf_op jit(solution)/shard_map/ppermute | solution.py:593
  16.6 0.0 collective-permute-start.4
  16.6 2.3 %collective-permute-start.5 = (bf16[1,2,128,256]{3,2,1,0:T(8,128)(2,1)S(1)}, bf16[1,2,128,256]{3,2,1,0:T(8,128)(2,1)S(1)}, u32[]{:S(2)}, u32[]{:S(2)}) collective-permute-start(bf16[1,2,128,256]{3,2,1,0:T(8,128)(2,1)S(1)} %collective-permute-done.refs_1_), channel_id=1, source_target_pairs={{0,12},{2,14},{4,8},{6,10},{8,4},{10,6},{12,0},{14,2},{1,13},{3,15... | collective-permute-start | bytes 393224 | tf_op jit(solution)/shard_map/ppermute | solution.py:593
  18.9 0.5 collective-permute-start.6
  19.4 0.0 collective-permute-done.2.refs_2_
  19.4 0.0 collective-permute-done.3.refs_6_
  19.4 3.2 %collective-permute-done.4.refs_3_ = bf16[1,2,128,256]{3,2,1,0:T(8,128)(2,1)S(1)} collective-permute-done((bf16[1,2,128,256]{3,2,1,0:T(8,128)(2,1)S(1)}, bf16[1,2,128,256]{3,2,1,0:T(8,128)(2,1)S(1)}, u32[]{:S(2)}, u32[]{:S(2)}) %collective-permute-start.4) | collective-permute-done | bytes 131104 | tf_op jit(solution)/shard_map/ppermute | solution.py:593
  22.6 1.4 %collective-permute-done.5.refs_7_ = bf16[1,2,128,256]{3,2,1,0:T(8,128)(2,1)S(1)} collective-permute-done((bf16[1,2,128,256]{3,2,1,0:T(8,128)(2,1)S(1)}, bf16[1,2,128,256]{3,2,1,0:T(8,128)(2,1)S(1)}, u32[]{:S(2)}, u32[]{:S(2)}) %collective-permute-start.5) | collective-permute-done | bytes 131104 | tf_op jit(solution)/shard_map/ppermute | solution.py:593
  24.0 0.0 collective-permute-done.6.refs_5_
  24.0 3.7 %all-to-all-start = ((bf16[8,168,128]{2,1,0:T(8,128)(2,1)}), bf16[8,168,128]{2,1,0:T(8,128)(2,1)S(1)}, u32[]{:S(2)}, u32[]{:S(2)}) async-start(bf16[8,168,128]{2,1,0:T(8,128)(2,1)} %shard_map.149), calls=%async_computation | async-start | bytes 688128 | tf_op jit(solution)/shard_map/all_to_all | solution.py:622
  27.7 0.0 copy-done.5
  27.7 0.0 copy-done.3
  27.7 0.0 copy-done.1
  27.7 0.0 copy-done.2
  27.7 5.5 %shard_map.150 = (f32[2,144,384]{2,1,0:T(8,128)S(1)}, f32[2,144,384]{2,1,0:T(8,128)S(1)}) custom-call(bf16[512,256]{1,0:T(8,128)(2,1)S(1)} %bitcast.4, bf16[512,128]{1,0:T(8,128)(2,1)S(1)} %copy-done.2, f32[8,128]{1,0:T(8,128)S(1)} %pad.8.ow_ref, bf16[1,2,128,256]{3,2,1,0:T(8,128)(2,1)S(1)} %bitcast.9, ...), custom_call_target="tpu_custom_call" | custom-call | flops 1073741824 | bytes 2097152 | tf_op jit(solution)/shard_map/pallas_call | solution.py:54
  33.3 0.0 copy-start.6
  33.3 0.0 copy-start
  33.3 0.1 collective-permute-start.7
  33.4 3.2 %all-to-all-done.got_ref.early_ref = bf16[8,168,128]{2,1,0:T(8,128)(2,1)S(1)} async-done(((bf16[8,168,128]{2,1,0:T(8,128)(2,1)}), bf16[8,168,128]{2,1,0:T(8,128)(2,1)S(1)}, u32[]{:S(2)}, u32[]{:S(2)}) %all-to-all-start) | async-done | bytes 344096 | tf_op jit(solution)/shard_map/all_to_all | solution.py:622
  36.6 0.0 collective-permute-start.8
  36.6 0.0 collective-permute-done.7.got_ref
  36.6 0.2 shard_map.151.base_ref
  36.7 0.7 shard_map.152
  37.4 0.8 %collective-permute-done.8.got_ref = bf16[8,168,128]{2,1,0:T(8,128)(2,1)S(1)} collective-permute-done((bf16[8,168,128]{2,1,0:T(8,128)(2,1)S(1)}, bf16[8,168,128]{2,1,0:T(8,128)(2,1)S(1)}, u32[]{:S(2)}, u32[]{:S(2)}) %collective-permute-start.8) | collective-permute-done | bytes 344096 | tf_op jit(solution)/shard_map/ppermute | solution.py:624
  38.2 1.0 %shard_map.153 = (bf16[2,144,128]{2,1,0:T(8,128)(2,1)S(1)}, f32[8,512]{1,0:T(8,128)S(1)}, f32[2,144,128]{2,1,0:T(8,128)S(1)}) custom-call(bf16[8,168,128]{2,1,0:T(8,128)(2,1)S(1)} %collective-permute-done.8.got_ref, f32[512,128]{1,0:T(8,128)S(1)} %get-tuple-element.31.part_ref, f32[8,512]{1,0:T(8,128)S(1)} %get-tuple-element.32.flow_part_ref, ...), custom_call_target="tpu_custom_call" | custom-call | flops 100663296 | bytes 1048576 | tf_op jit(solution)/shard_map/pallas_call | solution.py:54
  39.2 0.7 %shard_map.154 = bf16[8,64,256]{2,1,0:T(8,128)(2,1)} custom-call(f32[2,144,128]{2,1,0:T(8,128)S(1)} %shard_map.151.base_ref, f32[2,144,128]{2,1,0:T(8,128)S(1)} %get-tuple-element.33.term_ref, bf16[2,144,128]{2,1,0:T(8,128)(2,1)S(1)} %get-tuple-element.34.hidden_ref), custom_call_target="tpu_custom_call" | custom-call | bytes 1048576 | tf_op jit(solution)/shard_map/pallas_call | solution.py:54
  40.0 3.8 %all-to-all-start.1 = ((bf16[8,64,256]{2,1,0:T(8,128)(2,1)}), bf16[8,64,256]{2,1,0:T(8,128)(2,1)S(1)}, u32[]{:S(2)}, u32[]{:S(2)}) async-start(bf16[8,64,256]{2,1,0:T(8,128)(2,1)} %shard_map.154), calls=%async_computation.1 | async-start | bytes 524288 | tf_op jit(solution)/shard_map/all_to_all | solution.py:694
  43.8 0.0 copy-done.6
  43.8 0.0 copy-done
  43.8 0.0 copy-start.4
  43.8 2.2 %shard_map.155.fixed_ref = f32[2,512,384]{2,1,0:T(8,128)S(1)} custom-call(bf16[8,168,128]{2,1,0:T(8,128)(2,1)S(1)} %all-to-all-done.got_ref.early_ref, bf16[2,5,384,256]{3,2,1,0:T(8,128)(2,1)} %gate_hbm.3, bf16[2,5,384,128]{3,2,1,0:T(8,128)(2,1)} %state_hbm.3, f32[2,384]{1,0:T(2,128)S(1)} %copy-done), custom_call_target="tpu_custom_call" | custom-call | flops 503316480 | bytes 4194304 | tf_op jit(solution)/shard_map/pallas_call | solution.py:54
  46.0 7.0 %all-to-all-done.1.got_ref = bf16[8,64,256]{2,1,0:T(8,128)(2,1)S(1)} async-done(((bf16[8,64,256]{2,1,0:T(8,128)(2,1)}), bf16[8,64,256]{2,1,0:T(8,128)(2,1)S(1)}, u32[]{:S(2)}, u32[]{:S(2)}) %all-to-all-start.1) | async-done | bytes 262176 | tf_op jit(solution)/shard_map/all_to_all | solution.py:694
  53.0 0.0 copy-done.4
  53.0 7.6 %shard_map.156 = f32[8,40,128]{2,1,0:T(8,128)S(1)} custom-call(bf16[8,64,256]{2,1,0:T(8,128)(2,1)S(1)} %all-to-all-done.1.got_ref, f32[2,512,384]{2,1,0:T(8,128)S(1)} %shard_map.155.fixed_ref, f32[8,128]{1,0:T(8,128)S(1)} %pad.8.ow_ref, bf16[2,5,384,256]{3,2,1,0:T(8,128)(2,1)} %gate_hbm.3, bf16[2,5,384,128]{3,2,1,0:T(8,128)(2,1)} %state_hbm.3, ...), custom_call_target="tpu_custom_call" | custom-call | flops 2013265920 | bytes 4194304 | tf_op jit(solution)/shard_map/pallas_call | solution.py:54
  60.7 10.9 %all_to_all.15.mine_ref = f32[8,40,128]{2,1,0:T(8,128)S(1)} all-to-all(f32[8,40,128]{2,1,0:T(8,128)S(1)} %shard_map.156), channel_id=1, replica_groups=mesh['groups'=2,'rows'=8,'loop'=2] {'rows'}, dimensions={0} | all-to-all | bytes 327680 | tf_op jit(solution)/shard_map/all_to_all | solution.py:751
  71.6 0.0 collective-permute-start.9
  71.6 1.4 %collective-permute-done.9.other_ref = f32[8,40,128]{2,1,0:T(8,128)S(1)} collective-permute-done((f32[8,40,128]{2,1,0:T(8,128)S(1)}, f32[8,40,128]{2,1,0:T(8,128)S(1)}, u32[]{:S(2)}, u32[]{:S(2)}) %collective-permute-start.9) | collective-permute-done | bytes 163872 | tf_op jit(solution)/shard_map/ppermute | solution.py:763
  73.0 0.7 %shard_map.157 = (f32[2,256,128]{2,1,0:T(8,128)}, f32[2,2,256]{2,1,0:T(2,128)}) custom-call(f32[8,40,128]{2,1,0:T(8,128)S(1)} %all_to_all.15.mine_ref, f32[8,40,128]{2,1,0:T(8,128)S(1)} %collective-permute-done.9.other_ref, f32[8,512]{1,0:T(8,128)S(1)} %get-tuple-element.35.first_ref), custom_call_target="tpu_custom_call" | custom-call | bytes 1048576 | tf_op jit(solution)/shard_map/pallas_call | solution.py:54
  (2 shorter events, 0.0 us)
Async XLA Ops:
  0.6 27.1 %copy-start.3 = (bf16[2,128,256]{2,1,0:T(8,128)(2,1)S(1)}, bf16[2,128,256]{2,1,0:T(8,128)(2,1)}, u32[]{:S(2)}) copy-start(bf16[2,128,256]{2,1,0:T(8,128)(2,1)} %param.15) | copy-start | bytes 393220
  0.6 27.0 %copy-start.5 = (f32[6,128]{1,0:T(8,128)S(1)}, f32[6,128]{1,0:T(8,128)}, u32[]{:S(2)}) copy-start(f32[6,128]{1,0:T(8,128)} %param.22) | copy-start | bytes 9220
  0.7 27.1 %copy-start.1 = (bf16[2,256,256]{2,1,0:T(8,128)(2,1)S(1)}, bf16[2,256,256]{2,1,0:T(8,128)(2,1)}, u32[]{:S(2)}) copy-start(bf16[2,256,256]{2,1,0:T(8,128)(2,1)} %param.14) | copy-start | bytes 786436
  0.7 27.1 %copy-start.2 = (bf16[512,128]{1,0:T(8,128)(2,1)S(1)}, bf16[512,128]{1,0:T(8,128)(2,1)}, u32[]{:S(2)}) copy-start(bf16[512,128]{1,0:T(8,128)(2,1)} %weight_ref.1) | copy-start | bytes 393220
  0.7 8.1 %collective-permute-start = (bf16[1,2,128,256]{3,2,1,0:T(8,128)(2,1)}, bf16[1,2,128,256]{3,2,1,0:T(8,128)(2,1)S(1)}, u32[]{:S(2)}, u32[]{:S(2)}) collective-permute-start(bf16[1,2,128,256]{3,2,1,0:T(8,128)(2,1)} %bitcast.5), channel_id=1, source_target_pairs={{0,2},{2,0},{4,6},{6,4},{8,10},{10,8},{12,14},{14,12},{1,3},{3,1},... | collective-permute-start | bytes 393224 | tf_op jit(solution)/shard_map/ppermute | solution.py:593
  3.7 12.9 %collective-permute-start.1 = (bf16[1,2,128,256]{3,2,1,0:T(8,128)(2,1)}, bf16[1,2,128,256]{3,2,1,0:T(8,128)(2,1)S(1)}, u32[]{:S(2)}, u32[]{:S(2)}) collective-permute-start(bf16[1,2,128,256]{3,2,1,0:T(8,128)(2,1)} %bitcast.6), channel_id=1, source_target_pairs={{0,8},{2,10},{4,12},{6,14},{8,0},{10,2},{12,4},{14,6},{1,9},{3,11}... | collective-permute-start | bytes 393224 | tf_op jit(solution)/shard_map/ppermute | solution.py:593
  6.3 13.1 %collective-permute-start.2 = (bf16[1,2,128,256]{3,2,1,0:T(8,128)(2,1)}, bf16[1,2,128,256]{3,2,1,0:T(8,128)(2,1)S(1)}, u32[]{:S(2)}, u32[]{:S(2)}) collective-permute-start(bf16[1,2,128,256]{3,2,1,0:T(8,128)(2,1)} %bitcast.7), channel_id=1, source_target_pairs={{0,4},{2,6},{4,0},{6,2},{8,12},{10,14},{12,8},{14,10},{1,5},{3,7},... | collective-permute-start | bytes 393224 | tf_op jit(solution)/shard_map/ppermute | solution.py:593
  7.9 11.5 %collective-permute-start.3 = (bf16[1,2,128,256]{3,2,1,0:T(8,128)(2,1)}, bf16[1,2,128,256]{3,2,1,0:T(8,128)(2,1)S(1)}, u32[]{:S(2)}, u32[]{:S(2)}) collective-permute-start(bf16[1,2,128,256]{3,2,1,0:T(8,128)(2,1)} %bitcast.8), channel_id=1, source_target_pairs={{0,12},{2,14},{4,8},{6,10},{8,4},{10,6},{12,0},{14,2},{1,13},{3,15... | collective-permute-start | bytes 393224 | tf_op jit(solution)/shard_map/ppermute | solution.py:593
  16.6 6.0 %collective-permute-start.4 = (bf16[1,2,128,256]{3,2,1,0:T(8,128)(2,1)S(1)}, bf16[1,2,128,256]{3,2,1,0:T(8,128)(2,1)S(1)}, u32[]{:S(2)}, u32[]{:S(2)}) collective-permute-start(bf16[1,2,128,256]{3,2,1,0:T(8,128)(2,1)S(1)} %collective-permute-done.refs_1_), channel_id=1, source_target_pairs={{0,4},{2,6},{4,0},{6,2},{8,12},{10,14},{12,8},{14,10},{1,5},{3,7},... | collective-permute-start | bytes 393224 | tf_op jit(solution)/shard_map/ppermute | solution.py:593
  16.6 7.4 %collective-permute-start.5 = (bf16[1,2,128,256]{3,2,1,0:T(8,128)(2,1)S(1)}, bf16[1,2,128,256]{3,2,1,0:T(8,128)(2,1)S(1)}, u32[]{:S(2)}, u32[]{:S(2)}) collective-permute-start(bf16[1,2,128,256]{3,2,1,0:T(8,128)(2,1)S(1)} %collective-permute-done.refs_1_), channel_id=1, source_target_pairs={{0,12},{2,14},{4,8},{6,10},{8,4},{10,6},{12,0},{14,2},{1,13},{3,15... | collective-permute-start | bytes 393224 | tf_op jit(solution)/shard_map/ppermute | solution.py:593
  18.9 5.1 %collective-permute-start.6 = (bf16[1,2,128,256]{3,2,1,0:T(8,128)(2,1)S(1)}, bf16[1,2,128,256]{3,2,1,0:T(8,128)(2,1)S(1)}, u32[]{:S(2)}, u32[]{:S(2)}) collective-permute-start(bf16[1,2,128,256]{3,2,1,0:T(8,128)(2,1)S(1)} %collective-permute-done.1.refs_4_), channel_id=1, source_target_pairs={{0,2},{2,0},{4,6},{6,4},{8,10},{10,8},{12,14},{14,12},{1,3},{3,1},... | collective-permute-start | bytes 393224 | tf_op jit(solution)/shard_map/ppermute | solution.py:593
  24.0 12.5 %all-to-all-start = ((bf16[8,168,128]{2,1,0:T(8,128)(2,1)}), bf16[8,168,128]{2,1,0:T(8,128)(2,1)S(1)}, u32[]{:S(2)}, u32[]{:S(2)}) async-start(bf16[8,168,128]{2,1,0:T(8,128)(2,1)} %shard_map.149), calls=%async_computation | async-start | bytes 688128 | tf_op jit(solution)/shard_map/all_to_all | solution.py:622
  33.3 10.5 %copy-start.6 = (bf16[2,256]{1,0:T(2,128)(2,1)S(1)}, bf16[2,256]{1,0:T(2,128)(2,1)}, u32[]{:S(2)}) copy-start(bf16[2,256]{1,0:T(2,128)(2,1)} %param.27) | copy-start | bytes 3076
  33.3 10.5 %copy-start = (f32[2,384]{1,0:T(2,128)S(1)}, f32[2,384]{1,0:T(2,128)}, u32[]{:S(2)}) copy-start(f32[2,384]{1,0:T(2,128)} %bias_ref.1) | copy-start | bytes 9220
  33.3 3.3 %collective-permute-start.7 = (f32[2,144,384]{2,1,0:T(8,128)S(1)}, f32[2,144,384]{2,1,0:T(8,128)S(1)}, u32[]{:S(2)}, u32[]{:S(2)}) collective-permute-start(f32[2,144,384]{2,1,0:T(8,128)S(1)} %get-tuple-element.29), channel_id=1, source_target_pairs={{0,1},{1,0},{2,3},{3,2},{4,5},{5,4},{6,7},{7,6},{8,9},{9,8},{10,11... | collective-permute-start | bytes 1327112 | tf_op jit(solution)/shard_map/ppermute | solution.py:672
  36.6 1.7 %collective-permute-start.8 = (bf16[8,168,128]{2,1,0:T(8,128)(2,1)S(1)}, bf16[8,168,128]{2,1,0:T(8,128)(2,1)S(1)}, u32[]{:S(2)}, u32[]{:S(2)}) collective-permute-start(bf16[8,168,128]{2,1,0:T(8,128)(2,1)S(1)} %all-to-all-done.got_ref.early_ref), channel_id=1, source_target_pairs={{0,1},{1,0},{2,3},{3,2},{4,5},{5,4},{6,7},{7,6},{8,9},{9,8},{10,11... | collective-permute-start | bytes 1032200 | tf_op jit(solution)/shard_map/ppermute | solution.py:624
  40.0 13.0 %all-to-all-start.1 = ((bf16[8,64,256]{2,1,0:T(8,128)(2,1)}), bf16[8,64,256]{2,1,0:T(8,128)(2,1)S(1)}, u32[]{:S(2)}, u32[]{:S(2)}) async-start(bf16[8,64,256]{2,1,0:T(8,128)(2,1)} %shard_map.154), calls=%async_computation.1 | async-start | bytes 524288 | tf_op jit(solution)/shard_map/all_to_all | solution.py:694
  43.8 9.2 %copy-start.4 = (bf16[128,256]{1,0:T(8,128)(2,1)S(1)}, bf16[128,256]{1,0:T(8,128)(2,1)}, u32[]{:S(2)}) copy-start(bf16[128,256]{1,0:T(8,128)(2,1)} %head_ref.1) | copy-start | bytes 196612
  71.6 1.4 %collective-permute-start.9 = (f32[8,40,128]{2,1,0:T(8,128)S(1)}, f32[8,40,128]{2,1,0:T(8,128)S(1)}, u32[]{:S(2)}, u32[]{:S(2)}) collective-permute-start(f32[8,40,128]{2,1,0:T(8,128)S(1)} %all_to_all.15.mine_ref), channel_id=1, source_target_pairs={{0,1},{1,0},{2,3},{3,2},{4,5},{5,4},{6,7},{7,6},{8,9},{9,8},{10,11... | collective-permute-start | bytes 491528 | tf_op jit(solution)/shard_map/ppermute | solution.py:763

commit v9 on v8

--- a/solution.py
+++ b/solution.py
@@ -650,7 +650,7 @@
     )
     queries = frame_one.reshape(pixels, channels)
     chunks = dests // 2
-    tile = 128
+    tile = 256 if dests <= 8 else 128
     keep, send = call(
         functools.partial(match_kernel, len(keys), len(keys) > 1, half_wide, rows_per),
         (jax.ShapeDtypeStruct((rows_per, half_wide, 384), F32),) * 2,

time: 74.2 us -> 74 us (level)
  waiting for transfers between devices: 20.9 us -> 22.4 us
  Pallas kernels: 22.7 us -> 21.3 us
    pallas_call x9, Pallas kernels: 22.7 us -> 21.3 us  [call(): pl.pallas_call(kernel, out_shape=out_shape, in_specs=in_specs, out_specs=...]
    all_to_all x1, waiting for transfers between devices: 3.18 us -> 4.57 us  [local(): early = lax.all_to_all(packed, 'rows', 0, 0, tiled=True)]
  transfers between devices with their start and end apart: 12 -> 12, of which waited for: 7 -> 7; matrix products, arithmetic and copies ran while one was open for 0% -> 0% of each run, Pallas kernels for 17% -> 15%
where the time goes in v9:
time: 74 us; the launch traced here: 73.6 us
  waiting for transfers between devices  22.4 us (30%)
  Pallas kernels  21.3 us (29%)
  starting transfers between devices  17.4 us (24%)
  blocking collectives  10.9 us (15%)
  between operations  1.46 us (2%)
    pallas_call x9, Pallas kernels, call(): pl.pallas_call(kernel, out_shape=out_shape, in_specs=in_specs, out_specs=...  21.3 us
    all_to_all x1, blocking collectives, local(): back = lax.all_to_all(outgoing, 'rows', 0, 0, tiled=True)  10.9 us
    ppermute x7, starting transfers between devices, swap(): return lax.ppermute(value, 'rows', [(i, i ^ flip) for i in range(dests)])  10.2 us
    ppermute x7, waiting for transfers between devices, swap(): return lax.ppermute(value, 'rows', [(i, i ^ flip) for i in range(dests)])  8.55 us
    all_to_all x1, waiting for transfers between devices, local(): arrived = lax.all_to_all(sending, 'rows', 0, 0, tiled=True)  7.1 us
    all_to_all x1, waiting for transfers between devices, local(): early = lax.all_to_all(packed, 'rows', 0, 0, tiled=True)  4.57 us
    all_to_all x1, starting transfers between devices, local(): early = lax.all_to_all(packed, 'rows', 0, 0, tiled=True)  3.66 us
    all_to_all x1, starting transfers between devices, local(): arrived = lax.all_to_all(sending, 'rows', 0, 0, tiled=True)  3.52 us
  transfers between devices with their start and end apart: 12, of which 7 were waited for; matrix products, arithmetic and copies ran while one was open for 0% of the time, Pallas kernels for 15%

profile of v9, /device:TPU:0, one launch (start us, length us, event | category | flops | bytes accessed | tf_op | source)
XLA Modules:
  0.0 73.6 jit_solution(14661348246713528419)
XLA Ops:
  0.6 0.0 copy-start.3
  0.6 0.0 copy-start.5
  0.7 0.0 copy-start.1
  0.7 0.0 copy-start.2
  0.7 3.0 %collective-permute-start = (bf16[1,2,128,256]{3,2,1,0:T(8,128)(2,1)}, bf16[1,2,128,256]{3,2,1,0:T(8,128)(2,1)S(1)}, u32[]{:S(2)}, u32[]{:S(2)}) collective-permute-start(bf16[1,2,128,256]{3,2,1,0:T(8,128)(2,1)} %bitcast.5), channel_id=1, source_target_pairs={{0,2},{2,0},{4,6},{6,4},{8,10},{10,8},{12,14},{14,12},{1,3},{3,1},... | collective-permute-start | bytes 393224 | tf_op jit(solution)/shard_map/ppermute | solution.py:593
  3.7 2.6 %collective-permute-start.1 = (bf16[1,2,128,256]{3,2,1,0:T(8,128)(2,1)}, bf16[1,2,128,256]{3,2,1,0:T(8,128)(2,1)S(1)}, u32[]{:S(2)}, u32[]{:S(2)}) collective-permute-start(bf16[1,2,128,256]{3,2,1,0:T(8,128)(2,1)} %bitcast.6), channel_id=1, source_target_pairs={{0,8},{2,10},{4,12},{6,14},{8,0},{10,2},{12,4},{14,6},{1,9},{3,11}... | collective-permute-start | bytes 393224 | tf_op jit(solution)/shard_map/ppermute | solution.py:593
  6.3 1.6 %collective-permute-start.2 = (bf16[1,2,128,256]{3,2,1,0:T(8,128)(2,1)}, bf16[1,2,128,256]{3,2,1,0:T(8,128)(2,1)S(1)}, u32[]{:S(2)}, u32[]{:S(2)}) collective-permute-start(bf16[1,2,128,256]{3,2,1,0:T(8,128)(2,1)} %bitcast.7), channel_id=1, source_target_pairs={{0,4},{2,6},{4,0},{6,2},{8,12},{10,14},{12,8},{14,10},{1,5},{3,7},... | collective-permute-start | bytes 393224 | tf_op jit(solution)/shard_map/ppermute | solution.py:593
  7.9 0.2 collective-permute-start.3
  8.7 0.0 collective-permute-done.refs_1_
  8.8 3.9 %shard_map.149 = bf16[8,168,128]{2,1,0:T(8,128)(2,1)} custom-call(s32[1]{0:T(128)S(6)} %copy.16.count_ref, s32[12,128]{1,0:T(8,128)} %bitcast.10, bf16[2,1536]{1,0:T(2,128)(2,1)} %bitcast.11, bf16[1536,128]{1,0:T(8,128)(2,1)} %hidden_ref.1, bf16[2,256,128]{2,1,0:T(8,128)(2,1)} %context_ref.1), custom_call_target="tpu_custom_call" | custom-call | flops 603979776 | bytes 1048576 | tf_op jit(solution)/shard_map/pallas_call | solution.py:54
  12.7 3.9 %collective-permute-done.1.refs_4_ = bf16[1,2,128,256]{3,2,1,0:T(8,128)(2,1)S(1)} collective-permute-done((bf16[1,2,128,256]{3,2,1,0:T(8,128)(2,1)}, bf16[1,2,128,256]{3,2,1,0:T(8,128)(2,1)S(1)}, u32[]{:S(2)}, u32[]{:S(2)}) %collective-permute-start.1) | collective-permute-done | bytes 131104 | tf_op jit(solution)/shard_map/ppermute | solution.py:593
  16.6 0.0 collective-permute-start.4
  16.6 2.3 %collective-permute-start.5 = (bf16[1,2,128,256]{3,2,1,0:T(8,128)(2,1)S(1)}, bf16[1,2,128,256]{3,2,1,0:T(8,128)(2,1)S(1)}, u32[]{:S(2)}, u32[]{:S(2)}) collective-permute-start(bf16[1,2,128,256]{3,2,1,0:T(8,128)(2,1)S(1)} %collective-permute-done.refs_1_), channel_id=1, source_target_pairs={{0,12},{2,14},{4,8},{6,10},{8,4},{10,6},{12,0},{14,2},{1,13},{3,15... | collective-permute-start | bytes 393224 | tf_op jit(solution)/shard_map/ppermute | solution.py:593
  18.9 0.5 collective-permute-start.6
  19.4 0.0 collective-permute-done.2.refs_2_
  19.4 0.0 collective-permute-done.3.refs_6_
  19.4 3.2 %collective-permute-done.4.refs_3_ = bf16[1,2,128,256]{3,2,1,0:T(8,128)(2,1)S(1)} collective-permute-done((bf16[1,2,128,256]{3,2,1,0:T(8,128)(2,1)S(1)}, bf16[1,2,128,256]{3,2,1,0:T(8,128)(2,1)S(1)}, u32[]{:S(2)}, u32[]{:S(2)}) %collective-permute-start.4) | collective-permute-done | bytes 131104 | tf_op jit(solution)/shard_map/ppermute | solution.py:593
  22.6 1.4 %collective-permute-done.5.refs_7_ = bf16[1,2,128,256]{3,2,1,0:T(8,128)(2,1)S(1)} collective-permute-done((bf16[1,2,128,256]{3,2,1,0:T(8,128)(2,1)S(1)}, bf16[1,2,128,256]{3,2,1,0:T(8,128)(2,1)S(1)}, u32[]{:S(2)}, u32[]{:S(2)}) %collective-permute-start.5) | collective-permute-done | bytes 131104 | tf_op jit(solution)/shard_map/ppermute | solution.py:593
  24.0 0.0 collective-permute-done.6.refs_5_
  24.0 3.7 %all-to-all-start = ((bf16[8,168,128]{2,1,0:T(8,128)(2,1)}), bf16[8,168,128]{2,1,0:T(8,128)(2,1)S(1)}, u32[]{:S(2)}, u32[]{:S(2)}) async-start(bf16[8,168,128]{2,1,0:T(8,128)(2,1)} %shard_map.149), calls=%async_computation | async-start | bytes 688128 | tf_op jit(solution)/shard_map/all_to_all | solution.py:622
  27.7 0.0 copy-done.5
  27.7 0.0 copy-done.3
  27.7 0.0 copy-done.1
  27.7 0.0 copy-done.2
  27.7 4.1 %shard_map.150 = (f32[2,144,384]{2,1,0:T(8,128)S(1)}, f32[2,144,384]{2,1,0:T(8,128)S(1)}) custom-call(bf16[512,256]{1,0:T(8,128)(2,1)S(1)} %bitcast.4, bf16[512,128]{1,0:T(8,128)(2,1)S(1)} %copy-done.2, f32[8,128]{1,0:T(8,128)S(1)} %pad.8.ow_ref, bf16[1,2,128,256]{3,2,1,0:T(8,128)(2,1)S(1)} %bitcast.9, ...), custom_call_target="tpu_custom_call" | custom-call | flops 1073741824 | bytes 2097152 | tf_op jit(solution)/shard_map/pallas_call | solution.py:54
  31.9 0.0 copy-start.6
  31.9 0.0 copy-start
  31.9 0.1 collective-permute-start.7
  32.0 4.6 %all-to-all-done.got_ref.early_ref = bf16[8,168,128]{2,1,0:T(8,128)(2,1)S(1)} async-done(((bf16[8,168,128]{2,1,0:T(8,128)(2,1)}), bf16[8,168,128]{2,1,0:T(8,128)(2,1)S(1)}, u32[]{:S(2)}, u32[]{:S(2)}) %all-to-all-start) | async-done | bytes 344096 | tf_op jit(solution)/shard_map/all_to_all | solution.py:622
  36.6 0.0 collective-permute-start.8
  36.6 0.0 collective-permute-done.7.got_ref
  36.6 0.2 shard_map.151.base_ref
  36.7 0.7 shard_map.152
  37.4 0.8 %collective-permute-done.8.got_ref = bf16[8,168,128]{2,1,0:T(8,128)(2,1)S(1)} collective-permute-done((bf16[8,168,128]{2,1,0:T(8,128)(2,1)S(1)}, bf16[8,168,128]{2,1,0:T(8,128)(2,1)S(1)}, u32[]{:S(2)}, u32[]{:S(2)}) %collective-permute-start.8) | collective-permute-done | bytes 344096 | tf_op jit(solution)/shard_map/ppermute | solution.py:624
  38.2 1.0 %shard_map.153 = (bf16[2,144,128]{2,1,0:T(8,128)(2,1)S(1)}, f32[8,512]{1,0:T(8,128)S(1)}, f32[2,144,128]{2,1,0:T(8,128)S(1)}) custom-call(bf16[8,168,128]{2,1,0:T(8,128)(2,1)S(1)} %collective-permute-done.8.got_ref, f32[512,128]{1,0:T(8,128)S(1)} %get-tuple-element.31.part_ref, f32[8,512]{1,0:T(8,128)S(1)} %get-tuple-element.32.flow_part_ref, ...), custom_call_target="tpu_custom_call" | custom-call | flops 100663296 | bytes 1048576 | tf_op jit(solution)/shard_map/pallas_call | solution.py:54
  39.2 0.7 %shard_map.154 = bf16[8,64,256]{2,1,0:T(8,128)(2,1)} custom-call(f32[2,144,128]{2,1,0:T(8,128)S(1)} %shard_map.151.base_ref, f32[2,144,128]{2,1,0:T(8,128)S(1)} %get-tuple-element.33.term_ref, bf16[2,144,128]{2,1,0:T(8,128)(2,1)S(1)} %get-tuple-element.34.hidden_ref), custom_call_target="tpu_custom_call" | custom-call | bytes 1048576 | tf_op jit(solution)/shard_map/pallas_call | solution.py:54
  40.0 3.5 %all-to-all-start.1 = ((bf16[8,64,256]{2,1,0:T(8,128)(2,1)}), bf16[8,64,256]{2,1,0:T(8,128)(2,1)S(1)}, u32[]{:S(2)}, u32[]{:S(2)}) async-start(bf16[8,64,256]{2,1,0:T(8,128)(2,1)} %shard_map.154), calls=%async_computation.1 | async-start | bytes 524288 | tf_op jit(solution)/shard_map/all_to_all | solution.py:694
  43.5 0.0 copy-done.6
  43.5 0.0 copy-done
  43.5 0.0 copy-start.4
  43.6 2.2 %shard_map.155.fixed_ref = f32[2,512,384]{2,1,0:T(8,128)S(1)} custom-call(bf16[8,168,128]{2,1,0:T(8,128)(2,1)S(1)} %all-to-all-done.got_ref.early_ref, bf16[2,5,384,256]{3,2,1,0:T(8,128)(2,1)} %gate_hbm.3, bf16[2,5,384,128]{3,2,1,0:T(8,128)(2,1)} %state_hbm.3, f32[2,384]{1,0:T(2,128)S(1)} %copy-done), custom_call_target="tpu_custom_call" | custom-call | flops 503316480 | bytes 4194304 | tf_op jit(solution)/shard_map/pallas_call | solution.py:54
  45.8 7.1 %all-to-all-done.1.got_ref = bf16[8,64,256]{2,1,0:T(8,128)(2,1)S(1)} async-done(((bf16[8,64,256]{2,1,0:T(8,128)(2,1)}), bf16[8,64,256]{2,1,0:T(8,128)(2,1)S(1)}, u32[]{:S(2)}, u32[]{:S(2)}) %all-to-all-start.1) | async-done | bytes 262176 | tf_op jit(solution)/shard_map/all_to_all | solution.py:694
  52.9 0.0 copy-done.4
  52.9 7.6 %shard_map.156 = f32[8,40,128]{2,1,0:T(8,128)S(1)} custom-call(bf16[8,64,256]{2,1,0:T(8,128)(2,1)S(1)} %all-to-all-done.1.got_ref, f32[2,512,384]{2,1,0:T(8,128)S(1)} %shard_map.155.fixed_ref, f32[8,128]{1,0:T(8,128)S(1)} %pad.8.ow_ref, bf16[2,5,384,256]{3,2,1,0:T(8,128)(2,1)} %gate_hbm.3, bf16[2,5,384,128]{3,2,1,0:T(8,128)(2,1)} %state_hbm.3, ...), custom_call_target="tpu_custom_call" | custom-call | flops 2013265920 | bytes 4194304 | tf_op jit(solution)/shard_map/pallas_call | solution.py:54
  60.5 10.9 %all_to_all.15.mine_ref = f32[8,40,128]{2,1,0:T(8,128)S(1)} all-to-all(f32[8,40,128]{2,1,0:T(8,128)S(1)} %shard_map.156), channel_id=1, replica_groups=mesh['groups'=2,'rows'=8,'loop'=2] {'rows'}, dimensions={0} | all-to-all | bytes 327680 | tf_op jit(solution)/shard_map/all_to_all | solution.py:751
  71.4 0.0 collective-permute-start.9
  71.4 1.4 %collective-permute-done.9.other_ref = f32[8,40,128]{2,1,0:T(8,128)S(1)} collective-permute-done((f32[8,40,128]{2,1,0:T(8,128)S(1)}, f32[8,40,128]{2,1,0:T(8,128)S(1)}, u32[]{:S(2)}, u32[]{:S(2)}) %collective-permute-start.9) | collective-permute-done | bytes 163872 | tf_op jit(solution)/shard_map/ppermute | solution.py:763
  72.8 0.7 %shard_map.157 = (f32[2,256,128]{2,1,0:T(8,128)}, f32[2,2,256]{2,1,0:T(2,128)}) custom-call(f32[8,40,128]{2,1,0:T(8,128)S(1)} %all_to_all.15.mine_ref, f32[8,40,128]{2,1,0:T(8,128)S(1)} %collective-permute-done.9.other_ref, f32[8,512]{1,0:T(8,128)S(1)} %get-tuple-element.35.first_ref), custom_call_target="tpu_custom_call" | custom-call | bytes 1048576 | tf_op jit(solution)/shard_map/pallas_call | solution.py:54
  (2 shorter events, 0.0 us)
Async XLA Ops:
  0.6 27.1 %copy-start.3 = (bf16[2,128,256]{2,1,0:T(8,128)(2,1)S(1)}, bf16[2,128,256]{2,1,0:T(8,128)(2,1)}, u32[]{:S(2)}) copy-start(bf16[2,128,256]{2,1,0:T(8,128)(2,1)} %param.15) | copy-start | bytes 393220
  0.6 27.0 %copy-start.5 = (f32[6,128]{1,0:T(8,128)S(1)}, f32[6,128]{1,0:T(8,128)}, u32[]{:S(2)}) copy-start(f32[6,128]{1,0:T(8,128)} %param.22) | copy-start | bytes 9220
  0.7 27.1 %copy-start.1 = (bf16[2,256,256]{2,1,0:T(8,128)(2,1)S(1)}, bf16[2,256,256]{2,1,0:T(8,128)(2,1)}, u32[]{:S(2)}) copy-start(bf16[2,256,256]{2,1,0:T(8,128)(2,1)} %param.14) | copy-start | bytes 786436
  0.7 27.1 %copy-start.2 = (bf16[512,128]{1,0:T(8,128)(2,1)S(1)}, bf16[512,128]{1,0:T(8,128)(2,1)}, u32[]{:S(2)}) copy-start(bf16[512,128]{1,0:T(8,128)(2,1)} %weight_ref.1) | copy-start | bytes 393220
  0.7 8.1 %collective-permute-start = (bf16[1,2,128,256]{3,2,1,0:T(8,128)(2,1)}, bf16[1,2,128,256]{3,2,1,0:T(8,128)(2,1)S(1)}, u32[]{:S(2)}, u32[]{:S(2)}) collective-permute-start(bf16[1,2,128,256]{3,2,1,0:T(8,128)(2,1)} %bitcast.5), channel_id=1, source_target_pairs={{0,2},{2,0},{4,6},{6,4},{8,10},{10,8},{12,14},{14,12},{1,3},{3,1},... | collective-permute-start | bytes 393224 | tf_op jit(solution)/shard_map/ppermute | solution.py:593
  3.7 12.9 %collective-permute-start.1 = (bf16[1,2,128,256]{3,2,1,0:T(8,128)(2,1)}, bf16[1,2,128,256]{3,2,1,0:T(8,128)(2,1)S(1)}, u32[]{:S(2)}, u32[]{:S(2)}) collective-permute-start(bf16[1,2,128,256]{3,2,1,0:T(8,128)(2,1)} %bitcast.6), channel_id=1, source_target_pairs={{0,8},{2,10},{4,12},{6,14},{8,0},{10,2},{12,4},{14,6},{1,9},{3,11}... | collective-permute-start | bytes 393224 | tf_op jit(solution)/shard_map/ppermute | solution.py:593
  6.3 13.1 %collective-permute-start.2 = (bf16[1,2,128,256]{3,2,1,0:T(8,128)(2,1)}, bf16[1,2,128,256]{3,2,1,0:T(8,128)(2,1)S(1)}, u32[]{:S(2)}, u32[]{:S(2)}) collective-permute-start(bf16[1,2,128,256]{3,2,1,0:T(8,128)(2,1)} %bitcast.7), channel_id=1, source_target_pairs={{0,4},{2,6},{4,0},{6,2},{8,12},{10,14},{12,8},{14,10},{1,5},{3,7},... | collective-permute-start | bytes 393224 | tf_op jit(solution)/shard_map/ppermute | solution.py:593
  7.9 11.5 %collective-permute-start.3 = (bf16[1,2,128,256]{3,2,1,0:T(8,128)(2,1)}, bf16[1,2,128,256]{3,2,1,0:T(8,128)(2,1)S(1)}, u32[]{:S(2)}, u32[]{:S(2)}) collective-permute-start(bf16[1,2,128,256]{3,2,1,0:T(8,128)(2,1)} %bitcast.8), channel_id=1, source_target_pairs={{0,12},{2,14},{4,8},{6,10},{8,4},{10,6},{12,0},{14,2},{1,13},{3,15... | collective-permute-start | bytes 393224 | tf_op jit(solution)/shard_map/ppermute | solution.py:593
  16.6 6.0 %collective-permute-start.4 = (bf16[1,2,128,256]{3,2,1,0:T(8,128)(2,1)S(1)}, bf16[1,2,128,256]{3,2,1,0:T(8,128)(2,1)S(1)}, u32[]{:S(2)}, u32[]{:S(2)}) collective-permute-start(bf16[1,2,128,256]{3,2,1,0:T(8,128)(2,1)S(1)} %collective-permute-done.refs_1_), channel_id=1, source_target_pairs={{0,4},{2,6},{4,0},{6,2},{8,12},{10,14},{12,8},{14,10},{1,5},{3,7},... | collective-permute-start | bytes 393224 | tf_op jit(solution)/shard_map/ppermute | solution.py:593
  16.6 7.4 %collective-permute-start.5 = (bf16[1,2,128,256]{3,2,1,0:T(8,128)(2,1)S(1)}, bf16[1,2,128,256]{3,2,1,0:T(8,128)(2,1)S(1)}, u32[]{:S(2)}, u32[]{:S(2)}) collective-permute-start(bf16[1,2,128,256]{3,2,1,0:T(8,128)(2,1)S(1)} %collective-permute-done.refs_1_), channel_id=1, source_target_pairs={{0,12},{2,14},{4,8},{6,10},{8,4},{10,6},{12,0},{14,2},{1,13},{3,15... | collective-permute-start | bytes 393224 | tf_op jit(solution)/shard_map/ppermute | solution.py:593
  18.9 5.1 %collective-permute-start.6 = (bf16[1,2,128,256]{3,2,1,0:T(8,128)(2,1)S(1)}, bf16[1,2,128,256]{3,2,1,0:T(8,128)(2,1)S(1)}, u32[]{:S(2)}, u32[]{:S(2)}) collective-permute-start(bf16[1,2,128,256]{3,2,1,0:T(8,128)(2,1)S(1)} %collective-permute-done.1.refs_4_), channel_id=1, source_target_pairs={{0,2},{2,0},{4,6},{6,4},{8,10},{10,8},{12,14},{14,12},{1,3},{3,1},... | collective-permute-start | bytes 393224 | tf_op jit(solution)/shard_map/ppermute | solution.py:593
  24.0 12.5 %all-to-all-start = ((bf16[8,168,128]{2,1,0:T(8,128)(2,1)}), bf16[8,168,128]{2,1,0:T(8,128)(2,1)S(1)}, u32[]{:S(2)}, u32[]{:S(2)}) async-start(bf16[8,168,128]{2,1,0:T(8,128)(2,1)} %shard_map.149), calls=%async_computation | async-start | bytes 688128 | tf_op jit(solution)/shard_map/all_to_all | solution.py:622
  31.9 11.6 %copy-start.6 = (bf16[2,256]{1,0:T(2,128)(2,1)S(1)}, bf16[2,256]{1,0:T(2,128)(2,1)}, u32[]{:S(2)}) copy-start(bf16[2,256]{1,0:T(2,128)(2,1)} %param.27) | copy-start | bytes 3076
  31.9 11.6 %copy-start = (f32[2,384]{1,0:T(2,128)S(1)}, f32[2,384]{1,0:T(2,128)}, u32[]{:S(2)}) copy-start(f32[2,384]{1,0:T(2,128)} %bias_ref.1) | copy-start | bytes 9220
  31.9 4.7 %collective-permute-start.7 = (f32[2,144,384]{2,1,0:T(8,128)S(1)}, f32[2,144,384]{2,1,0:T(8,128)S(1)}, u32[]{:S(2)}, u32[]{:S(2)}) collective-permute-start(f32[2,144,384]{2,1,0:T(8,128)S(1)} %get-tuple-element.29), channel_id=1, source_target_pairs={{0,1},{1,0},{2,3},{3,2},{4,5},{5,4},{6,7},{7,6},{8,9},{9,8},{10,11... | collective-permute-start | bytes 1327112 | tf_op jit(solution)/shard_map/ppermute | solution.py:672
  36.6 1.7 %collective-permute-start.8 = (bf16[8,168,128]{2,1,0:T(8,128)(2,1)S(1)}, bf16[8,168,128]{2,1,0:T(8,128)(2,1)S(1)}, u32[]{:S(2)}, u32[]{:S(2)}) collective-permute-start(bf16[8,168,128]{2,1,0:T(8,128)(2,1)S(1)} %all-to-all-done.got_ref.early_ref), channel_id=1, source_target_pairs={{0,1},{1,0},{2,3},{3,2},{4,5},{5,4},{6,7},{7,6},{8,9},{9,8},{10,11... | collective-permute-start | bytes 1032200 | tf_op jit(solution)/shard_map/ppermute | solution.py:624
  40.0 12.9 %all-to-all-start.1 = ((bf16[8,64,256]{2,1,0:T(8,128)(2,1)}), bf16[8,64,256]{2,1,0:T(8,128)(2,1)S(1)}, u32[]{:S(2)}, u32[]{:S(2)}) async-start(bf16[8,64,256]{2,1,0:T(8,128)(2,1)} %shard_map.154), calls=%async_computation.1 | async-start | bytes 524288 | tf_op jit(solution)/shard_map/all_to_all | solution.py:694
  43.5 9.3 %copy-start.4 = (bf16[128,256]{1,0:T(8,128)(2,1)S(1)}, bf16[128,256]{1,0:T(8,128)(2,1)}, u32[]{:S(2)}) copy-start(bf16[128,256]{1,0:T(8,128)(2,1)} %head_ref.1) | copy-start | bytes 196612
  71.4 1.4 %collective-permute-start.9 = (f32[8,40,128]{2,1,0:T(8,128)S(1)}, f32[8,40,128]{2,1,0:T(8,128)S(1)}, u32[]{:S(2)}, u32[]{:S(2)}) collective-permute-start(f32[8,40,128]{2,1,0:T(8,128)S(1)} %all_to_all.15.mine_ref), channel_id=1, source_target_pairs={{0,1},{1,0},{2,3},{3,2},{4,5},{5,4},{6,7},{7,6},{8,9},{9,8},{10,11... | collective-permute-start | bytes 491528 | tf_op jit(solution)/shard_map/ppermute | solution.py:763
